TPU v7x, 512 devices: a whole 4x4x16 slice. The times are simulated.
512 devices in a mesh: dp: 32 (over z, core), expert: 16 (over y, x).
Axes of the slice: x: 4, y: 4, z: 16, core: 2. Of those that a mesh axis runs over, the one named last changes fastest.
Arguments:
- tokens: bfloat16 [4096, 2048], P('dp'), may hold values from -6 to 6
- cotangent: bfloat16 [4096, 2048], P('dp'), may hold values from -6 to 6
- expert_ids: int32 [4096, 8], P('dp'), may hold values from 0 to 63, all different within a row; in each aligned block of 128 rows (0 to 127, 128 to 255, ...) at most 32 rows name the same one
- gates: bfloat16 [4096, 8], P('dp'), may hold values from 0.019897461 to 0.5
- w_gate: bfloat16 [16, 32, 128, 2048], P('expert', 'dp'), may hold values from -0.125 to 0.125
- w_up: bfloat16 [16, 32, 128, 2048], P('expert', 'dp'), may hold values from -0.125 to 0.125
- w_down: bfloat16 [16, 32, 128, 2048], P('expert', 'dp'), may hold values from -0.1875 to 0.1875
Outputs:
- d_tokens: bfloat16 [4096, 2048], P(('dp', 'expert'))
- d_gates: float32 [4096, 8], P(('dp', 'expert'))
- grad_gate: bfloat16 [16, 32, 128, 2048], P('expert', 'dp')
- grad_up: bfloat16 [16, 32, 128, 2048], P('expert', 'dp')
- grad_down: bfloat16 [16, 32, 128, 2048], P('expert', 'dp')
Inputs may be any that keep to these rules, and one draw needn't show every extreme that they name: `expert_ids`: the 8 experts of a token are distinct; among the rows of one index of dp each expert is named by at most 32 rows, and some index has an expert named by exactly 32 rows.
All inputs are finite; a program needn't handle non-finite values.
Results may differ from a plain program's by a relative error of at most 0.018.
Values may be sent and summed in bfloat16 or wider, within the bound.
No kernel may reach another device: no remote copies, remote signals or barrier semaphores. Data moves between devices by JAX's collectives and lax.ppermute only.
A program may use at most 128 MiB of HBM per device.

v0:
```python
import jax
import jax.numpy as jnp
from jax import lax
from jax.sharding import PartitionSpec as P

EL = 4


def shards(tokens, cotangent, expert_ids, gates, w_gate, w_up, w_down):
    tok_rows = tokens.shape[0]
    width = tokens.shape[1]
    top_count = expert_ids.shape[1]
    columns = lax.axis_size("expert")
    pieces = lax.axis_size("dp")
    quarters = pieces // EL
    experts_all = columns * EL
    capacity = max(8, 2 * ((tok_rows * top_count + experts_all - 1) // experts_all))
    slot_count = EL * capacity
    my_column = lax.axis_index("expert")
    flat_ids = expert_ids.reshape(-1)
    local_ids = flat_ids - my_column * EL
    inside = (local_ids >= 0) & (local_ids < EL)
    onehot = (local_ids[:, None] == jnp.arange(EL, dtype=jnp.int32)[None, :]).astype(jnp.int32)
    earlier = jnp.cumsum(onehot, axis=0) - onehot
    slot_rank = jnp.sum(earlier * onehot, axis=1)
    position = jnp.where(inside, local_ids * capacity + slot_rank, slot_count)
    x_buffer = (
        jnp.zeros((slot_count, width), jnp.bfloat16)
        .at[position]
        .set(jnp.repeat(tokens, top_count, axis=0), mode="drop")
    )
    dy_buffer = (
        jnp.zeros((slot_count, width), jnp.bfloat16)
        .at[position]
        .set(jnp.repeat(cotangent, top_count, axis=0), mode="drop")
    )
    g_buffer = (
        jnp.zeros((slot_count,), jnp.bfloat16).at[position].set(gates.reshape(-1), mode="drop")
    )
    x_buffer = x_buffer.reshape(EL, capacity, width)
    dy_buffer = dy_buffer.reshape(EL, capacity, width)
    g_buffer = g_buffer.reshape(EL, capacity)

    def spread(source):
        return jnp.repeat(source, quarters, axis=0)

    piece_x, piece_dy, piece_g = (
        lax.all_to_all(spread(x_buffer), "dp", split_axis=0, concat_axis=0, tiled=True),
        lax.all_to_all(spread(dy_buffer), "dp", split_axis=0, concat_axis=0, tiled=True),
        lax.all_to_all(spread(g_buffer), "dp", split_axis=0, concat_axis=0, tiled=True),
    )
    row_count = pieces * capacity
    x_rows = piece_x.reshape(row_count, width)
    dy_rows = piece_dy.reshape(row_count, width)
    g_rows = piece_g.reshape(row_count).astype(jnp.float32)[:, None]
    weight_gate = w_gate[0, 0]
    weight_up = w_up[0, 0]
    weight_down = w_down[0, 0]
    inner = (((1,), (1,)), ((), ()))
    outer = (((0,), (0,)), ((), ()))
    pre_gate = lax.dot_general(x_rows, weight_gate, inner, preferred_element_type=jnp.float32)
    pre_up = lax.dot_general(x_rows, weight_up, inner, preferred_element_type=jnp.float32)
    sigma = jax.nn.sigmoid(pre_gate)
    active = pre_gate * sigma
    hidden = (active * pre_up).astype(jnp.bfloat16)
    back = lax.dot_general(dy_rows, weight_down, inner, preferred_element_type=jnp.float32)
    gate_part = jnp.sum(hidden.astype(jnp.float32) * back, axis=1).astype(jnp.bfloat16)
    d_hidden = g_rows * back
    d_pre_gate = (d_hidden * pre_up * sigma * (1.0 + pre_gate * (1.0 - sigma))).astype(jnp.bfloat16)
    d_pre_up = (d_hidden * active).astype(jnp.bfloat16)
    x_part = (
        jnp.dot(d_pre_gate, weight_gate, preferred_element_type=jnp.float32)
        + jnp.dot(d_pre_up, weight_up, preferred_element_type=jnp.float32)
    ).astype(jnp.bfloat16)
    scaled = (g_rows * hidden.astype(jnp.float32)).astype(jnp.bfloat16)
    grad_down = lax.dot_general(scaled, dy_rows, outer, preferred_element_type=jnp.float32).astype(
        jnp.bfloat16
    )
    grad_gate = lax.dot_general(
        d_pre_gate, x_rows, outer, preferred_element_type=jnp.float32
    ).astype(jnp.bfloat16)
    grad_up = lax.dot_general(d_pre_up, x_rows, outer, preferred_element_type=jnp.float32).astype(
        jnp.bfloat16
    )
    back_x, back_g = (
        lax.all_to_all(
            x_part.reshape(pieces, capacity, width), "dp", split_axis=0, concat_axis=0, tiled=True
        ),
        lax.all_to_all(
            gate_part.reshape(pieces, capacity), "dp", split_axis=0, concat_axis=0, tiled=True
        ),
    )
    summed_x = jnp.sum(back_x.reshape(EL, quarters, capacity, width), axis=1, dtype=jnp.float32)
    summed_g = jnp.sum(back_g.reshape(EL, quarters, capacity), axis=1, dtype=jnp.float32)
    slot_x = summed_x.reshape(slot_count, width)
    slot_g = summed_g.reshape(slot_count)
    safe_position = jnp.minimum(position, slot_count - 1)
    keep = inside.astype(jnp.float32)
    pair_x = slot_x[safe_position] * keep[:, None]
    pair_g = slot_g[safe_position] * keep
    tok_terms = jnp.sum(pair_x.reshape(tok_rows, top_count, width), axis=1)
    gate_terms = pair_g.reshape(tok_rows, top_count)
    tok_sum, gate_sum = (
        lax.psum_scatter(
            tok_terms.astype(jnp.bfloat16), "expert", scatter_dimension=0, tiled=True
        ).astype(jnp.float32),
        lax.psum_scatter(
            gate_terms.astype(jnp.bfloat16), "expert", scatter_dimension=0, tiled=True
        ).astype(jnp.float32),
    )
    return (
        tok_sum.astype(jnp.bfloat16),
        gate_sum,
        grad_gate[None, None],
        grad_up[None, None],
        grad_down[None, None],
    )


def solution(mesh):
    return jax.shard_map(
        shards,
        mesh=mesh,
        in_specs=(
            P("dp", None),
            P("dp", None),
            P("dp", None),
            P("dp", None),
            P("expert", "dp", None, None),
            P("expert", "dp", None, None),
            P("expert", "dp", None, None),
        ),
        out_specs=(
            P(("dp", "expert"), None),
            P(("dp", "expert"), None),
            P("expert", "dp", None, None),
            P("expert", "dp", None, None),
            P("expert", "dp", None, None),
        ),
        check_vma=False,
    )
```

profile of v0, /device:TPU:6, one launch (start us, length us, event | category | flops | bytes accessed | tf_op | source)
XLA Modules:
  0.0 790.8 jit_solution(16565948245269270694)
XLA Ops:
  7.2 0.8 copy.18
  8.1 0.1 sub.40
  8.1 0.1 sub.41
  8.3 0.8 copy.19
  9.1 0.1 reshape.228
  9.2 0.1 and.23
  9.3 0.1 mul.79
  9.4 1.1 reduce-window.6
  10.5 0.2 slice_reduce_fusion
  10.7 0.2 reduce-window.9
  10.9 0.1 add_bitcast_fusion
  11.1 7.6 scatter_custom_fusion
  18.6 0.1 reshape.193
  18.7 0.6 copy.20
  19.4 15.5 %all-to-all-start = ((bf16[32,1,32]{2,1,0:T(2,128)(2,1)}), bf16[32,1,32]{2,1,0:T(2,128)(2,1)S(1)}, u32[]{:S(2)}, u32[]{:S(2)}) async-start(bf16[32,1,32]{2,1,0:T(2,128)(2,1)} %copy.20), calls=%async_computation | async-start | bytes 32768 | tf_op jit(solution)/shard_map/all_to_all | solution.py:50
  34.8 6.7 scatter_custom_fusion.2
  41.6 5.6 all-to-all-done
  47.2 2.5 broadcast_in_dim.46
  49.7 7.0 all-to-all-start.2
  56.7 6.4 scatter_custom_fusion.1
  63.2 177.2 %all-to-all-done.2 = bf16[32,32,2048]{2,1,0:T(8,128)(2,1)} async-done(((bf16[32,32,2048]{2,1,0:T(8,128)(2,1)}), bf16[32,32,2048]{2,1,0:T(8,128)(2,1)}, u32[]{:S(2)}, u32[]{:S(2)}) %all-to-all-start.2) | async-done | bytes 4194336 | tf_op jit(solution)/shard_map/all_to_all | solution.py:48
  240.3 2.5 broadcast_in_dim.44
  242.8 9.9 %all-to-all-start.1 = ((bf16[32,32,2048]{2,1,0:T(8,128)(2,1)}), bf16[32,32,2048]{2,1,0:T(8,128)(2,1)}, u32[]{:S(2)}, u32[]{:S(2)}) async-start(bf16[32,32,2048]{2,1,0:T(8,128)(2,1)} %bitcast.85), calls=%async_computation.1 | async-start | bytes 8388608 | tf_op jit(solution)/shard_map/all_to_all | solution.py:49
  252.9 3.7 fusion.14
  256.7 3.8 fusion.17
  260.4 175.8 %all-to-all-done.1 = bf16[32,32,2048]{2,1,0:T(8,128)(2,1)} async-done(((bf16[32,32,2048]{2,1,0:T(8,128)(2,1)}), bf16[32,32,2048]{2,1,0:T(8,128)(2,1)}, u32[]{:S(2)}, u32[]{:S(2)}) %all-to-all-start.1) | async-done | bytes 4194336 | tf_op jit(solution)/shard_map/all_to_all | solution.py:49
  436.3 3.9 fusion.10
  440.1 1.3 fusion.12
  441.4 3.3 add_convert_fusion
  444.7 10.3 %all-to-all-start.3 = ((bf16[32,32,2048]{2,1,0:T(8,128)(2,1)}), bf16[32,32,2048]{2,1,0:T(8,128)(2,1)}, u32[]{:S(2)}, u32[]{:S(2)}) async-start(bf16[32,32,2048]{2,1,0:T(8,128)(2,1)} %bitcast.84), calls=%async_computation.3 | async-start | bytes 8388608 | tf_op jit(solution)/shard_map/all_to_all | solution.py:86
  454.9 1.3 dynamic-slice
  456.9 0.7 convert_element_type.118
  457.6 3.7 fusion.5
  461.3 3.7 fusion.7
  465.0 173.5 %all-to-all-done.3 = bf16[32,32,2048]{2,1,0:T(8,128)(2,1)} async-done(((bf16[32,32,2048]{2,1,0:T(8,128)(2,1)}), bf16[32,32,2048]{2,1,0:T(8,128)(2,1)}, u32[]{:S(2)}, u32[]{:S(2)}) %all-to-all-start.3) | async-done | bytes 4194336 | tf_op jit(solution)/shard_map/all_to_all | solution.py:86
  638.4 10.1 %all-to-all-start.4 = ((bf16[32,1,32]{2,1,0:T(2,128)(2,1)}), bf16[32,1,32]{2,1,0:T(2,128)(2,1)S(1)}, u32[]{:S(2)}, u32[]{:S(2)}) async-start(bf16[32,1,32]{2,1,0:T(2,128)(2,1)} %convert_element_type.118), calls=%async_computation.4 | async-start | bytes 32768 | tf_op jit(solution)/shard_map/all_to_all | solution.py:89
  648.5 0.3 all-reduce.4.cloned.1.call-start
  648.8 3.0 convert_reduce_fusion
  651.8 6.8 gather_fusion
  658.6 7.3 fusion
  665.9 3.7 fusion.6
  669.6 0.1 reshape.204
  669.7 6.5 gather_fusion.1
  676.2 0.1 gather.13
  676.3 65.6 %all-reduce.1 = bf16[128,8]{1,0:T(8,128)(2,1)S(1)} all-reduce(bf16[128,8]{1,0:T(8,128)(2,1)S(1)} %select_convert_fusion), channel_id=3, replica_groups=mesh['dp'=32,'expert'=16] {'expert'}, use_global_device_ids=true, to_apply=%region_11.12.clone | all-reduce | flops 1024 | bytes 4096
  742.0 0.6 dynamic-slice_convert_fusion
  742.6 40.0 %all-reduce.4.cloned.1.call-done = bf16[128,2048]{1,0:T(8,128)(2,1)} async-done(((bf16[128,2048]{1,0:T(8,128)(2,1)}), bf16[128,2048]{1,0:T(8,128)(2,1)}) %all-reduce.4.cloned.1.call-update) | async-done | bytes 524304
  782.6 1.4 constant_dynamic-slice_fusion
  (22 shorter events, 0.3 us)
Async XLA Ops:
  7.2 245.8 %copy-start = (bf16[1,1,128,2048]{3,2,1,0:T(8,128)(2,1)S(1)}, bf16[1,1,128,2048]{3,2,1,0:T(8,128)(2,1)}, u32[]{:S(2)}) copy-start(bf16[1,1,128,2048]{3,2,1,0:T(8,128)(2,1)} %param.11) | copy-start | bytes 1572868
  19.4 27.9 %all-to-all-start = ((bf16[32,1,32]{2,1,0:T(2,128)(2,1)}), bf16[32,1,32]{2,1,0:T(2,128)(2,1)S(1)}, u32[]{:S(2)}, u32[]{:S(2)}) async-start(bf16[32,1,32]{2,1,0:T(2,128)(2,1)} %copy.20), calls=%async_computation | async-start | bytes 32768 | tf_op jit(solution)/shard_map/all_to_all | solution.py:50
  49.7 7.0 copy-start.2
  49.7 190.6 %all-to-all-start.2 = ((bf16[32,32,2048]{2,1,0:T(8,128)(2,1)}), bf16[32,32,2048]{2,1,0:T(8,128)(2,1)}, u32[]{:S(2)}, u32[]{:S(2)}) async-start(bf16[32,32,2048]{2,1,0:T(8,128)(2,1)} %bitcast.86), calls=%async_computation.2 | async-start | bytes 8388608 | tf_op jit(solution)/shard_map/all_to_all | solution.py:48
  242.8 193.4 %all-to-all-start.1 = ((bf16[32,32,2048]{2,1,0:T(8,128)(2,1)}), bf16[32,32,2048]{2,1,0:T(8,128)(2,1)}, u32[]{:S(2)}, u32[]{:S(2)}) async-start(bf16[32,32,2048]{2,1,0:T(8,128)(2,1)} %bitcast.85), calls=%async_computation.1 | async-start | bytes 8388608 | tf_op jit(solution)/shard_map/all_to_all | solution.py:49
  252.8 3.9 copy-start.1
  256.7 179.6 %copy-start.3 = (bf16[1,1,128,2048]{3,2,1,0:T(8,128)(2,1)S(1)}, bf16[1,1,128,2048]{3,2,1,0:T(8,128)(2,1)}, u32[]{:S(2)}) copy-start(bf16[1,1,128,2048]{3,2,1,0:T(8,128)(2,1)} %param.13) | copy-start | bytes 1572868
  444.7 193.8 %all-to-all-start.3 = ((bf16[32,32,2048]{2,1,0:T(8,128)(2,1)}), bf16[32,32,2048]{2,1,0:T(8,128)(2,1)}, u32[]{:S(2)}, u32[]{:S(2)}) async-start(bf16[32,32,2048]{2,1,0:T(8,128)(2,1)} %bitcast.84), calls=%async_computation.3 | async-start | bytes 8388608 | tf_op jit(solution)/shard_map/all_to_all | solution.py:86
  638.4 31.2 %all-to-all-start.4 = ((bf16[32,1,32]{2,1,0:T(2,128)(2,1)}), bf16[32,1,32]{2,1,0:T(2,128)(2,1)S(1)}, u32[]{:S(2)}, u32[]{:S(2)}) async-start(bf16[32,1,32]{2,1,0:T(2,128)(2,1)} %convert_element_type.118), calls=%async_computation.4 | async-start | bytes 32768 | tf_op jit(solution)/shard_map/all_to_all | solution.py:89
  648.5 134.1 %all-reduce.4.cloned.1.call-start = ((), (), s32[]{:S(2)}) async-start(), calls=%async_computation.5 | async-start | bytes 1048576
Sparse Core Ops, SparseCore 0:
  666.0 116.5 all-reduce.3
where the time goes:
time: 792 us; the launch traced here: 791 us
  waiting for transfers between devices  572 us (72%)
  blocking collectives  65.6 us (8%)
  starting transfers between devices  53 us (7%)
  local copies, waits for them, and re-layouts  45.7 us (6%)
  matrix products  27 us (3%)
  between operations  14.9 us (2%)
  other arithmetic  12.5 us (2%)
    all_to_all x1, waiting for transfers between devices, shards(): lax.all_to_all(spread(x_buffer), 'dp', split_axis=0, concat_axis=0, tiled...  177 us
    all_to_all x1, waiting for transfers between devices, shards(): lax.all_to_all(spread(dy_buffer), 'dp', split_axis=0, concat_axis=0, tile...  176 us
    all_to_all x1, waiting for transfers between devices, shards(): lax.all_to_all(x_part.reshape(pieces, capacity, width), 'dp', split_axis=...  173 us
    unnamed x1, blocking collectives  65.6 us
    unnamed x2, waiting for transfers between devices  40 us
  transfers between devices with their start and end apart: 6, of which 5 were waited for; matrix products, arithmetic and copies ran while one was open for 7% of the time, Pallas kernels for 0%

commit v1 on v0

v1 whole, which is shorter than its diff:
```python
import jax
import jax.numpy as jnp
from jax import lax
from jax.sharding import Mesh, PartitionSpec as P

BF = jnp.bfloat16
F32 = jnp.float32
EL = 4
CAP = 32
LANES = 128


def dot(a, b, dims):
    return lax.dot_general(a, b, (dims, ((), ())), preferred_element_type=F32)


INNER = ((1,), (1,))
PLAIN = ((1,), (0,))
OUTER = ((0,), (0,))


def shards(tokens, cotangent, expert_ids, gates, w_gate, w_up, w_down):
    rows, width = tokens.shape
    top = expert_ids.shape[1]
    nz = lax.axis_size("z")
    cols = lax.axis_size("expert")
    z = lax.axis_index("z")
    col = lax.axis_index("expert")
    block = z // (nz // EL)
    part = rows // cols

    swap_core = [(0, 1), (1, 0)]
    swap_z = [(i, i ^ 1) for i in range(nz)]
    near = [(i, (i + 1) % nz if i % 2 else (i - 1) % nz) for i in range(nz)]

    def core_swap(v):
        return lax.ppermute(v, "core", swap_core)

    def shift(v, by):
        return lax.ppermute(v, "z", [(i, (i + by) % nz) for i in range(nz)])

    own = [w_gate[0, 0], w_up[0, 0], w_down[0, 0]]
    far = [lax.ppermute(w, "z", swap_z) for w in own]
    own_c = [core_swap(w) for w in own]
    far_c = [core_swap(w) for w in far]
    weights = [jnp.concatenate(q, axis=0) for q in zip(own, own_c, far, far_c)]

    def mine(v):
        return lax.dynamic_slice_in_dim(v, col * part, part, axis=0)

    pad = jnp.zeros((part, LANES - 2 * top), BF)
    packed = jnp.concatenate(
        [mine(tokens), mine(cotangent), mine(expert_ids).astype(BF), mine(gates), pad], axis=1
    )
    wide = packed.shape[1]
    quads = jnp.stack([packed] + [shift(packed, -4 * a) for a in range(1, 4)])
    both = jnp.stack([quads, lax.ppermute(quads, "z", near)])
    blocks = both.reshape(1, 8, part, wide)
    sent = jnp.broadcast_to(blocks, (2, 8, part, wide)).reshape(16, part, wide)
    whole = lax.all_to_all(sent, "expert", 0, 0, tiled=True).reshape(rows, wide)

    half = col // 8
    slots = CAP // 2
    ids = whole[:, 2 * width : 2 * width + top].astype(jnp.int32)
    wanted = jnp.arange(cols, dtype=jnp.int32) * EL + block
    named = jnp.any(ids[:, :, None] == wanted[None, None, :], axis=1)
    before = jnp.tril(jnp.ones((rows, rows), BF), -1)
    rank = dot(before, named.astype(BF), PLAIN).astype(jnp.int32) - half * slots
    rank = jnp.where(named, rank, -1)
    pick = (rank.T[:, None, :] == jnp.arange(slots, dtype=jnp.int32)[None, :, None]).astype(BF)
    pick = pick.reshape(cols * slots, rows)
    chosen = dot(pick, whole, PLAIN).astype(BF).reshape(cols, slots, wide)
    got = lax.all_to_all(chosen, "expert", 0, 0, tiled=True).reshape(cols * slots, wide)

    x = got[:, :width]
    dy = got[:, width : 2 * width]
    row_ids = got[:, 2 * width : 2 * width + top].astype(jnp.int32)
    row_gates = got[:, 2 * width + top : 2 * width + 2 * top].astype(F32)
    mark = (row_ids == col * EL + block).astype(F32)
    g = jnp.sum(row_gates * mark, axis=1, keepdims=True)
    wg, wu, wd = weights
    pre_gate = dot(x, wg, INNER)
    pre_up = dot(x, wu, INNER)
    sigma = jax.nn.sigmoid(pre_gate)
    active = pre_gate * sigma
    hidden = (active * pre_up).astype(BF)
    back = dot(dy, wd, INNER)
    gate_part = jnp.sum(hidden.astype(F32) * back, axis=1, keepdims=True)
    d_hidden = g * back
    d_pre_gate = (d_hidden * pre_up * sigma * (1.0 + pre_gate * (1.0 - sigma))).astype(BF)
    d_pre_up = (d_hidden * active).astype(BF)
    scaled = (g * hidden.astype(F32)).astype(BF)
    x_part = (dot(d_pre_gate, wg, PLAIN) + dot(d_pre_up, wu, PLAIN)).astype(BF)
    gate_lanes = (gate_part * mark).astype(BF)
    back_pad = jnp.zeros((cols * slots, LANES - top), BF)
    reply = jnp.concatenate([x_part, gate_lanes, back_pad], axis=1)
    thin = reply.shape[1]

    home = lax.all_to_all(reply.reshape(cols, slots, thin), "expert", 0, 0, tiled=True)
    terms = dot(pick, home.reshape(cols * slots, thin), OUTER).astype(BF)
    spread = lax.all_to_all(terms.reshape(cols, part, thin), "expert", 0, 0, tiled=True)
    spread = jnp.sum(spread.reshape(2, 2, 4, part, thin), axis=0, dtype=F32)
    here = spread[0] + lax.ppermute(spread[1].astype(BF), "z", near).astype(F32)
    total = here[0]
    for a in range(1, 4):
        total = total + shift(here[a].astype(BF), 4 * a).astype(F32)

    fq = own[0].shape[0]
    grads = []
    for left, right in ((d_pre_gate, x), (d_pre_up, x), (scaled, dy)):
        full = dot(left, right, OUTER).astype(BF).reshape(4, fq, width)
        g_own = full[0].astype(F32) + core_swap(full[1]).astype(F32)
        g_far = full[2].astype(F32) + core_swap(full[3]).astype(F32)
        g_own = g_own + lax.ppermute(g_far.astype(BF), "z", swap_z).astype(F32)
        grads.append(g_own.astype(BF)[None, None])
    return (total[:, :width].astype(BF), total[:, width : width + top], *grads)


def solution(mesh):
    devices = mesh.devices
    inner = Mesh(devices.reshape(devices.shape[0] // 2, 2, devices.shape[1]), ("z", "core", "expert"))
    dp = ("z", "core")
    tok = P(dp, None)
    wt = P("expert", dp, None, None)
    out = P(("z", "core", "expert"), None)
    return jax.shard_map(
        shards,
        mesh=inner,
        in_specs=(tok, tok, tok, tok, wt, wt, wt),
        out_specs=(out, out, wt, wt, wt),
        check_vma=False,
    )
```

time: 792 us -> 223 us (0.28)
  waiting for transfers between devices: 572 us -> 56.4 us
  starting transfers between devices: 53 us -> 119 us
  blocking collectives: 65.6 us -> 0 us
  local copies, waits for them, and re-layouts: 45.7 us -> 12.3 us
  between operations: 14.9 us -> 1.17 us
    all_to_all x5 -> x4, waiting for transfers between devices: 532 us -> 14.2 us  [the longest x1 14.2 us: shards(): whole = lax.all_to_all(sent, 'expert', 0, 0, tiled=True).reshape(rows, wide)]
    ppermute x0 -> x26, starting transfers between devices: none -> 90.6 us  [the longest x6 44.9 us: shift(): return lax.ppermute(v, 'z', [(i, (i + by) % nz) for i in range(nz)])]
    unnamed x1 -> x0, blocking collectives: 65.6 us -> none
    ppermute x0 -> x26, waiting for transfers between devices: none -> 42.2 us  [the longest x3 18.1 us: shards(): far = [lax.ppermute(w, 'z', swap_z) for w in own]]
    unnamed x2 -> x0, waiting for transfers between devices: 40 us -> none
    all_to_all x5 -> x4, starting transfers between devices: 52.8 us -> 28.6 us  [the longest x1 7.42 us: shards(): whole = lax.all_to_all(sent, 'expert', 0, 0, tiled=True).reshape(rows, wide)]
    scatter x3 -> x0, local copies, waits for them, and re-layouts: 20.8 us -> none  [the longest x1 7.58 us: shards(): jnp.zeros((slot_count,), jnp.bfloat16).at[position]]
    gather x3 -> x0, local copies, waits for them, and re-layouts: 13.3 us -> none  [the longest x1 6.76 us: shards(): pair_x = slot_x[safe_position] * keep[:, None]]
  transfers between devices with their start and end apart: 6 -> 30, of which waited for: 5 -> 10; matrix products, arithmetic and copies ran while one was open for 7% -> 10% of each run, Pallas kernels for 0% -> 0%
where the time goes in v1:
time: 223 us; the launch traced here: 221 us
  starting transfers between devices  119 us (53%)
  waiting for transfers between devices  56.4 us (25%)
  matrix products  19.4 us (9%)
  other arithmetic  12.6 us (6%)
  local copies, waits for them, and re-layouts  12.3 us (6%)
    ppermute x6, starting transfers between devices, shift(): return lax.ppermute(v, 'z', [(i, (i + by) % nz) for i in range(nz)])  44.9 us
    ppermute x12, starting transfers between devices, core_swap(): return lax.ppermute(v, 'core', swap_core)  25.4 us
    dot_general x11, matrix products, dot(): return lax.dot_general(a, b, (dims, ((), ())), preferred_element_type=F32)  19.4 us
    ppermute x3, waiting for transfers between devices, shards(): far = [lax.ppermute(w, 'z', swap_z) for w in own]  18.1 us
    all_to_all x1, waiting for transfers between devices, shards(): whole = lax.all_to_all(sent, 'expert', 0, 0, tiled=True).reshape(rows, wide)  14.2 us
    ppermute x1, waiting for transfers between devices, shards(): both = jnp.stack([quads, lax.ppermute(quads, 'z', near)])  9.57 us
    ppermute x6, waiting for transfers between devices, shift(): return lax.ppermute(v, 'z', [(i, (i + by) % nz) for i in range(nz)])  9.4 us
    ppermute x3, starting transfers between devices, shards(): g_own = g_own + lax.ppermute(g_far.astype(BF), 'z', swap_z).astype(F32)  8.14 us
  transfers between devices with their start and end apart: 30, of which 10 were waited for; matrix products, arithmetic and copies ran while one was open for 10% of the time, Pallas kernels for 0%

profile of v1, /device:TPU:6, one launch (start us, length us, event | category | flops | bytes accessed | tf_op | source)
XLA Modules:
  0.0 221.0 jit_solution(7659610369928320497)
XLA Ops:
  2.5 9.1 %collective-permute-start.2 = (bf16[8,4224]{1,0:T(8,128)(2,1)S(1)}, bf16[8,4224]{1,0:T(8,128)(2,1)S(1)}, u32[]{:S(2)}, u32[]{:S(2)}) collective-permute-start(bf16[8,4224]{1,0:T(8,128)(2,1)S(1)} %concatenate.15), channel_id=1, source_target_pairs={{0,128},{32,160},{64,192},{96,224},{128,256},{160,288},{192,320},{... | collective-permute-start | bytes 202760 | tf_op jit(solution)/shard_map/ppermute | solution.py:40
  11.6 10.9 %collective-permute-start.1 = (bf16[8,4224]{1,0:T(8,128)(2,1)S(1)}, bf16[8,4224]{1,0:T(8,128)(2,1)S(1)}, u32[]{:S(2)}, u32[]{:S(2)}) collective-permute-start(bf16[8,4224]{1,0:T(8,128)(2,1)S(1)} %concatenate.15), channel_id=1, source_target_pairs={{0,256},{32,288},{64,320},{96,352},{128,384},{160,416},{192,448},{... | collective-permute-start | bytes 202760 | tf_op jit(solution)/shard_map/ppermute | solution.py:40
  22.6 5.5 %collective-permute-start = (bf16[8,4224]{1,0:T(8,128)(2,1)S(1)}, bf16[8,4224]{1,0:T(8,128)(2,1)S(1)}, u32[]{:S(2)}, u32[]{:S(2)}) collective-permute-start(bf16[8,4224]{1,0:T(8,128)(2,1)S(1)} %concatenate.15), channel_id=1, source_target_pairs={{0,384},{32,416},{64,448},{96,480},{128,0},{160,32},{192,64},{224,... | collective-permute-start | bytes 202760 | tf_op jit(solution)/shard_map/ppermute | solution.py:40
  29.4 6.6 %collective-permute-done = bf16[8,4224]{1,0:T(8,128)(2,1)S(1)} collective-permute-done((bf16[8,4224]{1,0:T(8,128)(2,1)S(1)}, bf16[8,4224]{1,0:T(8,128)(2,1)S(1)}, u32[]{:S(2)}, u32[]{:S(2)}) %collective-permute-start) | collective-permute-done | bytes 67616 | tf_op jit(solution)/shard_map/ppermute | solution.py:40
  36.1 1.9 collective-permute-start.3
  38.0 9.6 %collective-permute-done.3 = bf16[4,8,4224]{2,1,0:T(8,128)(2,1)S(1)} collective-permute-done((bf16[4,8,4224]{2,1,0:T(8,128)(2,1)S(1)}, bf16[4,8,4224]{2,1,0:T(8,128)(2,1)S(1)}, u32[]{:S(2)}, u32[]{:S(2)}) %collective-permute-start.3) | collective-permute-done | bytes 270368 | tf_op jit(solution)/shard_map/ppermute | solution.py:57
  48.7 7.4 %all-to-all-start = ((bf16[16,8,4224]{2,1,0:T(8,128)(2,1)}), bf16[16,8,4224]{2,1,0:T(8,128)(2,1)S(1)}, u32[]{:S(2)}, u32[]{:S(2)}) async-start(bf16[16,8,4224]{2,1,0:T(8,128)(2,1)} %bitcast.7), calls=%async_computation | async-start | bytes 2162688 | tf_op jit(solution)/shard_map/all_to_all | solution.py:60
  56.1 14.2 %all-to-all-done = bf16[16,8,4224]{2,1,0:T(8,128)(2,1)S(1)} async-done(((bf16[16,8,4224]{2,1,0:T(8,128)(2,1)}), bf16[16,8,4224]{2,1,0:T(8,128)(2,1)S(1)}, u32[]{:S(2)}, u32[]{:S(2)}) %all-to-all-start) | async-done | bytes 1081376 | tf_op jit(solution)/shard_map/all_to_all | solution.py:60
  70.8 2.1 convolution_convert_fusion
  72.9 6.7 %all-to-all-start.1 = ((bf16[16,16,4224]{2,1,0:T(8,128)(2,1)}), bf16[16,16,4224]{2,1,0:T(8,128)(2,1)S(1)}, u32[]{:S(2)}, u32[]{:S(2)}) async-start(bf16[16,16,4224]{2,1,0:T(8,128)(2,1)} %bitcast.73), calls=%async_computation.1 | async-start | bytes 4325376 | tf_op jit(solution)/shard_map/all_to_all | solution.py:73
  79.6 1.9 collective-permute-start.8
  81.5 3.9 %collective-permute-start.11 = (bf16[128,2048]{1,0:T(8,128)(2,1)}, bf16[128,2048]{1,0:T(8,128)(2,1)}, u32[]{:S(2)}, u32[]{:S(2)}) collective-permute-start(bf16[128,2048]{1,0:T(8,128)(2,1)} %bitcast.91), channel_id=1, source_target_pairs={{0,32},{32,0},{64,96},{96,64},{128,160},{160,128},{192,224},{224,1... | collective-permute-start | bytes 1572872 | tf_op jit(solution)/shard_map/ppermute | solution.py:43
  85.4 1.9 collective-permute-start.7
  87.4 1.9 collective-permute-start.5
  89.3 7.1 %collective-permute-done.8 = bf16[128,2048]{1,0:T(8,128)(2,1)} collective-permute-done((bf16[128,2048]{1,0:T(8,128)(2,1)S(1)}, bf16[128,2048]{1,0:T(8,128)(2,1)}, u32[]{:S(2)}, u32[]{:S(2)}) %collective-permute-start.8) | collective-permute-done | bytes 524320 | tf_op jit(solution)/shard_map/ppermute | solution.py:43
  96.4 1.9 collective-permute-start.9
  98.3 2.4 %collective-permute-start.10 = (bf16[128,2048]{1,0:T(8,128)(2,1)}, bf16[128,2048]{1,0:T(8,128)(2,1)}, u32[]{:S(2)}, u32[]{:S(2)}) collective-permute-start(bf16[128,2048]{1,0:T(8,128)(2,1)} %bitcast.92), channel_id=1, source_target_pairs={{0,16},{16,0},{1,17},{17,1},{2,18},{18,2},{3,19},{19,3},{4,20},{20... | collective-permute-start | bytes 1572872 | tf_op jit(solution)/shard_map/ppermute | solution.py:37
  100.8 6.9 %collective-permute-done.11 = bf16[128,2048]{1,0:T(8,128)(2,1)} collective-permute-done((bf16[128,2048]{1,0:T(8,128)(2,1)}, bf16[128,2048]{1,0:T(8,128)(2,1)}, u32[]{:S(2)}, u32[]{:S(2)}) %collective-permute-start.11) | collective-permute-done | bytes 524320 | tf_op jit(solution)/shard_map/ppermute | solution.py:43
  107.7 1.9 collective-permute-start.12
  109.6 2.4 %collective-permute-start.4 = (bf16[128,2048]{1,0:T(8,128)(2,1)S(1)}, bf16[128,2048]{1,0:T(8,128)(2,1)}, u32[]{:S(2)}, u32[]{:S(2)}) collective-permute-start(bf16[128,2048]{1,0:T(8,128)(2,1)S(1)} %bitcast.85), channel_id=1, source_target_pairs={{0,16},{16,0},{1,17},{17,1},{2,18},{18,2},{3,19},{19,3},{4,20},{20... | collective-permute-start | bytes 1572872 | tf_op jit(solution)/shard_map/ppermute | solution.py:37
  112.0 4.1 %collective-permute-done.5 = bf16[128,2048]{1,0:T(8,128)(2,1)} collective-permute-done((bf16[128,2048]{1,0:T(8,128)(2,1)S(1)}, bf16[128,2048]{1,0:T(8,128)(2,1)}, u32[]{:S(2)}, u32[]{:S(2)}) %collective-permute-start.5) | collective-permute-done | bytes 524320 | tf_op jit(solution)/shard_map/ppermute | solution.py:43
  116.1 1.9 collective-permute-start.6
  118.1 2.2 fusion.19
  120.5 2.1 fusion.17
  122.6 2.4 %fusion.21 = (bf16[256]{0:T(256)(128)(2,1)S(1)}, bf16[256,512]{1,0:T(8,128)(2,1)S(1)}, bf16[256,512]{1,0:T(8,128)(2,1)S(1)}, bf16[256,512]{1,0:T(8,128)(2,1)S(1)}) fusion(f32[256,512]{1,0:T(8,128)S(1)} %fusion.19, f32[256,512]{1,0:T(8,128)S(1)} %fusion.17, f32[256]{0:T(256)S(1)} %select_reduce_fusion, bf16[128,2048]{1,0:T(8,128)(2,1)} %collective-permute-done.6, ...), kind=kOutput, calls=%fused_computation.40 | convolution fusion | flops 547749632 | bytes 4982272 | tf_op jit(solution)/shard_map/dot_general | solution.py:14
  125.1 2.1 convolution_convert_fusion.3
  127.2 2.1 convolution_convert_fusion.2
  129.3 2.1 fusion.27
  131.4 2.1 fusion.2
  134.2 2.6 %concatenate.19 = bf16[256,2176]{1,0:T(8,128)(2,1)} concatenate(bf16[256,2048]{1,0:T(8,128)(2,1)S(1)} %fusion.2, bf16[256,8]{1,0:T(8,128)(2,1)S(1)} %select_convert_fusion, bf16[256,120]{1,0:T(8,128)(2,1)} %broadcast_in_dim.45), dimensions={1} | concatenate | bytes 2228224 | tf_op jit(solution)/shard_map/concatenate | solution.py:96
  136.8 7.2 %all-to-all-start.2 = ((bf16[16,16,2176]{2,1,0:T(8,128)(2,1)}), bf16[16,16,2176]{2,1,0:T(8,128)(2,1)S(1)}, u32[]{:S(2)}, u32[]{:S(2)}) async-start(bf16[16,16,2176]{2,1,0:T(8,128)(2,1)} %bitcast.75), calls=%async_computation.2 | async-start | bytes 2228224 | tf_op jit(solution)/shard_map/all_to_all | solution.py:99
  144.0 2.2 %fusion.53 = (bf16[128,2048]{1,0:T(8,128)(2,1)}, bf16[128,2048]{1,0:T(8,128)(2,1)S(1)}) fusion(bf16[512,2048]{1,0:T(8,128)(2,1)} %convolution_convert_fusion.3), kind=kLoop, calls=%fused_computation.93 | loop fusion | bytes 2097152 | tf_op jit(solution)/shard_map/slice | solution.py:112
  148.2 2.4 %collective-permute-start.17 = (bf16[128,2048]{1,0:T(8,128)(2,1)}, bf16[128,2048]{1,0:T(8,128)(2,1)}, u32[]{:S(2)}, u32[]{:S(2)}) collective-permute-start(bf16[128,2048]{1,0:T(8,128)(2,1)} %get-tuple-element.13), channel_id=1, source_target_pairs={{0,16},{16,0},{1,17},{17,1},{2,18},{18,2},{3,19},{19,3},{4,20},{20... | collective-permute-start | bytes 1572872 | tf_op jit(solution)/shard_map/ppermute | solution.py:37
  153.4 2.4 %collective-permute-start.20 = (bf16[128,2048]{1,0:T(8,128)(2,1)}, bf16[128,2048]{1,0:T(8,128)(2,1)}, u32[]{:S(2)}, u32[]{:S(2)}) collective-permute-start(bf16[128,2048]{1,0:T(8,128)(2,1)} %get-tuple-element.11), channel_id=1, source_target_pairs={{0,16},{16,0},{1,17},{17,1},{2,18},{18,2},{3,19},{19,3},{4,20},{20... | collective-permute-start | bytes 1572872 | tf_op jit(solution)/shard_map/ppermute | solution.py:37
  161.0 2.4 %collective-permute-start.23 = (bf16[128,2048]{1,0:T(8,128)(2,1)}, bf16[128,2048]{1,0:T(8,128)(2,1)}, u32[]{:S(2)}, u32[]{:S(2)}) collective-permute-start(bf16[128,2048]{1,0:T(8,128)(2,1)} %get-tuple-element.9), channel_id=1, source_target_pairs={{0,16},{16,0},{1,17},{17,1},{2,18},{18,2},{3,19},{19,3},{4,20},{20... | collective-permute-start | bytes 1572872 | tf_op jit(solution)/shard_map/ppermute | solution.py:37
  163.4 2.0 add_convert_fusion.5
  165.4 2.3 %collective-permute-start.19 = (bf16[128,2048]{1,0:T(8,128)(2,1)}, bf16[128,2048]{1,0:T(8,128)(2,1)}, u32[]{:S(2)}, u32[]{:S(2)}) collective-permute-start(bf16[128,2048]{1,0:T(8,128)(2,1)} %add_convert_fusion.5), channel_id=1, source_target_pairs={{0,32},{32,0},{64,96},{96,64},{128,160},{160,128},{192,224},{224,1... | collective-permute-start | bytes 1572872 | tf_op jit(solution)/shard_map/ppermute | solution.py:114
  169.8 7.2 %all-to-all-start.3 = ((bf16[16,8,2176]{2,1,0:T(8,128)(2,1)}), bf16[16,8,2176]{2,1,0:T(8,128)(2,1)S(1)}, u32[]{:S(2)}, u32[]{:S(2)}) async-start(bf16[16,8,2176]{2,1,0:T(8,128)(2,1)} %fusion.1), calls=%async_computation.3 | async-start | bytes 1114112 | tf_op jit(solution)/shard_map/all_to_all | solution.py:101
  177.0 3.7 %collective-permute-start.22 = (bf16[128,2048]{1,0:T(8,128)(2,1)}, bf16[128,2048]{1,0:T(8,128)(2,1)}, u32[]{:S(2)}, u32[]{:S(2)}) collective-permute-start(bf16[128,2048]{1,0:T(8,128)(2,1)} %add_convert_fusion.3), channel_id=1, source_target_pairs={{0,32},{32,0},{64,96},{96,64},{128,160},{160,128},{192,224},{224,1... | collective-permute-start | bytes 1572872 | tf_op jit(solution)/shard_map/ppermute | solution.py:114
  182.0 2.2 collective-permute-start.25
  184.2 2.4 %fusion.23 = bf16[1,1,128,2048]{3,2,1,0:T(8,128)(2,1)} fusion(bf16[128,2048]{1,0:T(8,128)(2,1)} %collective-permute-done.19, bf16[128,2048]{1,0:T(8,128)(2,1)} %collective-permute-done.17, bf16[512,2048]{1,0:T(8,128)(2,1)} %convolution_convert_fusion.3), kind=kLoop, calls=%fused_computation.42 | loop fusion | flops 1572864 | bytes 2097152 | tf_op jit(solution)/shard_map/broadcast_in_dim | solution.py:115
  186.7 2.4 %collective-permute-start.13 = (bf16[4,8,2176]{2,1,0:T(8,128)(2,1)S(1)}, bf16[4,8,2176]{2,1,0:T(8,128)(2,1)S(1)}, u32[]{:S(2)}, u32[]{:S(2)}) collective-permute-start(bf16[4,8,2176]{2,1,0:T(8,128)(2,1)S(1)} %fusion.31), channel_id=1, source_target_pairs={{0,480},{32,64},{64,32},{96,128},{128,96},{160,192},{192,160},{224... | collective-permute-start | bytes 417800 | tf_op jit(solution)/shard_map/ppermute | solution.py:103
  189.1 5.0 %collective-permute-done.22 = bf16[128,2048]{1,0:T(8,128)(2,1)} collective-permute-done((bf16[128,2048]{1,0:T(8,128)(2,1)}, bf16[128,2048]{1,0:T(8,128)(2,1)}, u32[]{:S(2)}, u32[]{:S(2)}) %collective-permute-start.22) | collective-permute-done | bytes 524320 | tf_op jit(solution)/shard_map/ppermute | solution.py:114
  194.1 2.4 %fusion.24 = bf16[1,1,128,2048]{3,2,1,0:T(8,128)(2,1)} fusion(bf16[128,2048]{1,0:T(8,128)(2,1)} %collective-permute-done.22, bf16[128,2048]{1,0:T(8,128)(2,1)} %collective-permute-done.20, bf16[512,2048]{1,0:T(8,128)(2,1)} %convolution_convert_fusion.2), kind=kLoop, calls=%fused_computation.43 | loop fusion | flops 1572864 | bytes 2097152 | tf_op jit(solution)/shard_map/broadcast_in_dim | solution.py:115
  196.6 6.5 %collective-permute-start.16 = (bf16[8,2176]{1,0:T(8,128)(2,1)S(1)}, bf16[8,2176]{1,0:T(8,128)(2,1)S(1)}, u32[]{:S(2)}, u32[]{:S(2)}) collective-permute-start(bf16[8,2176]{1,0:T(8,128)(2,1)S(1)} %get-tuple-element.20), channel_id=1, source_target_pairs={{0,384},{32,416},{64,448},{96,480},{128,0},{160,32},{192,64},{224,... | collective-permute-start | bytes 104456 | tf_op jit(solution)/shard_map/ppermute | solution.py:40
  203.0 6.6 %collective-permute-start.15 = (bf16[8,2176]{1,0:T(8,128)(2,1)S(1)}, bf16[8,2176]{1,0:T(8,128)(2,1)S(1)}, u32[]{:S(2)}, u32[]{:S(2)}) collective-permute-start(bf16[8,2176]{1,0:T(8,128)(2,1)S(1)} %get-tuple-element.21), channel_id=1, source_target_pairs={{0,256},{32,288},{64,320},{96,352},{128,384},{160,416},{192,448},{... | collective-permute-start | bytes 104456 | tf_op jit(solution)/shard_map/ppermute | solution.py:40
  209.6 6.4 %collective-permute-start.14 = (bf16[8,2176]{1,0:T(8,128)(2,1)S(1)}, bf16[8,2176]{1,0:T(8,128)(2,1)S(1)}, u32[]{:S(2)}, u32[]{:S(2)}) collective-permute-start(bf16[8,2176]{1,0:T(8,128)(2,1)S(1)} %get-tuple-element.19), channel_id=1, source_target_pairs={{0,128},{32,160},{64,192},{96,224},{128,256},{160,288},{192,320},{... | collective-permute-start | bytes 104456 | tf_op jit(solution)/shard_map/ppermute | solution.py:40
  216.1 2.3 %fusion.25 = bf16[1,1,128,2048]{3,2,1,0:T(8,128)(2,1)} fusion(bf16[128,2048]{1,0:T(8,128)(2,1)} %collective-permute-done.25, bf16[128,2048]{1,0:T(8,128)(2,1)} %collective-permute-done.23, bf16[512,2048]{1,0:T(8,128)(2,1)S(1)} %copy-done.2), kind=kLoop, calls=%fused_computation.44 | loop fusion | flops 1572864 | bytes 2097152 | tf_op jit(solution)/shard_map/broadcast_in_dim | solution.py:115
  (76 shorter events, 21.9 us)
Async XLA Ops:
  0.6 0.9 copy-start
  2.5 25.5 %collective-permute-start.2 = (bf16[8,4224]{1,0:T(8,128)(2,1)S(1)}, bf16[8,4224]{1,0:T(8,128)(2,1)S(1)}, u32[]{:S(2)}, u32[]{:S(2)}) collective-permute-start(bf16[8,4224]{1,0:T(8,128)(2,1)S(1)} %concatenate.15), channel_id=1, source_target_pairs={{0,128},{32,160},{64,192},{96,224},{128,256},{160,288},{192,320},{... | collective-permute-start | bytes 202760 | tf_op jit(solution)/shard_map/ppermute | solution.py:40
  11.6 17.7 %collective-permute-start.1 = (bf16[8,4224]{1,0:T(8,128)(2,1)S(1)}, bf16[8,4224]{1,0:T(8,128)(2,1)S(1)}, u32[]{:S(2)}, u32[]{:S(2)}) collective-permute-start(bf16[8,4224]{1,0:T(8,128)(2,1)S(1)} %concatenate.15), channel_id=1, source_target_pairs={{0,256},{32,288},{64,320},{96,352},{128,384},{160,416},{192,448},{... | collective-permute-start | bytes 202760 | tf_op jit(solution)/shard_map/ppermute | solution.py:40
  22.6 13.4 %collective-permute-start = (bf16[8,4224]{1,0:T(8,128)(2,1)S(1)}, bf16[8,4224]{1,0:T(8,128)(2,1)S(1)}, u32[]{:S(2)}, u32[]{:S(2)}) collective-permute-start(bf16[8,4224]{1,0:T(8,128)(2,1)S(1)} %concatenate.15), channel_id=1, source_target_pairs={{0,384},{32,416},{64,448},{96,480},{128,0},{160,32},{192,64},{224,... | collective-permute-start | bytes 202760 | tf_op jit(solution)/shard_map/ppermute | solution.py:40
  36.1 11.5 %collective-permute-start.3 = (bf16[4,8,4224]{2,1,0:T(8,128)(2,1)S(1)}, bf16[4,8,4224]{2,1,0:T(8,128)(2,1)S(1)}, u32[]{:S(2)}, u32[]{:S(2)}) collective-permute-start(bf16[4,8,4224]{2,1,0:T(8,128)(2,1)S(1)} %get-tuple-element.18), channel_id=1, source_target_pairs={{0,480},{32,64},{64,32},{96,128},{128,96},{160,192},{192,160},{224... | collective-permute-start | bytes 811016 | tf_op jit(solution)/shard_map/ppermute | solution.py:57
  48.7 21.6 %all-to-all-start = ((bf16[16,8,4224]{2,1,0:T(8,128)(2,1)}), bf16[16,8,4224]{2,1,0:T(8,128)(2,1)S(1)}, u32[]{:S(2)}, u32[]{:S(2)}) async-start(bf16[16,8,4224]{2,1,0:T(8,128)(2,1)} %bitcast.7), calls=%async_computation | async-start | bytes 2162688 | tf_op jit(solution)/shard_map/all_to_all | solution.py:60
  72.9 6.7 %copy-start.5 = (bf16[1,1,128,2048]{3,2,1,0:T(8,128)(2,1)S(1)}, bf16[1,1,128,2048]{3,2,1,0:T(8,128)(2,1)}, u32[]{:S(2)}) copy-start(bf16[1,1,128,2048]{3,2,1,0:T(8,128)(2,1)} %param.12) | copy-start | bytes 1572868
  72.9 14.5 %copy-start.4 = (bf16[1,1,128,2048]{3,2,1,0:T(8,128)(2,1)S(1)}, bf16[1,1,128,2048]{3,2,1,0:T(8,128)(2,1)}, u32[]{:S(2)}) copy-start(bf16[1,1,128,2048]{3,2,1,0:T(8,128)(2,1)} %param.13) | copy-start | bytes 1572868
  72.9 45.2 %all-to-all-start.1 = ((bf16[16,16,4224]{2,1,0:T(8,128)(2,1)}), bf16[16,16,4224]{2,1,0:T(8,128)(2,1)S(1)}, u32[]{:S(2)}, u32[]{:S(2)}) async-start(bf16[16,16,4224]{2,1,0:T(8,128)(2,1)} %bitcast.73), calls=%async_computation.1 | async-start | bytes 4325376 | tf_op jit(solution)/shard_map/all_to_all | solution.py:73
  79.6 16.9 %collective-permute-start.8 = (bf16[128,2048]{1,0:T(8,128)(2,1)S(1)}, bf16[128,2048]{1,0:T(8,128)(2,1)}, u32[]{:S(2)}, u32[]{:S(2)}) collective-permute-start(bf16[128,2048]{1,0:T(8,128)(2,1)S(1)} %bitcast.87), channel_id=1, source_target_pairs={{0,32},{32,0},{64,96},{96,64},{128,160},{160,128},{192,224},{224,1... | collective-permute-start | bytes 1572872 | tf_op jit(solution)/shard_map/ppermute | solution.py:43
  81.5 26.2 %collective-permute-start.11 = (bf16[128,2048]{1,0:T(8,128)(2,1)}, bf16[128,2048]{1,0:T(8,128)(2,1)}, u32[]{:S(2)}, u32[]{:S(2)}) collective-permute-start(bf16[128,2048]{1,0:T(8,128)(2,1)} %bitcast.91), channel_id=1, source_target_pairs={{0,32},{32,0},{64,96},{96,64},{128,160},{160,128},{192,224},{224,1... | collective-permute-start | bytes 1572872 | tf_op jit(solution)/shard_map/ppermute | solution.py:43
  85.4 24.2 %collective-permute-start.7 = (bf16[128,2048]{1,0:T(8,128)(2,1)S(1)}, bf16[128,2048]{1,0:T(8,128)(2,1)}, u32[]{:S(2)}, u32[]{:S(2)}) collective-permute-start(bf16[128,2048]{1,0:T(8,128)(2,1)S(1)} %bitcast.88), channel_id=1, source_target_pairs={{0,16},{16,0},{1,17},{17,1},{2,18},{18,2},{3,19},{19,3},{4,20},{20... | collective-permute-start | bytes 1572872 | tf_op jit(solution)/shard_map/ppermute | solution.py:37
  87.4 28.7 %collective-permute-start.5 = (bf16[128,2048]{1,0:T(8,128)(2,1)S(1)}, bf16[128,2048]{1,0:T(8,128)(2,1)}, u32[]{:S(2)}, u32[]{:S(2)}) collective-permute-start(bf16[128,2048]{1,0:T(8,128)(2,1)S(1)} %bitcast.84), channel_id=1, source_target_pairs={{0,32},{32,0},{64,96},{96,64},{128,160},{160,128},{192,224},{224,1... | collective-permute-start | bytes 1572872 | tf_op jit(solution)/shard_map/ppermute | solution.py:43
  96.4 21.6 %collective-permute-start.9 = (bf16[128,2048]{1,0:T(8,128)(2,1)}, bf16[128,2048]{1,0:T(8,128)(2,1)}, u32[]{:S(2)}, u32[]{:S(2)}) collective-permute-start(bf16[128,2048]{1,0:T(8,128)(2,1)} %collective-permute-done.8), channel_id=1, source_target_pairs={{0,16},{16,0},{1,17},{17,1},{2,18},{18,2},{3,19},{19,3},{4,20},{20... | collective-permute-start | bytes 1572872 | tf_op jit(solution)/shard_map/ppermute | solution.py:37
  98.3 22.1 %collective-permute-start.10 = (bf16[128,2048]{1,0:T(8,128)(2,1)}, bf16[128,2048]{1,0:T(8,128)(2,1)}, u32[]{:S(2)}, u32[]{:S(2)}) collective-permute-start(bf16[128,2048]{1,0:T(8,128)(2,1)} %bitcast.92), channel_id=1, source_target_pairs={{0,16},{16,0},{1,17},{17,1},{2,18},{18,2},{3,19},{19,3},{4,20},{20... | collective-permute-start | bytes 1572872 | tf_op jit(solution)/shard_map/ppermute | solution.py:37
  107.7 12.8 %collective-permute-start.12 = (bf16[128,2048]{1,0:T(8,128)(2,1)}, bf16[128,2048]{1,0:T(8,128)(2,1)}, u32[]{:S(2)}, u32[]{:S(2)}) collective-permute-start(bf16[128,2048]{1,0:T(8,128)(2,1)} %collective-permute-done.11), channel_id=1, source_target_pairs={{0,16},{16,0},{1,17},{17,1},{2,18},{18,2},{3,19},{19,3},{4,20},{20... | collective-permute-start | bytes 1572872 | tf_op jit(solution)/shard_map/ppermute | solution.py:37
  109.6 13.0 %collective-permute-start.4 = (bf16[128,2048]{1,0:T(8,128)(2,1)S(1)}, bf16[128,2048]{1,0:T(8,128)(2,1)}, u32[]{:S(2)}, u32[]{:S(2)}) collective-permute-start(bf16[128,2048]{1,0:T(8,128)(2,1)S(1)} %bitcast.85), channel_id=1, source_target_pairs={{0,16},{16,0},{1,17},{17,1},{2,18},{18,2},{3,19},{19,3},{4,20},{20... | collective-permute-start | bytes 1572872 | tf_op jit(solution)/shard_map/ppermute | solution.py:37
  116.1 6.5 %collective-permute-start.6 = (bf16[128,2048]{1,0:T(8,128)(2,1)}, bf16[128,2048]{1,0:T(8,128)(2,1)}, u32[]{:S(2)}, u32[]{:S(2)}) collective-permute-start(bf16[128,2048]{1,0:T(8,128)(2,1)} %collective-permute-done.5), channel_id=1, source_target_pairs={{0,16},{16,0},{1,17},{17,1},{2,18},{18,2},{3,19},{19,3},{4,20},{20... | collective-permute-start | bytes 1572872 | tf_op jit(solution)/shard_map/ppermute | solution.py:37
  118.0 2.4 %copy-start.7 = (bf16[1,1,128,2048]{3,2,1,0:T(8,128)(2,1)S(1)}, bf16[1,1,128,2048]{3,2,1,0:T(8,128)(2,1)}, u32[]{:S(2)}) copy-start(bf16[1,1,128,2048]{3,2,1,0:T(8,128)(2,1)} %param.11) | copy-start | bytes 1572868
  127.2 2.1 copy-start.6
  136.8 31.9 %all-to-all-start.2 = ((bf16[16,16,2176]{2,1,0:T(8,128)(2,1)}), bf16[16,16,2176]{2,1,0:T(8,128)(2,1)S(1)}, u32[]{:S(2)}, u32[]{:S(2)}) async-start(bf16[16,16,2176]{2,1,0:T(8,128)(2,1)} %bitcast.75), calls=%async_computation.2 | async-start | bytes 2228224 | tf_op jit(solution)/shard_map/all_to_all | solution.py:99
  144.0 6.6 %copy-start.3 = (bf16[512,2048]{1,0:T(8,128)(2,1)S(1)}, bf16[512,2048]{1,0:T(8,128)(2,1)}, u32[]{:S(2)}) copy-start(bf16[512,2048]{1,0:T(8,128)(2,1)} %convolution_convert_fusion.2) | copy-start | bytes 6291460
  146.2 14.7 %collective-permute-start.18 = (bf16[128,2048]{1,0:T(8,128)(2,1)S(1)}, bf16[128,2048]{1,0:T(8,128)(2,1)S(1)}, u32[]{:S(2)}, u32[]{:S(2)}) collective-permute-start(bf16[128,2048]{1,0:T(8,128)(2,1)S(1)} %get-tuple-element.14), channel_id=1, source_target_pairs={{0,16},{16,0},{1,17},{17,1},{2,18},{18,2},{3,19},{19,3},{4,20},{20... | collective-permute-start | bytes 1572872 | tf_op jit(solution)/shard_map/ppermute | solution.py:37
  148.2 33.8 %collective-permute-start.17 = (bf16[128,2048]{1,0:T(8,128)(2,1)}, bf16[128,2048]{1,0:T(8,128)(2,1)}, u32[]{:S(2)}, u32[]{:S(2)}) collective-permute-start(bf16[128,2048]{1,0:T(8,128)(2,1)} %get-tuple-element.13), channel_id=1, source_target_pairs={{0,16},{16,0},{1,17},{17,1},{2,18},{18,2},{3,19},{19,3},{4,20},{20... | collective-permute-start | bytes 1572872 | tf_op jit(solution)/shard_map/ppermute | solution.py:37
  151.5 13.9 %collective-permute-start.21 = (bf16[128,2048]{1,0:T(8,128)(2,1)S(1)}, bf16[128,2048]{1,0:T(8,128)(2,1)S(1)}, u32[]{:S(2)}, u32[]{:S(2)}) collective-permute-start(bf16[128,2048]{1,0:T(8,128)(2,1)S(1)} %get-tuple-element.12), channel_id=1, source_target_pairs={{0,16},{16,0},{1,17},{17,1},{2,18},{18,2},{3,19},{19,3},{4,20},{20... | collective-permute-start | bytes 1572872 | tf_op jit(solution)/shard_map/ppermute | solution.py:37
  153.4 35.7 %collective-permute-start.20 = (bf16[128,2048]{1,0:T(8,128)(2,1)}, bf16[128,2048]{1,0:T(8,128)(2,1)}, u32[]{:S(2)}, u32[]{:S(2)}) collective-permute-start(bf16[128,2048]{1,0:T(8,128)(2,1)} %get-tuple-element.11), channel_id=1, source_target_pairs={{0,16},{16,0},{1,17},{17,1},{2,18},{18,2},{3,19},{19,3},{4,20},{20... | collective-permute-start | bytes 1572872 | tf_op jit(solution)/shard_map/ppermute | solution.py:37
  156.6 1.4 copy-start.1
  159.0 18.0 %collective-permute-start.24 = (bf16[128,2048]{1,0:T(8,128)(2,1)}, bf16[128,2048]{1,0:T(8,128)(2,1)}, u32[]{:S(2)}, u32[]{:S(2)}) collective-permute-start(bf16[128,2048]{1,0:T(8,128)(2,1)} %get-tuple-element.10), channel_id=1, source_target_pairs={{0,16},{16,0},{1,17},{17,1},{2,18},{18,2},{3,19},{19,3},{4,20},{20... | collective-permute-start | bytes 1572872 | tf_op jit(solution)/shard_map/ppermute | solution.py:37
  161.0 55.1 %collective-permute-start.23 = (bf16[128,2048]{1,0:T(8,128)(2,1)}, bf16[128,2048]{1,0:T(8,128)(2,1)}, u32[]{:S(2)}, u32[]{:S(2)}) collective-permute-start(bf16[128,2048]{1,0:T(8,128)(2,1)} %get-tuple-element.9), channel_id=1, source_target_pairs={{0,16},{16,0},{1,17},{17,1},{2,18},{18,2},{3,19},{19,3},{4,20},{20... | collective-permute-start | bytes 1572872 | tf_op jit(solution)/shard_map/ppermute | solution.py:37
  165.4 15.4 %copy-start.2 = (bf16[512,2048]{1,0:T(8,128)(2,1)S(1)}, bf16[512,2048]{1,0:T(8,128)(2,1)}, u32[]{:S(2)}) copy-start(bf16[512,2048]{1,0:T(8,128)(2,1)} %copy-done.1) | copy-start | bytes 6291460
  165.4 18.8 %collective-permute-start.19 = (bf16[128,2048]{1,0:T(8,128)(2,1)}, bf16[128,2048]{1,0:T(8,128)(2,1)}, u32[]{:S(2)}, u32[]{:S(2)}) collective-permute-start(bf16[128,2048]{1,0:T(8,128)(2,1)} %add_convert_fusion.5), channel_id=1, source_target_pairs={{0,32},{32,0},{64,96},{96,64},{128,160},{160,128},{192,224},{224,1... | collective-permute-start | bytes 1572872 | tf_op jit(solution)/shard_map/ppermute | solution.py:114
  169.8 16.7 %all-to-all-start.3 = ((bf16[16,8,2176]{2,1,0:T(8,128)(2,1)}), bf16[16,8,2176]{2,1,0:T(8,128)(2,1)S(1)}, u32[]{:S(2)}, u32[]{:S(2)}) async-start(bf16[16,8,2176]{2,1,0:T(8,128)(2,1)} %fusion.1), calls=%async_computation.3 | async-start | bytes 1114112 | tf_op jit(solution)/shard_map/all_to_all | solution.py:101
  177.0 17.1 %collective-permute-start.22 = (bf16[128,2048]{1,0:T(8,128)(2,1)}, bf16[128,2048]{1,0:T(8,128)(2,1)}, u32[]{:S(2)}, u32[]{:S(2)}) collective-permute-start(bf16[128,2048]{1,0:T(8,128)(2,1)} %add_convert_fusion.3), channel_id=1, source_target_pairs={{0,32},{32,0},{64,96},{96,64},{128,160},{160,128},{192,224},{224,1... | collective-permute-start | bytes 1572872 | tf_op jit(solution)/shard_map/ppermute | solution.py:114
  182.0 34.1 %collective-permute-start.25 = (bf16[128,2048]{1,0:T(8,128)(2,1)S(1)}, bf16[128,2048]{1,0:T(8,128)(2,1)}, u32[]{:S(2)}, u32[]{:S(2)}) collective-permute-start(bf16[128,2048]{1,0:T(8,128)(2,1)S(1)} %add_convert_fusion.1), channel_id=1, source_target_pairs={{0,32},{32,0},{64,96},{96,64},{128,160},{160,128},{192,224},{224,1... | collective-permute-start | bytes 1572872 | tf_op jit(solution)/shard_map/ppermute | solution.py:114
  186.7 9.8 %collective-permute-start.13 = (bf16[4,8,2176]{2,1,0:T(8,128)(2,1)S(1)}, bf16[4,8,2176]{2,1,0:T(8,128)(2,1)S(1)}, u32[]{:S(2)}, u32[]{:S(2)}) collective-permute-start(bf16[4,8,2176]{2,1,0:T(8,128)(2,1)S(1)} %fusion.31), channel_id=1, source_target_pairs={{0,480},{32,64},{64,32},{96,128},{128,96},{160,192},{192,160},{224... | collective-permute-start | bytes 417800 | tf_op jit(solution)/shard_map/ppermute | solution.py:103
  196.6 21.8 %collective-permute-start.16 = (bf16[8,2176]{1,0:T(8,128)(2,1)S(1)}, bf16[8,2176]{1,0:T(8,128)(2,1)S(1)}, u32[]{:S(2)}, u32[]{:S(2)}) collective-permute-start(bf16[8,2176]{1,0:T(8,128)(2,1)S(1)} %get-tuple-element.20), channel_id=1, source_target_pairs={{0,384},{32,416},{64,448},{96,480},{128,0},{160,32},{192,64},{224,... | collective-permute-start | bytes 104456 | tf_op jit(solution)/shard_map/ppermute | solution.py:40
  203.0 15.9 %collective-permute-start.15 = (bf16[8,2176]{1,0:T(8,128)(2,1)S(1)}, bf16[8,2176]{1,0:T(8,128)(2,1)S(1)}, u32[]{:S(2)}, u32[]{:S(2)}) collective-permute-start(bf16[8,2176]{1,0:T(8,128)(2,1)S(1)} %get-tuple-element.21), channel_id=1, source_target_pairs={{0,256},{32,288},{64,320},{96,352},{128,384},{160,416},{192,448},{... | collective-permute-start | bytes 104456 | tf_op jit(solution)/shard_map/ppermute | solution.py:40
  209.6 10.2 %collective-permute-start.14 = (bf16[8,2176]{1,0:T(8,128)(2,1)S(1)}, bf16[8,2176]{1,0:T(8,128)(2,1)S(1)}, u32[]{:S(2)}, u32[]{:S(2)}) collective-permute-start(bf16[8,2176]{1,0:T(8,128)(2,1)S(1)} %get-tuple-element.19), channel_id=1, source_target_pairs={{0,128},{32,160},{64,192},{96,224},{128,256},{160,288},{192,320},{... | collective-permute-start | bytes 104456 | tf_op jit(solution)/shard_map/ppermute | solution.py:40

commit v2 on v1

v2 whole, which is shorter than its diff:
```python
import jax
import jax.numpy as jnp
from jax import lax
from jax.sharding import Mesh, PartitionSpec as P

BF = jnp.bfloat16
F32 = jnp.float32
EL = 4
CAP = 32
LANES = 128
INNER = ((1,), (1,))
PLAIN = ((1,), (0,))
OUTER = ((0,), (0,))
AXES = ("zh", "zq", "core", "expert")


def dot(a, b, dims):
    return lax.dot_general(a, b, (dims, ((), ())), preferred_element_type=F32)


def mirror(sizes):
    nh, nq, nc, ne = sizes
    pairs = []
    for u in range(nh):
        for q in range(nq):
            for c in range(nc):
                for e in range(ne):
                    v = (e + 4 * c + q - u) % nh
                    pairs.append((((u * nq + q) * nc + c) * ne + e, ((v * nq + q) * nc + c) * ne + e))
    return pairs


def layer(x, dy, g, wg, wu, wd):
    pre_gate = dot(x, wg, INNER)
    pre_up = dot(x, wu, INNER)
    sigma = jax.nn.sigmoid(pre_gate)
    active = pre_gate * sigma
    hidden = (active * pre_up).astype(BF)
    back = dot(dy, wd, INNER)
    gate_part = jnp.sum(hidden.astype(F32) * back, axis=1, keepdims=True)
    d_hidden = g * back
    d_pre_gate = (d_hidden * pre_up * sigma * (1.0 + pre_gate * (1.0 - sigma))).astype(BF)
    d_pre_up = (d_hidden * active).astype(BF)
    scaled = (g * hidden.astype(F32)).astype(BF)
    x_part = dot(d_pre_gate, wg, PLAIN) + dot(d_pre_up, wu, PLAIN)
    half = wg.shape[0] // 2
    grads = [dot(a, b, OUTER).astype(BF) for a, b in ((d_pre_gate, x), (d_pre_up, x), (scaled, dy))]
    mine = jnp.stack([v[:half] for v in grads])
    theirs = jnp.stack([v[half:] for v in grads])
    return x_part, gate_part, mine, theirs


def shards(tokens, cotangent, expert_ids, gates, w_gate, w_up, w_down):
    rows, width = tokens.shape
    top = expert_ids.shape[1]
    sizes = tuple(lax.axis_size(a) for a in AXES)
    nh, nq, _, cols = sizes
    col = lax.axis_index("expert")
    block = lax.axis_index("zh") // (nh // EL)
    half = width // 2
    pairs = mirror(sizes)

    def core_swap(v):
        return lax.ppermute(v, "core", [(0, 1), (1, 0)])

    def chip_swap(v):
        return lax.ppermute(v, "zq", [(0, 1), (1, 0)])

    pad = jnp.zeros((rows, LANES - 2 * top), BF)
    body = jnp.where(col < cols // 2, tokens, cotangent)
    packed = jnp.concatenate([body, expert_ids.astype(BF), gates, pad], axis=1)
    wide = packed.shape[1]
    whole = lax.ppermute(packed, AXES, pairs)

    own = [w_gate[0, 0], w_up[0, 0], w_down[0, 0]]
    near = [jnp.concatenate([w, core_swap(w)], axis=0) for w in own]
    later, whole = lax.optimization_barrier((own, whole))
    far = [chip_swap(w) for w in later]
    far = [jnp.concatenate([w, core_swap(w)], axis=0) for w in far]

    ids = whole[:, width : width + top].astype(jnp.int32)
    wanted = jnp.arange(cols, dtype=jnp.int32) * EL + block
    named = jnp.any(ids[:, :, None] == wanted[None, None, :], axis=1)
    before = jnp.tril(jnp.ones((rows, rows), BF), -1)
    rank = dot(before, named.astype(BF), PLAIN).astype(jnp.int32)
    rank = jnp.where(named, rank, -1)
    pick = (rank.T[:, None, :] == jnp.arange(CAP, dtype=jnp.int32)[None, :, None]).astype(BF)
    pick = pick.reshape(cols * CAP, rows)
    chosen = dot(pick, whole, PLAIN).astype(BF).reshape(cols, CAP, wide)
    got = lax.all_to_all(chosen, "expert", 0, 0, tiled=True).reshape(2, cols // 2 * CAP, wide)

    x = got[0, :, :width]
    dy = got[1, :, :width]
    row_ids = got[0, :, width : width + top].astype(jnp.int32)
    row_gates = got[0, :, width + top : width + 2 * top].astype(F32)
    mark = (row_ids == col * EL + block).astype(F32)
    g = jnp.sum(row_gates * mark, axis=1, keepdims=True)
    near_x, near_g, near_mine, near_theirs = layer(x, dy, g, *near)
    far_x, far_g, far_mine, far_theirs = layer(x, dy, g, *far)
    x_part = (near_x + far_x).astype(BF)
    lanes = ((near_g + far_g) * mark).astype(BF)
    lanes = jnp.concatenate([lanes, jnp.zeros((lanes.shape[0], LANES - top), BF)], axis=1)
    reply = jnp.stack(
        [jnp.concatenate([x_part[:, :half], lanes], axis=1), jnp.concatenate([x_part[:, half:], lanes], axis=1)]
    )
    thin = reply.shape[2]

    home = lax.all_to_all(reply.reshape(cols, CAP, thin), "expert", 0, 0, tiled=True)
    terms = dot(pick, home.reshape(cols * CAP, thin), OUTER).astype(BF)
    terms = lax.ppermute(terms, AXES, pairs)
    spread = lax.all_to_all(terms.reshape(cols, rows // cols, thin), "expert", 0, 0, tiled=True)
    total = jnp.sum(spread.reshape(2, cols // 2, rows // cols, thin), axis=1, dtype=F32)
    d_tokens = jnp.concatenate([total[0, :, :half], total[1, :, :half]], axis=1).astype(BF)
    d_gates = total[0, :, half : half + top]

    far_sum = (far_mine.astype(F32) + core_swap(far_theirs).astype(F32)).astype(BF)
    near_sum = near_mine.astype(F32) + core_swap(near_theirs).astype(F32)
    grads = (near_sum + chip_swap(far_sum).astype(F32)).astype(BF)
    return (d_tokens, d_gates, grads[0][None, None], grads[1][None, None], grads[2][None, None])


def solution(mesh):
    devices = mesh.devices
    inner = Mesh(devices.reshape(devices.shape[0] // 4, 2, 2, devices.shape[1]), AXES)
    dp = AXES[:3]
    tok = P(dp, None)
    wt = P("expert", dp, None, None)
    out = P(AXES, None)
    return jax.shard_map(
        shards,
        mesh=inner,
        in_specs=(tok, tok, tok, tok, wt, wt, wt),
        out_specs=(out, out, wt, wt, wt),
        check_vma=False,
    )
```

time: 223 us -> 235 us (1.054)
  the two profiles are of different devices: /device:TPU:6 before, /device:TPU:32 now
where the time goes in v2:
time: 235 us; the launch traced here: 234 us
  starting transfers between devices  77.8 us (33%)
  waiting for transfers between devices  60.9 us (26%)
  blocking collectives  40.4 us (17%)
  matrix products  23.6 us (10%)
  local copies, waits for them, and re-layouts  18 us (8%)
  other arithmetic  12 us (5%)
    all_to_all x1, blocking collectives, shards(): lax.all_to_all(terms.reshape(cols, rows // cols, thin), 'expert', 0, 0, t...  40.4 us
    all_to_all x1, starting transfers between devices, shards(): lax.all_to_all(chosen, 'expert', 0, 0, tiled=True)  37.1 us
    ppermute x1, waiting for transfers between devices, shards(): terms = lax.ppermute(terms, AXES, pairs)  26 us
    dot_general x19, matrix products, dot(): return lax.dot_general(a, b, (dims, ((), ())), preferred_element_type=F32)  23.6 us
    ppermute x4, waiting for transfers between devices, chip_swap(): return lax.ppermute(v, 'zq', [(0, 1), (1, 0)])  17.2 us
    ppermute x8, starting transfers between devices, core_swap(): return lax.ppermute(v, 'core', [(0, 1), (1, 0)])  16.5 us
    ppermute x4, starting transfers between devices, chip_swap(): return lax.ppermute(v, 'zq', [(0, 1), (1, 0)])  10.1 us
    all_to_all x1, waiting for transfers between devices, shards(): lax.all_to_all(reply.reshape(cols, CAP, thin), 'expert', 0, 0, tiled=True)  8.89 us
  transfers between devices with their start and end apart: 16, of which 6 were waited for; matrix products, arithmetic and copies ran while one was open for 10% of the time, Pallas kernels for 0%

profile of v2, /device:TPU:32, one launch (start us, length us, event | category | flops | bytes accessed | tf_op | source)
XLA Modules:
  0.0 233.8 jit_solution(2931672925080417751)
XLA Ops:
  1.3 1.3 copy.17
  2.7 1.3 copy.18
  4.5 5.2 %collective-permute-start = (bf16[128,2176]{0,1:T(8,128)(2,1)S(1)}, bf16[128,2176]{0,1:T(8,128)(2,1)S(1)}, u32[]{:S(2)}, u32[]{:S(2)}) collective-permute-start(bf16[128,2176]{0,1:T(8,128)(2,1)S(1)} %maximum_maximum_fusion), channel_id=1, source_target_pairs={{0,0},{1,65},{2,130},{3,195},{4,260},{5,325},{6,390},{7,455},{8,8}... | collective-permute-start | bytes 1671176 | tf_op jit(solution)/shard_map/ppermute | solution.py:73
  9.8 8.8 %collective-permute-done = bf16[128,2176]{0,1:T(8,128)(2,1)S(1)} collective-permute-done((bf16[128,2176]{0,1:T(8,128)(2,1)S(1)}, bf16[128,2176]{0,1:T(8,128)(2,1)S(1)}, u32[]{:S(2)}, u32[]{:S(2)}) %collective-permute-start) | collective-permute-done | bytes 557088 | tf_op jit(solution)/shard_map/ppermute | solution.py:73
  19.1 2.1 convolution_convert_fusion
  21.2 37.1 %all-to-all-start = ((bf16[16,32,2176]{2,1,0:T(8,128)(2,1)}), bf16[16,32,2176]{2,1,0:T(8,128)(2,1)S(1)}, u32[]{:S(2)}, u32[]{:S(2)}) async-start(bf16[16,32,2176]{2,1,0:T(8,128)(2,1)} %bitcast.117), calls=%async_computation | async-start | bytes 4456448 | tf_op jit(solution)/shard_map/all_to_all | solution.py:90
  58.4 1.9 collective-permute-start.6
  60.3 3.9 %collective-permute-start.8 = (bf16[128,2048]{1,0:T(8,128)(2,1)}, bf16[128,2048]{1,0:T(8,128)(2,1)}, u32[]{:S(2)}, u32[]{:S(2)}) collective-permute-start(bf16[128,2048]{1,0:T(8,128)(2,1)} %bitcast), channel_id=1, source_target_pairs={{0,32},{32,0},{1,33},{33,1},{2,34},{34,2},{3,35},{35,3},{4,36},{36... | collective-permute-start | bytes 1572872 | tf_op jit(solution)/shard_map/ppermute | solution.py:67
  64.3 1.9 collective-permute-start.4
  66.2 9.3 %collective-permute-done.6 = bf16[128,2048]{1,0:T(8,128)(2,1)} collective-permute-done((bf16[128,2048]{1,0:T(8,128)(2,1)}, bf16[128,2048]{1,0:T(8,128)(2,1)}, u32[]{:S(2)}, u32[]{:S(2)}) %collective-permute-start.6) | collective-permute-done | bytes 524320 | tf_op jit(solution)/shard_map/ppermute | solution.py:67
  75.5 1.9 collective-permute-start.7
  77.4 2.4 %collective-permute-start.2 = (bf16[128,2048]{1,0:T(8,128)(2,1)}, bf16[128,2048]{1,0:T(8,128)(2,1)}, u32[]{:S(2)}, u32[]{:S(2)}) collective-permute-start(bf16[128,2048]{1,0:T(8,128)(2,1)} %bitcast.1), channel_id=1, source_target_pairs={{0,16},{16,0},{1,17},{17,1},{2,18},{18,2},{3,19},{19,3},{4,20},{20... | collective-permute-start | bytes 1572872 | tf_op jit(solution)/shard_map/ppermute | solution.py:64
  79.8 1.9 collective-permute-start.3
  81.7 5.0 %collective-permute-done.8 = bf16[128,2048]{1,0:T(8,128)(2,1)} collective-permute-done((bf16[128,2048]{1,0:T(8,128)(2,1)}, bf16[128,2048]{1,0:T(8,128)(2,1)}, u32[]{:S(2)}, u32[]{:S(2)}) %collective-permute-start.8) | collective-permute-done | bytes 524320 | tf_op jit(solution)/shard_map/ppermute | solution.py:67
  86.7 1.9 collective-permute-start.9
  88.6 1.1 constant_dynamic-update-slice_fusion.1
  90.8 2.9 %collective-permute-done.4 = bf16[128,2048]{1,0:T(8,128)(2,1)} collective-permute-done((bf16[128,2048]{1,0:T(8,128)(2,1)}, bf16[128,2048]{1,0:T(8,128)(2,1)}, u32[]{:S(2)}, u32[]{:S(2)}) %collective-permute-start.4) | collective-permute-done | bytes 524320 | tf_op jit(solution)/shard_map/ppermute | solution.py:67
  93.7 1.9 collective-permute-start.1
  95.6 2.4 %collective-permute-start.5 = (bf16[128,2048]{1,0:T(8,128)(2,1)}, bf16[128,2048]{1,0:T(8,128)(2,1)}, u32[]{:S(2)}, u32[]{:S(2)}) collective-permute-start(bf16[128,2048]{1,0:T(8,128)(2,1)} %collective-permute-done.4), channel_id=1, source_target_pairs={{0,16},{16,0},{1,17},{17,1},{2,18},{18,2},{3,19},{19,3},{4,20},{20... | collective-permute-start | bytes 1572872 | tf_op jit(solution)/shard_map/ppermute | solution.py:64
  98.1 1.1 constant_dynamic-update-slice_fusion
  100.4 1.9 fusion.22
  102.8 2.4 %fusion.17 = (f32[256]{0:T(256)S(1)}, bf16[256,256]{0,1:T(8,128)(2,1)}, bf16[256,256]{0,1:T(8,128)(2,1)S(1)}, bf16[256,256]{0,1:T(8,128)(2,1)S(1)}) fusion(f32[256,256]{0,1:T(8,128)S(1)} %fusion.22, f32[256,256]{0,1:T(8,128)S(1)} %fusion.21, f32[256]{0:T(256)S(1)} %fusion.25, bf16[128,2048]{1,0:T(8,128)(2,1)} %collective-permute-done.5, ...), kind=kOutput, calls=%fused_computation.59 | convolution fusion | flops 271777536 | bytes 3016704 | tf_op jit(solution)/shard_map/dot_general | solution.py:18
  105.2 1.5 convolution_convert_fusion.2
  106.6 1.7 fusion.14
  108.8 1.8 fusion.12
  111.0 1.7 fusion.15
  112.8 1.4 convolution_convert_fusion.5
  114.2 1.4 convolution_convert_fusion.6
  115.6 1.7 fusion.13
  117.3 1.8 convolution_add_fusion.1
  120.7 1.9 concatenate.42
  122.6 1.9 concatenate.41
  124.4 1.4 convolution_convert_fusion.1
  126.8 1.2 slice_bitcast_fusion.12
  127.9 1.3 pad_maximum_fusion.1
  129.2 1.9 collective-permute-start.12
  131.2 1.1 pad_maximum_fusion.2
  132.3 6.9 %all-to-all-start.1 = ((bf16[16,32,1152]{2,1,0:T(8,128)(2,1)}), bf16[16,32,1152]{2,1,0:T(8,128)(2,1)S(1)}, u32[]{:S(2)}, u32[]{:S(2)}) async-start(bf16[16,32,1152]{2,1,0:T(8,128)(2,1)} %bitcast.118), calls=%async_computation.1 | async-start | bytes 2359296 | tf_op jit(solution)/shard_map/all_to_all | solution.py:108
  142.0 1.4 pad_maximum_fusion
  143.4 2.1 collective-permute-start.11
  145.6 3.1 %add_convert_fusion.1 = bf16[3,128,2048]{2,1,0:T(8,128)(2,1)} fusion(bf16[3,128,2048]{2,1,0:T(8,128)(2,1)} %collective-permute-done.12, bf16[1,128,2048]{2,1,0:T(8,128)(2,1)S(1)} %copy-done.11, bf16[1,128,2048]{2,1,0:T(8,128)(2,1)S(1)} %copy-done.12, bf16[1,128,2048]{2,1,0:T(8,128)(2,1)S(1)} %copy-done.9), kind=kLoop, calls=%fused_computation.2 | loop fusion | flops 4718592 | bytes 4718592 | tf_op jit(solution)/shard_map/convert_element_type | solution.py:116
  148.7 2.3 collective-permute-start.13
  151.0 8.9 %all-to-all-done.1 = bf16[16,32,1152]{2,1,0:T(8,128)(2,1)S(1)} async-done(((bf16[16,32,1152]{2,1,0:T(8,128)(2,1)}), bf16[16,32,1152]{2,1,0:T(8,128)(2,1)S(1)}, u32[]{:S(2)}, u32[]{:S(2)}) %all-to-all-start.1) | async-done | bytes 1179680 | tf_op jit(solution)/shard_map/all_to_all | solution.py:108
  160.3 1.9 collective-permute-start.10
  162.2 26.0 %collective-permute-done.10 = bf16[128,1152]{1,0:T(8,128)(2,1)S(1)} collective-permute-done((bf16[128,1152]{1,0:T(8,128)(2,1)S(1)}, bf16[128,1152]{1,0:T(8,128)(2,1)S(1)}, u32[]{:S(2)}, u32[]{:S(2)}) %collective-permute-start.10) | collective-permute-done | bytes 294944 | tf_op jit(solution)/shard_map/ppermute | solution.py:110
  188.2 40.4 %all_to_all.15 = bf16[16,8,1152]{2,1,0:T(8,128)(2,1)S(1)} all-to-all(bf16[16,8,1152]{2,1,0:T(8,128)(2,1)S(1)} %bitcast.121), channel_id=1, replica_groups=mesh['zh'=8,'zq'=2,'core'=2,'expert'=16] {'expert'}, dimensions={0} | all-to-all | bytes 589824 | tf_op jit(solution)/shard_map/all_to_all | solution.py:111
  229.9 2.7 %add_convert_fusion = bf16[3,128,2048]{2,1,0:T(8,128)(2,1)S(1)} fusion(bf16[3,128,2048]{2,1,0:T(8,128)(2,1)} %collective-permute-done.13, bf16[3,128,2048]{2,1,0:T(8,128)(2,1)} %collective-permute-done.11, bf16[1,128,2048]{2,1,0:T(8,128)(2,1)S(1)} %get-tuple-element.24, bf16[1,128,2048]{2,1,0:T(8,128)(2,1)S(1)} %copy-done.10, ...), kind=kLoop, calls=%fused_computation.1 | loop fusion | flops 6291456 | bytes 6291456 | tf_op jit(solution)/shard_map/convert_element_type | solution.py:118
  232.6 1.2 slice_bitcast_fusion.6
  (72 shorter events, 12.3 us)
Async XLA Ops:
  0.6 3.5 %copy-start.13 = (bf16[128,8]{0,1:T(8,128)(2,1)S(1)}, bf16[128,8]{0,1:T(8,128)(2,1)}, u32[]{:S(2)}) copy-start(bf16[128,8]{0,1:T(8,128)(2,1)} %param.10) | copy-start | bytes 6148
  4.5 14.1 %collective-permute-start = (bf16[128,2176]{0,1:T(8,128)(2,1)S(1)}, bf16[128,2176]{0,1:T(8,128)(2,1)S(1)}, u32[]{:S(2)}, u32[]{:S(2)}) collective-permute-start(bf16[128,2176]{0,1:T(8,128)(2,1)S(1)} %maximum_maximum_fusion), channel_id=1, source_target_pairs={{0,0},{1,65},{2,130},{3,195},{4,260},{5,325},{6,390},{7,455},{8,8}... | collective-permute-start | bytes 1671176 | tf_op jit(solution)/shard_map/ppermute | solution.py:73
  21.2 79.0 %all-to-all-start = ((bf16[16,32,2176]{2,1,0:T(8,128)(2,1)}), bf16[16,32,2176]{2,1,0:T(8,128)(2,1)S(1)}, u32[]{:S(2)}, u32[]{:S(2)}) async-start(bf16[16,32,2176]{2,1,0:T(8,128)(2,1)} %bitcast.117), calls=%async_computation | async-start | bytes 4456448 | tf_op jit(solution)/shard_map/all_to_all | solution.py:90
  58.4 17.1 %collective-permute-start.6 = (bf16[128,2048]{1,0:T(8,128)(2,1)}, bf16[128,2048]{1,0:T(8,128)(2,1)}, u32[]{:S(2)}, u32[]{:S(2)}) collective-permute-start(bf16[128,2048]{1,0:T(8,128)(2,1)} %bitcast.1), channel_id=1, source_target_pairs={{0,32},{32,0},{1,33},{33,1},{2,34},{34,2},{3,35},{35,3},{4,36},{36... | collective-permute-start | bytes 1572872 | tf_op jit(solution)/shard_map/ppermute | solution.py:67
  60.3 26.4 %collective-permute-start.8 = (bf16[128,2048]{1,0:T(8,128)(2,1)}, bf16[128,2048]{1,0:T(8,128)(2,1)}, u32[]{:S(2)}, u32[]{:S(2)}) collective-permute-start(bf16[128,2048]{1,0:T(8,128)(2,1)} %bitcast), channel_id=1, source_target_pairs={{0,32},{32,0},{1,33},{33,1},{2,34},{34,2},{3,35},{35,3},{4,36},{36... | collective-permute-start | bytes 1572872 | tf_op jit(solution)/shard_map/ppermute | solution.py:67
  64.3 29.5 %collective-permute-start.4 = (bf16[128,2048]{1,0:T(8,128)(2,1)}, bf16[128,2048]{1,0:T(8,128)(2,1)}, u32[]{:S(2)}, u32[]{:S(2)}) collective-permute-start(bf16[128,2048]{1,0:T(8,128)(2,1)} %bitcast.2), channel_id=1, source_target_pairs={{0,32},{32,0},{1,33},{33,1},{2,34},{34,2},{3,35},{35,3},{4,36},{36... | collective-permute-start | bytes 1572872 | tf_op jit(solution)/shard_map/ppermute | solution.py:67
  75.5 20.2 %collective-permute-start.7 = (bf16[128,2048]{1,0:T(8,128)(2,1)}, bf16[128,2048]{1,0:T(8,128)(2,1)}, u32[]{:S(2)}, u32[]{:S(2)}) collective-permute-start(bf16[128,2048]{1,0:T(8,128)(2,1)} %collective-permute-done.6), channel_id=1, source_target_pairs={{0,16},{16,0},{1,17},{17,1},{2,18},{18,2},{3,19},{19,3},{4,20},{20... | collective-permute-start | bytes 1572872 | tf_op jit(solution)/shard_map/ppermute | solution.py:64
  77.4 29.2 %collective-permute-start.2 = (bf16[128,2048]{1,0:T(8,128)(2,1)}, bf16[128,2048]{1,0:T(8,128)(2,1)}, u32[]{:S(2)}, u32[]{:S(2)}) collective-permute-start(bf16[128,2048]{1,0:T(8,128)(2,1)} %bitcast.1), channel_id=1, source_target_pairs={{0,16},{16,0},{1,17},{17,1},{2,18},{18,2},{3,19},{19,3},{4,20},{20... | collective-permute-start | bytes 1572872 | tf_op jit(solution)/shard_map/ppermute | solution.py:64
  79.8 29.0 %collective-permute-start.3 = (bf16[128,2048]{1,0:T(8,128)(2,1)}, bf16[128,2048]{1,0:T(8,128)(2,1)}, u32[]{:S(2)}, u32[]{:S(2)}) collective-permute-start(bf16[128,2048]{1,0:T(8,128)(2,1)} %bitcast), channel_id=1, source_target_pairs={{0,16},{16,0},{1,17},{17,1},{2,18},{18,2},{3,19},{19,3},{4,20},{20... | collective-permute-start | bytes 1572872 | tf_op jit(solution)/shard_map/ppermute | solution.py:64
  86.7 12.5 %collective-permute-start.9 = (bf16[128,2048]{1,0:T(8,128)(2,1)}, bf16[128,2048]{1,0:T(8,128)(2,1)S(1)}, u32[]{:S(2)}, u32[]{:S(2)}) collective-permute-start(bf16[128,2048]{1,0:T(8,128)(2,1)} %collective-permute-done.8), channel_id=1, source_target_pairs={{0,16},{16,0},{1,17},{17,1},{2,18},{18,2},{3,19},{19,3},{4,20},{20... | collective-permute-start | bytes 1572872 | tf_op jit(solution)/shard_map/ppermute | solution.py:64
  93.7 17.3 %collective-permute-start.1 = (bf16[128,2048]{1,0:T(8,128)(2,1)}, bf16[128,2048]{1,0:T(8,128)(2,1)}, u32[]{:S(2)}, u32[]{:S(2)}) collective-permute-start(bf16[128,2048]{1,0:T(8,128)(2,1)} %bitcast.2), channel_id=1, source_target_pairs={{0,16},{16,0},{1,17},{17,1},{2,18},{18,2},{3,19},{19,3},{4,20},{20... | collective-permute-start | bytes 1572872 | tf_op jit(solution)/shard_map/ppermute | solution.py:64
  95.6 7.1 %collective-permute-start.5 = (bf16[128,2048]{1,0:T(8,128)(2,1)}, bf16[128,2048]{1,0:T(8,128)(2,1)}, u32[]{:S(2)}, u32[]{:S(2)}) collective-permute-start(bf16[128,2048]{1,0:T(8,128)(2,1)} %collective-permute-done.4), channel_id=1, source_target_pairs={{0,16},{16,0},{1,17},{17,1},{2,18},{18,2},{3,19},{19,3},{4,20},{20... | collective-permute-start | bytes 1572872 | tf_op jit(solution)/shard_map/ppermute | solution.py:64
  99.1 1.0 copy-start.5
  100.2 2.6 %copy-start.3 = (bf16[256,2048]{1,0:T(8,128)(2,1)}, bf16[256,2048]{1,0:T(8,128)(2,1)S(1)}, u32[]{:S(2)}) copy-start(bf16[256,2048]{1,0:T(8,128)(2,1)S(1)} %constant_dynamic-update-slice_fusion.2) | copy-start | bytes 3145732
  108.8 1.8 copy-start.6
  117.3 1.8 copy-start.4
  124.4 2.3 copy-start.2
  127.9 3.2 %copy-start.7 = (bf16[256,1152]{1,0:T(8,128)(2,1)S(1)}, bf16[256,1152]{1,0:T(8,128)(2,1)}, u32[]{:S(2)}) copy-start(bf16[256,1152]{1,0:T(8,128)(2,1)} %concatenate.42) | copy-start | bytes 1769476
  127.9 3.2 %copy-start.8 = (bf16[256,1152]{1,0:T(8,128)(2,1)S(1)}, bf16[256,1152]{1,0:T(8,128)(2,1)}, u32[]{:S(2)}) copy-start(bf16[256,1152]{1,0:T(8,128)(2,1)} %concatenate.41) | copy-start | bytes 1769476
  129.2 16.3 %collective-permute-start.12 = (bf16[3,128,2048]{2,1,0:T(8,128)(2,1)}, bf16[3,128,2048]{2,1,0:T(8,128)(2,1)}, u32[]{:S(2)}, u32[]{:S(2)}) collective-permute-start(bf16[3,128,2048]{2,1,0:T(8,128)(2,1)} %pad_maximum_fusion.1), channel_id=1, source_target_pairs={{0,16},{16,0},{1,17},{17,1},{2,18},{18,2},{3,19},{19,3},{4,20},{20... | collective-permute-start | bytes 4718600 | tf_op jit(solution)/shard_map/ppermute | solution.py:64
  132.3 27.6 %all-to-all-start.1 = ((bf16[16,32,1152]{2,1,0:T(8,128)(2,1)}), bf16[16,32,1152]{2,1,0:T(8,128)(2,1)S(1)}, u32[]{:S(2)}, u32[]{:S(2)}) async-start(bf16[16,32,1152]{2,1,0:T(8,128)(2,1)} %bitcast.118), calls=%async_computation.1 | async-start | bytes 2359296 | tf_op jit(solution)/shard_map/all_to_all | solution.py:108
  139.2 1.2 copy-start.1
  140.5 1.4 copy-start
  142.0 3.5 %copy-start.9 = (bf16[1,128,2048]{2,1,0:T(8,128)(2,1)S(1)}, bf16[1,128,2048]{2,1,0:T(8,128)(2,1)}, u32[]{:S(2)}) copy-start(bf16[1,128,2048]{2,1,0:T(8,128)(2,1)} %get-tuple-element.26) | copy-start | bytes 1572868
  142.0 3.5 %copy-start.11 = (bf16[1,128,2048]{2,1,0:T(8,128)(2,1)S(1)}, bf16[1,128,2048]{2,1,0:T(8,128)(2,1)}, u32[]{:S(2)}) copy-start(bf16[1,128,2048]{2,1,0:T(8,128)(2,1)} %get-tuple-element.30) | copy-start | bytes 1572868
  142.0 3.5 %copy-start.12 = (bf16[1,128,2048]{2,1,0:T(8,128)(2,1)S(1)}, bf16[1,128,2048]{2,1,0:T(8,128)(2,1)}, u32[]{:S(2)}) copy-start(bf16[1,128,2048]{2,1,0:T(8,128)(2,1)} %get-tuple-element.41) | copy-start | bytes 1572868
  143.4 86.5 %collective-permute-start.11 = (bf16[3,128,2048]{2,1,0:T(8,128)(2,1)}, bf16[3,128,2048]{2,1,0:T(8,128)(2,1)}, u32[]{:S(2)}, u32[]{:S(2)}) collective-permute-start(bf16[3,128,2048]{2,1,0:T(8,128)(2,1)} %pad_maximum_fusion), channel_id=1, source_target_pairs={{0,16},{16,0},{1,17},{17,1},{2,18},{18,2},{3,19},{19,3},{4,20},{20... | collective-permute-start | bytes 4718600 | tf_op jit(solution)/shard_map/ppermute | solution.py:64
  148.7 81.2 %copy-start.10 = (bf16[1,128,2048]{2,1,0:T(8,128)(2,1)S(1)}, bf16[1,128,2048]{2,1,0:T(8,128)(2,1)}, u32[]{:S(2)}) copy-start(bf16[1,128,2048]{2,1,0:T(8,128)(2,1)} %get-tuple-element.43) | copy-start | bytes 1572868
  148.7 81.2 %collective-permute-start.13 = (bf16[3,128,2048]{2,1,0:T(8,128)(2,1)}, bf16[3,128,2048]{2,1,0:T(8,128)(2,1)}, u32[]{:S(2)}, u32[]{:S(2)}) collective-permute-start(bf16[3,128,2048]{2,1,0:T(8,128)(2,1)} %add_convert_fusion.1), channel_id=1, source_target_pairs={{0,32},{32,0},{1,33},{33,1},{2,34},{34,2},{3,35},{35,3},{4,36},{36... | collective-permute-start | bytes 4718600 | tf_op jit(solution)/shard_map/ppermute | solution.py:67
  160.3 27.9 %collective-permute-start.10 = (bf16[128,1152]{1,0:T(8,128)(2,1)S(1)}, bf16[128,1152]{1,0:T(8,128)(2,1)S(1)}, u32[]{:S(2)}, u32[]{:S(2)}) collective-permute-start(bf16[128,1152]{1,0:T(8,128)(2,1)S(1)} %fusion.2), channel_id=1, source_target_pairs={{0,0},{1,65},{2,130},{3,195},{4,260},{5,325},{6,390},{7,455},{8,8}... | collective-permute-start | bytes 884744 | tf_op jit(solution)/shard_map/ppermute | solution.py:110

commit v3 on v2

v3 whole, which is shorter than its diff:
```python
import functools

import jax
import jax.numpy as jnp
from jax import lax
from jax.experimental import pallas as pl
from jax.experimental.pallas import tpu as pltpu
from jax.sharding import Mesh, PartitionSpec as P

BF = jnp.bfloat16
F32 = jnp.float32
EL = 4
CAP = 32
LANES = 128
INNER = ((1,), (1,))
PLAIN = ((1,), (0,))
AXES = ("zh", "zq", "core", "expert")
VMEM_BYTES = 48 << 20


def dot(a, b, dims):
    return lax.dot_general(a, b, (dims, ((), ())), preferred_element_type=F32)


def mirror(sizes):
    nh, nq, nc, ne = sizes
    pairs = []
    for u in range(nh):
        for q in range(nq):
            for c in range(nc):
                for e in range(ne):
                    v = (e + 4 * c + q - u) % nh
                    pairs.append((((u * nq + q) * nc + c) * ne + e, ((v * nq + q) * nc + c) * ne + e))
    return pairs


def call(body, args, outs, flops):
    vmem = pl.BlockSpec(memory_space=pltpu.VMEM)
    smem = pl.BlockSpec(memory_space=pltpu.SMEM)
    moved = sum(a.size * a.dtype.itemsize for a in list(args) + list(outs))
    return pl.pallas_call(
        body,
        out_shape=outs,
        in_specs=[smem if a.dtype == jnp.int32 else vmem for a in args],
        out_specs=[vmem] * len(outs),
        compiler_params=pltpu.CompilerParams(vmem_limit_bytes=VMEM_BYTES),
        cost_estimate=pl.CostEstimate(flops=flops, bytes_accessed=moved, transcendentals=0),
    )(*args)


def select_body(top, width, block_ref, whole_ref, chosen_ref, pick_ref):
    rows, slots = pick_ref.shape
    meta = whole_ref[:, width : width + LANES].astype(F32)
    slot = lax.broadcasted_iota(jnp.int32, (1, slots), 1)
    wanted = (slot // CAP * EL + block_ref[0]).astype(F32)
    named = meta[:, 0:1] == wanted
    for k in range(1, top):
        named = named | (meta[:, k : k + 1] == wanted)
    earlier = lax.broadcasted_iota(jnp.int32, (rows, rows), 0) > lax.broadcasted_iota(jnp.int32, (rows, rows), 1)
    rank = dot(earlier.astype(F32).astype(BF), named.astype(F32).astype(BF), PLAIN)
    pick = jnp.where(named & (rank == (slot % CAP).astype(F32)), 1.0, 0.0)
    pick_ref[...] = pick.astype(BF)
    chosen_ref[...] = dot(pick.T.astype(BF), whole_ref[...], PLAIN).astype(BF)


def layer_body(top, last, expert_ref, rows_ref, wg0, wg1, wu0, wu1, wd0, wd1, *refs):
    fq, width = wg0.shape
    count = rows_ref.shape[0] // 2
    half = width // 2
    x = rows_ref[:count, :width]
    dy = rows_ref[count:, :width]
    meta = rows_ref[:count, width : width + LANES].astype(F32)
    expert = expert_ref[0].astype(F32)
    g = jnp.sum(jnp.where(meta[:, :top] == expert, meta[:, top : 2 * top], 0.0), axis=1, keepdims=True)
    lane = lax.broadcasted_iota(jnp.int32, (count, LANES), 1)
    mark = jnp.where((meta == expert) & (lane < top), 1.0, 0.0)
    wg = jnp.concatenate([wg0[...], wg1[...]], axis=0)
    wu = jnp.concatenate([wu0[...], wu1[...]], axis=0)
    wd = jnp.concatenate([wd0[...], wd1[...]], axis=0)
    pre_gate = dot(x, wg, INNER)
    pre_up = dot(x, wu, INNER)
    back = dot(dy, wd, INNER)
    sigma = jax.nn.sigmoid(pre_gate)
    active = pre_gate * sigma
    hidden = (active * pre_up).astype(BF).astype(F32)
    gate_part = jnp.sum(hidden * back, axis=1, keepdims=True)
    d_hidden = g * back
    d_pre_gate = d_hidden * pre_up * sigma * (1.0 + pre_gate * (1.0 - sigma))
    d_pre_up = d_hidden * active
    scaled = g * hidden
    mine_ref, theirs_ref = refs[-2:]
    for i, (left, right) in enumerate(((d_pre_gate, x), (d_pre_up, x), (scaled, dy))):
        grad = dot(left.T.astype(BF), right, PLAIN).astype(BF)
        mine_ref[i] = grad[:fq]
        theirs_ref[i] = grad[fq:]
    x_part = dot(d_pre_gate.astype(BF), wg, PLAIN) + dot(d_pre_up.astype(BF), wu, PLAIN)
    lanes = gate_part * mark
    if not last:
        sum_ref = refs[0]
        sum_ref[:, :width] = x_part
        sum_ref[:, width:] = lanes
    else:
        sum_ref, reply_ref = refs[:2]
        lanes = (lanes + sum_ref[:, width:]).astype(BF)
        for h in range(2):
            at = h * half
            reply_ref[h, :, :half] = (x_part[:, at : at + half] + sum_ref[:, at : at + half]).astype(BF)
            reply_ref[h, :, half:] = lanes


def combine_body(pick_ref, home_ref, terms_ref):
    terms_ref[...] = dot(pick_ref[...], home_ref[...], PLAIN).astype(BF)


def shards(tokens, cotangent, expert_ids, gates, w_gate, w_up, w_down):
    rows, width = tokens.shape
    top = expert_ids.shape[1]
    fq = w_gate.shape[2]
    sizes = tuple(lax.axis_size(a) for a in AXES)
    nh, _, _, cols = sizes
    col = lax.axis_index("expert")
    block = lax.axis_index("zh") // (nh // EL)
    half = width // 2
    slots = cols * CAP
    wide = width + LANES
    thin = half + LANES
    pairs = mirror(sizes)
    shape = jax.ShapeDtypeStruct

    def core_swap(v):
        return lax.ppermute(v, "core", [(0, 1), (1, 0)])

    def chip_swap(v):
        return lax.ppermute(v, "zq", [(0, 1), (1, 0)])

    pad = jnp.zeros((rows, LANES - 2 * top), BF)
    body = jnp.where(col < cols // 2, tokens, cotangent)
    packed = jnp.concatenate([body, expert_ids.astype(BF), gates, pad], axis=1)
    whole = lax.ppermute(packed, AXES, pairs)

    own = [w_gate[0, 0], w_up[0, 0], w_down[0, 0]]
    near = [v for w in own for v in (w, core_swap(w))]
    later, whole = lax.optimization_barrier((own, whole))
    far = [chip_swap(w) for w in later]
    far = [v for w in far for v in (w, core_swap(w))]

    chosen, pick = call(
        functools.partial(select_body, top, width),
        (block.astype(jnp.int32)[None], whole),
        (shape((slots, wide), BF), shape((rows, slots), BF)),
        2 * slots * rows * wide,
    )
    got = lax.all_to_all(chosen.reshape(cols, CAP, wide), "expert", 0, 0, tiled=True).reshape(slots, wide)

    expert = (col * EL + block).astype(jnp.int32)[None]
    work = 16 * (slots // 2) * width * 2 * fq
    weight_shape = shape((3, fq, width), BF)
    partial, near_mine, near_theirs = call(
        functools.partial(layer_body, top, False),
        (expert, got, *near),
        (shape((slots // 2, wide), F32), weight_shape, weight_shape),
        work,
    )
    reply, far_mine, far_theirs = call(
        functools.partial(layer_body, top, True),
        (expert, got, *far, partial),
        (shape((2, slots // 2, thin), BF), weight_shape, weight_shape),
        work,
    )

    home = lax.all_to_all(reply.reshape(cols, CAP, thin), "expert", 0, 0, tiled=True)
    (terms,) = call(combine_body, (pick, home.reshape(slots, thin)), (shape((rows, thin), BF),), 2 * slots * rows * thin)
    terms = lax.ppermute(terms, AXES, pairs)
    spread = lax.all_to_all(terms.reshape(cols, rows // cols, thin), "expert", 0, 0, tiled=True)
    total = jnp.sum(spread.reshape(2, cols // 2, rows // cols, thin), axis=1, dtype=F32)
    d_tokens = jnp.concatenate([total[0, :, :half], total[1, :, :half]], axis=1).astype(BF)
    d_gates = total[0, :, half : half + top]

    far_sum = (far_mine.astype(F32) + core_swap(far_theirs).astype(F32)).astype(BF)
    near_sum = near_mine.astype(F32) + core_swap(near_theirs).astype(F32)
    grads = (near_sum + chip_swap(far_sum).astype(F32)).astype(BF)
    return (d_tokens, d_gates, grads[0][None, None], grads[1][None, None], grads[2][None, None])


def solution(mesh):
    devices = mesh.devices
    inner = Mesh(devices.reshape(devices.shape[0] // 4, 2, 2, devices.shape[1]), AXES)
    dp = AXES[:3]
    tok = P(dp, None)
    wt = P("expert", dp, None, None)
    out = P(AXES, None)
    return jax.shard_map(
        shards,
        mesh=inner,
        in_specs=(tok, tok, tok, tok, wt, wt, wt),
        out_specs=(out, out, wt, wt, wt),
        check_vma=False,
    )
```

time: 235 us -> 221 us (0.940)
  matrix products: 23.6 us -> 0 us
  Pallas kernels: 0 us -> 16.1 us
  waiting for transfers between devices: 60.9 us -> 69.2 us
  local copies, waits for them, and re-layouts: 18 us -> 10.7 us
  blocking collectives: 40.4 us -> 35.9 us
  other arithmetic: 12 us -> 8.87 us
    dot_general x19 -> x0, matrix products: 23.6 us -> none  [dot(): return lax.dot_general(a, b, (dims, ((), ())), preferred_element_type=F32)]
    pallas_call x0 -> x4, Pallas kernels: none -> 16.1 us  [call(): pl.pallas_call(body, out_shape=outs, in_specs=[smem if a.dtype == jnp.int...]
    concatenate x4 -> x0, local copies, waits for them, and re-layouts: 4.85 us -> none  [the longest x1 1.87 us: shards(): jnp.concatenate([x_part[:, half:], lanes], axis=1)]
    ppermute x4, waiting for transfers between devices: 17.2 us -> 22 us  [chip_swap(): return lax.ppermute(v, 'zq', [(0, 1), (1, 0)])]
    all_to_all x1, blocking collectives: 40.4 us -> 35.9 us  [shards(): lax.all_to_all(terms.reshape(cols, rows // cols, thin), 'expert', 0, 0, t...]
    another operation x4 -> x1, other arithmetic: 3.82 us -> 0.01 us  [the longest x2 2.68 us: layer(): theirs = jnp.stack([v[half:] for v in grads])]
    another operation x4 -> x0, local copies, waits for them, and re-layouts: 3.2 us -> none  [layer(): mine = jnp.stack([v[:half] for v in grads])]
    all_to_all x1, waiting for transfers between devices: 8.89 us -> 11.6 us  [shards(): lax.all_to_all(reply.reshape(cols, CAP, thin), 'expert', 0, 0, tiled=True)]
  transfers between devices with their start and end apart: 16 -> 16, of which waited for: 6 -> 6; matrix products, arithmetic and copies ran while one was open for 10% -> 2% of each run, Pallas kernels for 0% -> 3%
where the time goes in v3:
time: 221 us; the launch traced here: 220 us
  starting transfers between devices  77.8 us (35%)
  waiting for transfers between devices  69.2 us (31%)
  blocking collectives  35.9 us (16%)
  Pallas kernels  16.1 us (7%)
  local copies, waits for them, and re-layouts  10.7 us (5%)
  other arithmetic  8.87 us (4%)
    all_to_all x1, starting transfers between devices, shards(): lax.all_to_all(chosen.reshape(cols, CAP, wide), 'expert', 0, 0, tiled=True)  37.3 us
    all_to_all x1, blocking collectives, shards(): lax.all_to_all(terms.reshape(cols, rows // cols, thin), 'expert', 0, 0, t...  35.9 us
    ppermute x1, waiting for transfers between devices, shards(): terms = lax.ppermute(terms, AXES, pairs)  26.7 us
    ppermute x4, waiting for transfers between devices, chip_swap(): return lax.ppermute(v, 'zq', [(0, 1), (1, 0)])  22 us
    ppermute x8, starting transfers between devices, core_swap(): return lax.ppermute(v, 'core', [(0, 1), (1, 0)])  16.3 us
    pallas_call x4, Pallas kernels, call(): pl.pallas_call(body, out_shape=outs, in_specs=[smem if a.dtype == jnp.int...  16.1 us
    all_to_all x1, waiting for transfers between devices, shards(): lax.all_to_all(reply.reshape(cols, CAP, thin), 'expert', 0, 0, tiled=True)  11.6 us
    ppermute x4, starting transfers between devices, chip_swap(): return lax.ppermute(v, 'zq', [(0, 1), (1, 0)])  9.95 us
  transfers between devices with their start and end apart: 16, of which 6 were waited for; matrix products, arithmetic and copies ran while one was open for 2% of the time, Pallas kernels for 3%

profile of v3, /device:TPU:32, one launch (start us, length us, event | category | flops | bytes accessed | tf_op | source)
XLA Modules:
  0.0 219.6 jit_solution(3146885396636496750)
XLA Ops:
  0.6 0.7 convert_element_type.31
  1.3 0.1 copy.12
  1.5 0.8 copy.13
  2.3 1.1 broadcast_select_fusion
  3.4 0.3 concatenate.7
  3.7 5.2 %collective-permute-start = (bf16[128,2176]{1,0:T(8,128)(2,1)S(1)}, bf16[128,2176]{1,0:T(8,128)(2,1)S(1)}, u32[]{:S(2)}, u32[]{:S(2)}) collective-permute-start(bf16[128,2176]{1,0:T(8,128)(2,1)S(1)} %concatenate.7), channel_id=1, source_target_pairs={{0,0},{1,65},{2,130},{3,195},{4,260},{5,325},{6,390},{7,455},{8,8}... | collective-permute-start | bytes 1671176 | tf_op jit(solution)/shard_map/ppermute | solution.py:139
  8.9 8.9 %collective-permute-done.whole_ref = bf16[128,2176]{1,0:T(8,128)(2,1)S(1)} collective-permute-done((bf16[128,2176]{1,0:T(8,128)(2,1)S(1)}, bf16[128,2176]{1,0:T(8,128)(2,1)S(1)}, u32[]{:S(2)}, u32[]{:S(2)}) %collective-permute-start) | collective-permute-done | bytes 557088 | tf_op jit(solution)/shard_map/ppermute | solution.py:139
  17.8 2.6 %shard_map.110 = (bf16[512,2176]{1,0:T(8,128)(2,1)}, bf16[128,512]{1,0:T(8,128)(2,1)S(1)}) custom-call(s32[1]{0:T(128)} %bitcast.block_ref, bf16[128,2176]{1,0:T(8,128)(2,1)S(1)} %collective-permute-done.whole_ref), custom_call_target="tpu_custom_call" | custom-call | flops 285212672 | bytes 2916356 | tf_op jit(solution)/shard_map/pallas_call | solution.py:41
  20.4 37.3 %all-to-all-start = ((bf16[16,32,2176]{2,1,0:T(8,128)(2,1)}), bf16[16,32,2176]{2,1,0:T(8,128)(2,1)}, u32[]{:S(2)}, u32[]{:S(2)}) async-start(bf16[16,32,2176]{2,1,0:T(8,128)(2,1)} %bitcast.5), calls=%async_computation | async-start | bytes 4456448 | tf_op jit(solution)/shard_map/all_to_all | solution.py:153
  57.8 1.9 collective-permute-start.7
  59.7 1.9 collective-permute-start.1
  61.6 3.9 %collective-permute-start.3 = (bf16[128,2048]{1,0:T(8,128)(2,1)S(1)}, bf16[128,2048]{1,0:T(8,128)(2,1)}, u32[]{:S(2)}, u32[]{:S(2)}) collective-permute-start(bf16[128,2048]{1,0:T(8,128)(2,1)S(1)} %bitcast.30), channel_id=1, source_target_pairs={{0,32},{32,0},{1,33},{33,1},{2,34},{34,2},{3,35},{35,3},{4,36},{36... | collective-permute-start | bytes 1572872 | tf_op jit(solution)/shard_map/ppermute | solution.py:134
  65.6 1.9 collective-permute-start.5
  67.5 1.9 collective-permute-start.8
  69.4 0.0 collective-permute-done.7.wg1
  69.5 0.0 copy-start.5
  69.5 0.8 copy-done.5
  70.3 2.4 %collective-permute-start.9 = (bf16[128,2048]{1,0:T(8,128)(2,1)S(1)}, bf16[128,2048]{1,0:T(8,128)(2,1)S(1)}, u32[]{:S(2)}, u32[]{:S(2)}) collective-permute-start(bf16[128,2048]{1,0:T(8,128)(2,1)S(1)} %bitcast.34), channel_id=1, source_target_pairs={{0,16},{16,0},{1,17},{17,1},{2,18},{18,2},{3,19},{19,3},{4,20},{20... | collective-permute-start | bytes 1572872 | tf_op jit(solution)/shard_map/ppermute | solution.py:131
  72.7 3.8 %collective-permute-done.1.wg0 = bf16[128,2048]{1,0:T(8,128)(2,1)} collective-permute-done((bf16[128,2048]{1,0:T(8,128)(2,1)S(1)}, bf16[128,2048]{1,0:T(8,128)(2,1)}, u32[]{:S(2)}, u32[]{:S(2)}) %collective-permute-start.1) | collective-permute-done | bytes 524320 | tf_op jit(solution)/shard_map/ppermute | solution.py:134
  76.4 1.9 collective-permute-start.2
  78.3 9.3 %collective-permute-done.3.wu0 = bf16[128,2048]{1,0:T(8,128)(2,1)} collective-permute-done((bf16[128,2048]{1,0:T(8,128)(2,1)S(1)}, bf16[128,2048]{1,0:T(8,128)(2,1)}, u32[]{:S(2)}, u32[]{:S(2)}) %collective-permute-start.3) | collective-permute-done | bytes 524320 | tf_op jit(solution)/shard_map/ppermute | solution.py:134
  87.7 1.9 collective-permute-start.4
  89.6 8.9 %collective-permute-done.5.wd0 = bf16[128,2048]{1,0:T(8,128)(2,1)} collective-permute-done((bf16[128,2048]{1,0:T(8,128)(2,1)S(1)}, bf16[128,2048]{1,0:T(8,128)(2,1)}, u32[]{:S(2)}, u32[]{:S(2)}) %collective-permute-start.5) | collective-permute-done | bytes 524320 | tf_op jit(solution)/shard_map/ppermute | solution.py:134
  98.5 1.9 collective-permute-start.6
  100.4 0.0 copy-start.7
  100.5 0.8 copy-done.7
  101.2 0.8 copy-done.9
  102.0 1.0 copy-done.6
  103.1 1.0 copy-done.8
  104.1 1.0 copy-done.10
  105.2 6.1 %shard_map.111 = (f32[256,2176]{1,0:T(8,128)}, bf16[3,128,2048]{2,1,0:T(8,128)(2,1)S(1)}, bf16[3,128,2048]{2,1,0:T(8,128)(2,1)}) custom-call(s32[1]{0:T(128)} %bitcast.4.expert_ref, bf16[512,2176]{1,0:T(8,128)(2,1)} %bitcast.6.rows_ref, bf16[128,2048]{1,0:T(8,128)(2,1)S(1)} %bitcast.29, bf16[128,2048]{1,0:T(8,128)(2,1)S(1)} %copy-done.6, ...), custom_call_target="tpu_custom_call" | custom-call | flops 2147483648 | bytes 10747908 | tf_op jit(solution)/shard_map/pallas_call | solution.py:41
  111.3 7.0 %shard_map.112 = (bf16[2,256,1152]{2,1,0:T(8,128)(2,1)S(1)}, bf16[3,128,2048]{2,1,0:T(8,128)(2,1)S(1)}, bf16[3,128,2048]{2,1,0:T(8,128)(2,1)}) custom-call(s32[1]{0:T(128)} %bitcast.4.expert_ref, bf16[512,2176]{1,0:T(8,128)(2,1)} %bitcast.6.rows_ref, bf16[128,2048]{1,0:T(8,128)(2,1)} %collective-permute-done.1.wg0, ...), custom_call_target="tpu_custom_call" | custom-call | flops 2147483648 | bytes 11927556 | tf_op jit(solution)/shard_map/pallas_call | solution.py:41
  118.4 1.1 copy-done
  119.5 1.0 copy-done.1
  120.5 2.4 %collective-permute-start.12 = (bf16[3,128,2048]{2,1,0:T(8,128)(2,1)}, bf16[3,128,2048]{2,1,0:T(8,128)(2,1)}, u32[]{:S(2)}, u32[]{:S(2)}) collective-permute-start(bf16[3,128,2048]{2,1,0:T(8,128)(2,1)} %get-tuple-element.28), channel_id=1, source_target_pairs={{0,16},{16,0},{1,17},{17,1},{2,18},{18,2},{3,19},{19,3},{4,20},{20... | collective-permute-start | bytes 4718600 | tf_op jit(solution)/shard_map/ppermute | solution.py:131
  122.9 7.2 %all-to-all-start.1 = ((bf16[16,32,1152]{2,1,0:T(8,128)(2,1)}), bf16[16,32,1152]{2,1,0:T(8,128)(2,1)S(1)}, u32[]{:S(2)}, u32[]{:S(2)}) async-start(bf16[16,32,1152]{2,1,0:T(8,128)(2,1)} %bitcast.26), calls=%async_computation.1 | async-start | bytes 2359296 | tf_op jit(solution)/shard_map/all_to_all | solution.py:171
  130.1 1.9 collective-permute-start.11
  132.1 3.7 %add_convert_fusion.1 = bf16[3,128,2048]{2,1,0:T(8,128)(2,1)} fusion(bf16[3,128,2048]{2,1,0:T(8,128)(2,1)} %collective-permute-done.12, bf16[3,128,2048]{2,1,0:T(8,128)(2,1)} %copy-done), kind=kLoop, calls=%fused_computation.1 | loop fusion | flops 3145728 | bytes 4718592 | tf_op jit(solution)/shard_map/convert_element_type | solution.py:179
  135.8 2.2 collective-permute-start.13
  138.0 11.6 %all-to-all-done.1 = bf16[16,32,1152]{2,1,0:T(8,128)(2,1)S(1)} async-done(((bf16[16,32,1152]{2,1,0:T(8,128)(2,1)}), bf16[16,32,1152]{2,1,0:T(8,128)(2,1)S(1)}, u32[]{:S(2)}, u32[]{:S(2)}) %all-to-all-start.1) | async-done | bytes 1179680 | tf_op jit(solution)/shard_map/all_to_all | solution.py:171
  149.5 0.3 shard_map.113
  149.9 1.9 collective-permute-start.10
  151.8 26.7 %collective-permute-done.10 = bf16[128,1152]{1,0:T(8,128)(2,1)S(1)} collective-permute-done((bf16[128,1152]{1,0:T(8,128)(2,1)S(1)}, bf16[128,1152]{1,0:T(8,128)(2,1)S(1)}, u32[]{:S(2)}, u32[]{:S(2)}) %collective-permute-start.10) | collective-permute-done | bytes 294944 | tf_op jit(solution)/shard_map/ppermute | solution.py:173
  178.5 35.9 %all_to_all.15 = bf16[16,8,1152]{2,1,0:T(8,128)(2,1)S(1)} all-to-all(bf16[16,8,1152]{2,1,0:T(8,128)(2,1)S(1)} %bitcast.36), channel_id=1, replica_groups=mesh['zh'=8,'zq'=2,'core'=2,'expert'=16] {'expert'}, dimensions={0} | all-to-all | bytes 589824 | tf_op jit(solution)/shard_map/all_to_all | solution.py:174
  214.4 0.6 slice_bitcast_fusion.5
  215.0 0.6 pad_maximum_fusion
  215.7 2.7 %add_convert_fusion = bf16[3,128,2048]{2,1,0:T(8,128)(2,1)S(1)} fusion(bf16[3,128,2048]{2,1,0:T(8,128)(2,1)} %collective-permute-done.13, bf16[3,128,2048]{2,1,0:T(8,128)(2,1)} %collective-permute-done.11, bf16[3,128,2048]{2,1,0:T(8,128)(2,1)S(1)} %get-tuple-element.25), kind=kLoop, calls=%fused_computation | loop fusion | flops 4718592 | bytes 6291456 | tf_op jit(solution)/shard_map/convert_element_type | solution.py:181
  218.4 1.2 slice_bitcast_fusion
  (25 shorter events, 0.1 us)
Async XLA Ops:
  3.7 14.1 %collective-permute-start = (bf16[128,2176]{1,0:T(8,128)(2,1)S(1)}, bf16[128,2176]{1,0:T(8,128)(2,1)S(1)}, u32[]{:S(2)}, u32[]{:S(2)}) collective-permute-start(bf16[128,2176]{1,0:T(8,128)(2,1)S(1)} %concatenate.7), channel_id=1, source_target_pairs={{0,0},{1,65},{2,130},{3,195},{4,260},{5,325},{6,390},{7,455},{8,8}... | collective-permute-start | bytes 1671176 | tf_op jit(solution)/shard_map/ppermute | solution.py:139
  20.4 37.3 %copy-start.2 = (bf16[1,1,128,2048]{3,2,1,0:T(8,128)(2,1)S(1)}, bf16[1,1,128,2048]{3,2,1,0:T(8,128)(2,1)}, u32[]{:S(2)}) copy-start(bf16[1,1,128,2048]{3,2,1,0:T(8,128)(2,1)} %param.11) | copy-start | bytes 1572868
  20.4 41.2 %copy-start.3 = (bf16[1,1,128,2048]{3,2,1,0:T(8,128)(2,1)S(1)}, bf16[1,1,128,2048]{3,2,1,0:T(8,128)(2,1)}, u32[]{:S(2)}) copy-start(bf16[1,1,128,2048]{3,2,1,0:T(8,128)(2,1)} %param.12) | copy-start | bytes 1572868
  20.4 45.1 %copy-start.4 = (bf16[1,1,128,2048]{3,2,1,0:T(8,128)(2,1)S(1)}, bf16[1,1,128,2048]{3,2,1,0:T(8,128)(2,1)}, u32[]{:S(2)}) copy-start(bf16[1,1,128,2048]{3,2,1,0:T(8,128)(2,1)} %param.13) | copy-start | bytes 1572868
  20.4 81.6 %all-to-all-start = ((bf16[16,32,2176]{2,1,0:T(8,128)(2,1)}), bf16[16,32,2176]{2,1,0:T(8,128)(2,1)}, u32[]{:S(2)}, u32[]{:S(2)}) async-start(bf16[16,32,2176]{2,1,0:T(8,128)(2,1)} %bitcast.5), calls=%async_computation | async-start | bytes 4456448 | tf_op jit(solution)/shard_map/all_to_all | solution.py:153
  57.8 11.7 %collective-permute-start.7 = (bf16[128,2048]{1,0:T(8,128)(2,1)S(1)}, bf16[128,2048]{1,0:T(8,128)(2,1)S(1)}, u32[]{:S(2)}, u32[]{:S(2)}) collective-permute-start(bf16[128,2048]{1,0:T(8,128)(2,1)S(1)} %bitcast.27), channel_id=1, source_target_pairs={{0,16},{16,0},{1,17},{17,1},{2,18},{18,2},{3,19},{19,3},{4,20},{20... | collective-permute-start | bytes 1572872 | tf_op jit(solution)/shard_map/ppermute | solution.py:131
  59.7 16.7 %collective-permute-start.1 = (bf16[128,2048]{1,0:T(8,128)(2,1)S(1)}, bf16[128,2048]{1,0:T(8,128)(2,1)}, u32[]{:S(2)}, u32[]{:S(2)}) collective-permute-start(bf16[128,2048]{1,0:T(8,128)(2,1)S(1)} %bitcast.28), channel_id=1, source_target_pairs={{0,32},{32,0},{1,33},{33,1},{2,34},{34,2},{3,35},{35,3},{4,36},{36... | collective-permute-start | bytes 1572872 | tf_op jit(solution)/shard_map/ppermute | solution.py:134
  61.6 26.0 %collective-permute-start.3 = (bf16[128,2048]{1,0:T(8,128)(2,1)S(1)}, bf16[128,2048]{1,0:T(8,128)(2,1)}, u32[]{:S(2)}, u32[]{:S(2)}) collective-permute-start(bf16[128,2048]{1,0:T(8,128)(2,1)S(1)} %bitcast.30), channel_id=1, source_target_pairs={{0,32},{32,0},{1,33},{33,1},{2,34},{34,2},{3,35},{35,3},{4,36},{36... | collective-permute-start | bytes 1572872 | tf_op jit(solution)/shard_map/ppermute | solution.py:134
  65.6 32.9 %collective-permute-start.5 = (bf16[128,2048]{1,0:T(8,128)(2,1)S(1)}, bf16[128,2048]{1,0:T(8,128)(2,1)}, u32[]{:S(2)}, u32[]{:S(2)}) collective-permute-start(bf16[128,2048]{1,0:T(8,128)(2,1)S(1)} %bitcast.33), channel_id=1, source_target_pairs={{0,32},{32,0},{1,33},{33,1},{2,34},{34,2},{3,35},{35,3},{4,36},{36... | collective-permute-start | bytes 1572872 | tf_op jit(solution)/shard_map/ppermute | solution.py:134
  67.5 32.9 %collective-permute-start.8 = (bf16[128,2048]{1,0:T(8,128)(2,1)S(1)}, bf16[128,2048]{1,0:T(8,128)(2,1)S(1)}, u32[]{:S(2)}, u32[]{:S(2)}) collective-permute-start(bf16[128,2048]{1,0:T(8,128)(2,1)S(1)} %bitcast.31), channel_id=1, source_target_pairs={{0,16},{16,0},{1,17},{17,1},{2,18},{18,2},{3,19},{19,3},{4,20},{20... | collective-permute-start | bytes 1572872 | tf_op jit(solution)/shard_map/ppermute | solution.py:131
  69.5 0.8 copy-start.5
  70.3 31.0 %collective-permute-start.9 = (bf16[128,2048]{1,0:T(8,128)(2,1)S(1)}, bf16[128,2048]{1,0:T(8,128)(2,1)S(1)}, u32[]{:S(2)}, u32[]{:S(2)}) collective-permute-start(bf16[128,2048]{1,0:T(8,128)(2,1)S(1)} %bitcast.34), channel_id=1, source_target_pairs={{0,16},{16,0},{1,17},{17,1},{2,18},{18,2},{3,19},{19,3},{4,20},{20... | collective-permute-start | bytes 1572872 | tf_op jit(solution)/shard_map/ppermute | solution.py:131
  76.4 34.9 %collective-permute-start.2 = (bf16[128,2048]{1,0:T(8,128)(2,1)}, bf16[128,2048]{1,0:T(8,128)(2,1)}, u32[]{:S(2)}, u32[]{:S(2)}) collective-permute-start(bf16[128,2048]{1,0:T(8,128)(2,1)} %collective-permute-done.1.wg0), channel_id=1, source_target_pairs={{0,16},{16,0},{1,17},{17,1},{2,18},{18,2},{3,19},{19,3},{4,20},{20... | collective-permute-start | bytes 1572872 | tf_op jit(solution)/shard_map/ppermute | solution.py:131
  87.7 23.7 %collective-permute-start.4 = (bf16[128,2048]{1,0:T(8,128)(2,1)}, bf16[128,2048]{1,0:T(8,128)(2,1)}, u32[]{:S(2)}, u32[]{:S(2)}) collective-permute-start(bf16[128,2048]{1,0:T(8,128)(2,1)} %collective-permute-done.3.wu0), channel_id=1, source_target_pairs={{0,16},{16,0},{1,17},{17,1},{2,18},{18,2},{3,19},{19,3},{4,20},{20... | collective-permute-start | bytes 1572872 | tf_op jit(solution)/shard_map/ppermute | solution.py:131
  98.5 12.8 %collective-permute-start.6 = (bf16[128,2048]{1,0:T(8,128)(2,1)}, bf16[128,2048]{1,0:T(8,128)(2,1)}, u32[]{:S(2)}, u32[]{:S(2)}) collective-permute-start(bf16[128,2048]{1,0:T(8,128)(2,1)} %collective-permute-done.5.wd0), channel_id=1, source_target_pairs={{0,16},{16,0},{1,17},{17,1},{2,18},{18,2},{3,19},{19,3},{4,20},{20... | collective-permute-start | bytes 1572872 | tf_op jit(solution)/shard_map/ppermute | solution.py:131
  100.4 0.8 copy-start.7
  101.2 0.8 copy-start.9
  102.0 1.0 copy-start.6
  103.1 1.0 copy-start.8
  104.1 1.0 copy-start.10
  118.4 1.1 copy-start
  119.5 1.0 copy-start.1
  120.5 11.5 %collective-permute-start.12 = (bf16[3,128,2048]{2,1,0:T(8,128)(2,1)}, bf16[3,128,2048]{2,1,0:T(8,128)(2,1)}, u32[]{:S(2)}, u32[]{:S(2)}) collective-permute-start(bf16[3,128,2048]{2,1,0:T(8,128)(2,1)} %get-tuple-element.28), channel_id=1, source_target_pairs={{0,16},{16,0},{1,17},{17,1},{2,18},{18,2},{3,19},{19,3},{4,20},{20... | collective-permute-start | bytes 4718600 | tf_op jit(solution)/shard_map/ppermute | solution.py:131
  122.9 26.6 %all-to-all-start.1 = ((bf16[16,32,1152]{2,1,0:T(8,128)(2,1)}), bf16[16,32,1152]{2,1,0:T(8,128)(2,1)S(1)}, u32[]{:S(2)}, u32[]{:S(2)}) async-start(bf16[16,32,1152]{2,1,0:T(8,128)(2,1)} %bitcast.26), calls=%async_computation.1 | async-start | bytes 2359296 | tf_op jit(solution)/shard_map/all_to_all | solution.py:171
  130.1 85.5 %collective-permute-start.11 = (bf16[3,128,2048]{2,1,0:T(8,128)(2,1)}, bf16[3,128,2048]{2,1,0:T(8,128)(2,1)}, u32[]{:S(2)}, u32[]{:S(2)}) collective-permute-start(bf16[3,128,2048]{2,1,0:T(8,128)(2,1)} %get-tuple-element.26), channel_id=1, source_target_pairs={{0,16},{16,0},{1,17},{17,1},{2,18},{18,2},{3,19},{19,3},{4,20},{20... | collective-permute-start | bytes 4718600 | tf_op jit(solution)/shard_map/ppermute | solution.py:131
  135.8 79.9 %collective-permute-start.13 = (bf16[3,128,2048]{2,1,0:T(8,128)(2,1)}, bf16[3,128,2048]{2,1,0:T(8,128)(2,1)}, u32[]{:S(2)}, u32[]{:S(2)}) collective-permute-start(bf16[3,128,2048]{2,1,0:T(8,128)(2,1)} %add_convert_fusion.1), channel_id=1, source_target_pairs={{0,32},{32,0},{1,33},{33,1},{2,34},{34,2},{3,35},{35,3},{4,36},{36... | collective-permute-start | bytes 4718600 | tf_op jit(solution)/shard_map/ppermute | solution.py:134
  149.9 28.6 %collective-permute-start.10 = (bf16[128,1152]{1,0:T(8,128)(2,1)S(1)}, bf16[128,1152]{1,0:T(8,128)(2,1)S(1)}, u32[]{:S(2)}, u32[]{:S(2)}) collective-permute-start(bf16[128,1152]{1,0:T(8,128)(2,1)S(1)} %shard_map.113), channel_id=1, source_target_pairs={{0,0},{1,65},{2,130},{3,195},{4,260},{5,325},{6,390},{7,455},{8,8}... | collective-permute-start | bytes 884744 | tf_op jit(solution)/shard_map/ppermute | solution.py:173

commit v4 on v3

v4 whole, which is shorter than its diff:
```python
import functools

import jax
import jax.numpy as jnp
from jax import lax
from jax.experimental import pallas as pl
from jax.experimental.pallas import tpu as pltpu
from jax.sharding import Mesh, PartitionSpec as P

BF = jnp.bfloat16
F32 = jnp.float32
EL = 4
CAP = 32
LANES = 128
INNER = ((1,), (1,))
PLAIN = ((1,), (0,))
AXES = ("zb", "zl", "core", "expert")
VMEM_BYTES = 28 << 20


def dot(a, b, dims):
    return lax.dot_general(a, b, (dims, ((), ())), preferred_element_type=F32)


def call(body, args, outs, flops):
    vmem = pl.BlockSpec(memory_space=pltpu.VMEM)
    smem = pl.BlockSpec(memory_space=pltpu.SMEM)
    moved = sum(a.size * a.dtype.itemsize for a in list(args) + list(outs))
    return pl.pallas_call(
        body,
        out_shape=outs,
        in_specs=[smem if a.dtype == jnp.int32 else vmem for a in args],
        out_specs=[vmem] * len(outs),
        compiler_params=pltpu.CompilerParams(vmem_limit_bytes=VMEM_BYTES),
        cost_estimate=pl.CostEstimate(flops=flops, bytes_accessed=moved, transcendentals=0),
    )(*args)


def select_body(top, width, block_ref, whole_ref, chosen_ref, pick_ref):
    rows, slots = pick_ref.shape
    meta = whole_ref[:, width : width + LANES].astype(F32)
    slot = lax.broadcasted_iota(jnp.int32, (1, slots), 1)
    wanted = (slot // CAP * EL + block_ref[0]).astype(F32)
    named = meta[:, 0:1] == wanted
    for k in range(1, top):
        named = named | (meta[:, k : k + 1] == wanted)
    earlier = lax.broadcasted_iota(jnp.int32, (rows, rows), 0) > lax.broadcasted_iota(jnp.int32, (rows, rows), 1)
    rank = dot(earlier.astype(F32).astype(BF), named.astype(F32).astype(BF), PLAIN)
    pick = jnp.where(named & (rank == (slot % CAP).astype(F32)), 1.0, 0.0)
    pick_ref[...] = pick.astype(BF)
    chosen_ref[...] = dot(pick.T.astype(BF), whole_ref[...], PLAIN).astype(BF)


def both(a_ref, b_ref, i):
    return jnp.concatenate([a_ref[i], b_ref[i]], axis=0)


def hidden_grads(top, expert_ref, rows_ref, a_ref, b_ref, mine_ref, theirs_ref):
    _, fq, width = a_ref.shape
    count = rows_ref.shape[0] // 2
    x = rows_ref[:count, :width]
    dy = rows_ref[count:, :width]
    meta = rows_ref[:count, width : width + LANES].astype(F32)
    expert = expert_ref[0].astype(F32)
    g = jnp.sum(jnp.where(meta[:, :top] == expert, meta[:, top : 2 * top], 0.0), axis=1, keepdims=True)
    lane = lax.broadcasted_iota(jnp.int32, (count, LANES), 1)
    mark = jnp.where((meta == expert) & (lane < top), 1.0, 0.0)
    pre_gate = dot(x, both(a_ref, b_ref, 0), INNER)
    pre_up = dot(x, both(a_ref, b_ref, 1), INNER)
    back = dot(dy, both(a_ref, b_ref, 2), INNER)
    sigma = jax.nn.sigmoid(pre_gate)
    active = pre_gate * sigma
    hidden = (active * pre_up).astype(BF).astype(F32)
    lanes = jnp.sum(hidden * back, axis=1, keepdims=True) * mark
    d_hidden = g * back
    d_pre_gate = d_hidden * pre_up * sigma * (1.0 + pre_gate * (1.0 - sigma))
    d_pre_up = d_hidden * active
    scaled = g * hidden
    for i, (left, right) in enumerate(((d_pre_gate, x), (d_pre_up, x), (scaled, dy))):
        grad = dot(left.T.astype(BF), right, PLAIN).astype(BF)
        mine_ref[i] = grad[:fq]
        theirs_ref[i] = grad[fq:]
    return d_pre_gate.astype(BF), d_pre_up.astype(BF), lanes


def near_body(top, expert_ref, rows_ref, a_ref, b_ref, sum_ref, mine_ref, theirs_ref):
    width = a_ref.shape[2]
    d_gate, d_up, lanes = hidden_grads(top, expert_ref, rows_ref, a_ref, b_ref, mine_ref, theirs_ref)
    sum_ref[:, :width] = dot(d_gate, both(a_ref, b_ref, 0), PLAIN) + dot(d_up, both(a_ref, b_ref, 1), PLAIN)
    sum_ref[:, width:] = lanes


def far_body(top, expert_ref, rows_ref, a_ref, b_ref, gate_ref, up_ref, lanes_ref, mine_ref, theirs_ref):
    gate_ref[...], up_ref[...], lanes_ref[...] = hidden_grads(
        top, expert_ref, rows_ref, a_ref, b_ref, mine_ref, theirs_ref
    )


def reply_body(gate_ref, up_ref, lanes_ref, a_ref, b_ref, sum_ref, reply_ref):
    width = a_ref.shape[2]
    half = width // 2
    lanes = (lanes_ref[...] + sum_ref[:, width:]).astype(BF)
    x_part = dot(gate_ref[...], both(a_ref, b_ref, 0), PLAIN) + dot(up_ref[...], both(a_ref, b_ref, 1), PLAIN)
    for h in range(2):
        at = h * half
        reply_ref[h, :, :half] = (x_part[:, at : at + half] + sum_ref[:, at : at + half]).astype(BF)
        reply_ref[h, :, half:] = lanes


def combine_body(pick_ref, home_ref, terms_ref):
    terms_ref[...] = dot(pick_ref[...], home_ref[...], PLAIN).astype(BF)


def shards(tokens, cotangent, expert_ids, gates, w_gate, w_up, w_down):
    rows, width = tokens.shape
    top = expert_ids.shape[1]
    fq = w_gate.shape[2]
    nb, nl, _, cols = (lax.axis_size(a) for a in AXES)
    nz = nb * nl
    col = lax.axis_index("expert")
    block = lax.axis_index("zb")
    half = width // 2
    part = rows // cols
    slots = cols * CAP
    wide = width + LANES
    thin = half + LANES
    shape = jax.ShapeDtypeStruct
    neighbours = [(i, (i + 1) % nz if i % 2 else (i - 1) % nz) for i in range(nz)]

    def core_swap(v):
        return lax.ppermute(v, "core", [(0, 1), (1, 0)])

    def chip_swap(v):
        return lax.ppermute(v, "zl", [(i, i ^ 1) for i in range(nl)])

    def near_plane(v):
        return lax.ppermute(v, ("zb", "zl"), neighbours)

    def mine(v):
        return lax.dynamic_slice_in_dim(v, col * part, part, axis=0)

    meta = [mine(expert_ids).astype(BF), mine(gates), jnp.zeros((part, LANES - 2 * top), BF)]
    packed = jnp.stack([jnp.concatenate([mine(v), *meta], axis=1) for v in (tokens, cotangent)])
    quad = lax.all_to_all(jnp.broadcast_to(packed, (nb, 2, part, wide)), "zb", 0, 0, tiled=True)
    slices = jnp.stack([quad, near_plane(quad)])

    own = jnp.stack([w_gate[0, 0], w_up[0, 0], w_down[0, 0]])
    own_c = core_swap(own)
    slices, own_c, later = lax.optimization_barrier((slices, own_c, own))
    far = chip_swap(later)
    far_c = core_swap(far)

    sent = slices.transpose(2, 0, 1, 3, 4).reshape(cols, part, wide)
    whole = lax.all_to_all(sent, "expert", 0, 0, tiled=True).reshape(rows, wide)

    chosen, pick = call(
        functools.partial(select_body, top, width),
        (block.astype(jnp.int32)[None], whole),
        (shape((slots, wide), BF), shape((rows, slots), BF)),
        2 * slots * rows * wide,
    )
    got = lax.all_to_all(chosen.reshape(cols, CAP, wide), "expert", 0, 0, tiled=True).reshape(slots, wide)

    expert = (col * EL + block).astype(jnp.int32)[None]
    count = slots // 2
    one = 2 * count * width * 2 * fq
    weight_shape = shape((3, fq, width), BF)
    partial, near_mine, near_theirs = call(
        functools.partial(near_body, top),
        (expert, got, own, own_c),
        (shape((count, wide), F32), weight_shape, weight_shape),
        8 * one,
    )
    pre_shape = shape((count, 2 * fq), BF)
    d_gate, d_up, lanes, far_mine, far_theirs = call(
        functools.partial(far_body, top),
        (expert, got, far, far_c),
        (pre_shape, pre_shape, shape((count, LANES), F32), weight_shape, weight_shape),
        6 * one,
    )
    far_other = core_swap(far_theirs)
    (reply,) = call(
        reply_body, (d_gate, d_up, lanes, far, far_c, partial), (shape((2, count, thin), BF),), 2 * one
    )
    far_sum = (far_mine.astype(F32) + far_other.astype(F32)).astype(BF)
    reply, far_sum = lax.optimization_barrier((reply, far_sum))
    far_in = chip_swap(far_sum)

    home = lax.all_to_all(reply.reshape(cols, CAP, thin), "expert", 0, 0, tiled=True)
    (terms,) = call(combine_body, (pick, home.reshape(slots, thin)), (shape((rows, thin), BF),), 2 * slots * rows * thin)
    spread = lax.all_to_all(terms.reshape(cols, part, thin), "expert", 0, 0, tiled=True)
    spread = spread.reshape(2, 2, nb, part, thin).transpose(1, 2, 0, 3, 4)
    here = (spread[0].astype(F32) + near_plane(spread[1]).astype(F32)).astype(BF)
    total = jnp.sum(lax.all_to_all(here, "zb", 0, 0, tiled=True), axis=0, dtype=F32)
    d_tokens = jnp.concatenate([total[0, :, :half], total[1, :, :half]], axis=1).astype(BF)
    d_gates = total[0, :, half : half + top]

    near_sum = near_mine.astype(F32) + core_swap(near_theirs).astype(F32)
    grads = [(near_sum[i] + far_in[i].astype(F32)).astype(BF)[None, None] for i in range(3)]
    return (d_tokens, d_gates, *grads)


def solution(mesh):
    devices = mesh.devices
    inner = Mesh(devices.reshape(4, devices.shape[0] // 8, 2, devices.shape[1]), AXES)
    dp = AXES[:3]
    tok = P(dp, None)
    wt = P("expert", dp, None, None)
    out = P(AXES, None)
    return jax.shard_map(
        shards,
        mesh=inner,
        in_specs=(tok, tok, tok, tok, wt, wt, wt),
        out_specs=(out, out, wt, wt, wt),
        check_vma=False,
    )
```

time: 221 us -> 208 us (0.941)
  the two profiles are of different devices: /device:TPU:32 before, /device:TPU:6 now
where the time goes in v4:
time: 208 us; the launch traced here: 207 us
  waiting for transfers between devices  74.2 us (36%)
  starting transfers between devices  59.1 us (28%)
  blocking collectives  35.8 us (17%)
  Pallas kernels  15.7 us (8%)
  other arithmetic  13.9 us (7%)
  local copies, waits for them, and re-layouts  7.26 us (3%)
    all_to_all x1, blocking collectives, shards(): lax.all_to_all(jnp.broadcast_to(packed, (nb, 2, part, wide)), 'zb', 0, 0,...  35.8 us
    ppermute x2, waiting for transfers between devices, chip_swap(): return lax.ppermute(v, 'zl', [(i, i ^ 1) for i in range(nl)])  26.7 us
    pallas_call x5, Pallas kernels, call(): pl.pallas_call(body, out_shape=outs, in_specs=[smem if a.dtype == jnp.int...  15.7 us
    all_to_all x1, waiting for transfers between devices, shards(): lax.all_to_all(reply.reshape(cols, CAP, thin), 'expert', 0, 0, tiled=True)  14.7 us
    all_to_all x1, waiting for transfers between devices, shards(): lax.all_to_all(chosen.reshape(cols, CAP, wide), 'expert', 0, 0, tiled=True)  13.7 us
    all_to_all x1, starting transfers between devices, shards(): lax.all_to_all(terms.reshape(cols, part, thin), 'expert', 0, 0, tiled=True)  9.21 us
    ppermute x4, starting transfers between devices, core_swap(): return lax.ppermute(v, 'core', [(0, 1), (1, 0)])  8 us
    all_to_all x1, waiting for transfers between devices, shards(): whole = lax.all_to_all(sent, 'expert', 0, 0, tiled=True).reshape(rows, wide)  7.84 us
  transfers between devices with their start and end apart: 13, of which 9 were waited for; matrix products, arithmetic and copies ran while one was open for 6% of the time, Pallas kernels for 5%

profile of v4, /device:TPU:6, one launch (start us, length us, event | category | flops | bytes accessed | tf_op | source)
XLA Modules:
  0.0 206.8 jit_solution(9075753797748045788)
XLA Ops:
  0.7 2.7 %pad_maximum_fusion.a_ref = bf16[3,128,2048]{2,1,0:T(8,128)(2,1)} fusion(bf16[1,128,2048]{2,1,0:T(8,128)(2,1)} %bitcast.50, bf16[1,128,2048]{2,1,0:T(8,128)(2,1)} %bitcast.51, bf16[1,128,2048]{2,1,0:T(8,128)(2,1)} %bitcast.52), kind=kLoop, calls=%fused_computation.2 | loop fusion | flops 1572864 | bytes 3145728 | tf_op jit(solution)/shard_map/stack | solution.py:147
  3.3 1.9 collective-permute-start.1
  5.3 0.1 dynamic-slice_convert_fusion
  5.3 0.1 copy.22
  5.4 0.1 constant_dynamic-slice_fusion.1
  5.5 0.1 copy.23
  5.6 0.8 constant_dynamic-slice_fusion
  6.4 0.1 concatenate.11
  6.5 0.1 concatenate.10
  6.6 35.8 %all_to_all.30 = bf16[4,2,8,2176]{3,2,1,0:T(8,128)(2,1)S(1)} all-to-all(bf16[4,2,8,2176]{3,2,1,0:T(8,128)(2,1)S(1)} %broadcast_in_dim.17), channel_id=1, replica_groups=mesh['zb'=4,'zl'=4,'core'=2,'expert'=16] {'zb'}, dimensions={0} | all-to-all | bytes 557056 | tf_op jit(solution)/shard_map/all_to_all | solution.py:144
  42.5 3.9 %collective-permute-start = (bf16[4,2,8,2176]{3,2,0,1:T(8,128)(2,1)S(1)}, bf16[4,2,8,2176]{3,2,0,1:T(8,128)(2,1)S(1)}, u32[]{:S(2)}, u32[]{:S(2)}) collective-permute-start(bf16[4,2,8,2176]{3,2,0,1:T(8,128)(2,1)S(1)} %copy.33), channel_id=1, source_target_pairs={{0,480},{32,64},{64,32},{96,128},{128,96},{160,192},{192,160},{224... | collective-permute-start | bytes 835592 | tf_op jit(solution)/shard_map/ppermute | solution.py:137
  46.3 5.8 %collective-permute-done = bf16[4,2,8,2176]{3,2,0,1:T(8,128)(2,1)S(1)} collective-permute-done((bf16[4,2,8,2176]{3,2,0,1:T(8,128)(2,1)S(1)}, bf16[4,2,8,2176]{3,2,0,1:T(8,128)(2,1)S(1)}, u32[]{:S(2)}, u32[]{:S(2)}) %collective-permute-start) | collective-permute-done | bytes 278560 | tf_op jit(solution)/shard_map/ppermute | solution.py:137
  52.1 0.9 pad_maximum_fusion.1
  53.0 1.2 copy-done.4
  54.2 4.8 %collective-permute-start.2 = (bf16[3,128,2048]{2,1,0:T(8,128)(2,1)}, bf16[3,128,2048]{2,1,0:T(8,128)(2,1)}, u32[]{:S(2)}, u32[]{:S(2)}) collective-permute-start(bf16[3,128,2048]{2,1,0:T(8,128)(2,1)} %pad_maximum_fusion.a_ref), channel_id=1, source_target_pairs={{0,32},{32,0},{64,96},{96,64},{1,33},{33,1},{65,97},{97,65},{2,34}... | collective-permute-start | bytes 4718600 | tf_op jit(solution)/shard_map/ppermute | solution.py:134
  59.0 7.4 %all-to-all-start.1 = ((bf16[16,8,2176]{2,1,0:T(8,128)(2,1)}), bf16[16,8,2176]{2,1,0:T(8,128)(2,1)S(1)}, u32[]{:S(2)}, u32[]{:S(2)}) async-start(bf16[16,8,2176]{2,1,0:T(8,128)(2,1)} %bitcast.9), calls=%async_computation.1 | async-start | bytes 1114112 | tf_op jit(solution)/shard_map/all_to_all | solution.py:154
  66.4 7.8 %all-to-all-done.1 = bf16[16,8,2176]{2,1,0:T(8,128)(2,1)S(1)} async-done(((bf16[16,8,2176]{2,1,0:T(8,128)(2,1)}), bf16[16,8,2176]{2,1,0:T(8,128)(2,1)S(1)}, u32[]{:S(2)}, u32[]{:S(2)}) %all-to-all-start.1) | async-done | bytes 557088 | tf_op jit(solution)/shard_map/all_to_all | solution.py:154
  74.3 1.3 shard_map.110
  75.6 1.4 copy-done.1
  77.0 6.1 %all-to-all-start.2 = ((bf16[16,32,2176]{2,1,0:T(8,128)(2,1)}), bf16[16,32,2176]{2,1,0:T(8,128)(2,1)S(1)}, u32[]{:S(2)}, u32[]{:S(2)}) async-start(bf16[16,32,2176]{2,1,0:T(8,128)(2,1)} %bitcast.47), calls=%async_computation.2 | async-start | bytes 4456448 | tf_op jit(solution)/shard_map/all_to_all | solution.py:162
  83.0 9.2 %collective-permute-done.2.a_ref = bf16[3,128,2048]{2,1,0:T(8,128)(2,1)} collective-permute-done((bf16[3,128,2048]{2,1,0:T(8,128)(2,1)}, bf16[3,128,2048]{2,1,0:T(8,128)(2,1)}, u32[]{:S(2)}, u32[]{:S(2)}) %collective-permute-start.2) | collective-permute-done | bytes 1572896 | tf_op jit(solution)/shard_map/ppermute | solution.py:134
  92.2 1.9 collective-permute-start.3
  94.2 13.7 %all-to-all-done.2 = bf16[16,32,2176]{2,1,0:T(8,128)(2,1)S(1)} async-done(((bf16[16,32,2176]{2,1,0:T(8,128)(2,1)}), bf16[16,32,2176]{2,1,0:T(8,128)(2,1)S(1)}, u32[]{:S(2)}, u32[]{:S(2)}) %all-to-all-start.2) | async-done | bytes 2228256 | tf_op jit(solution)/shard_map/all_to_all | solution.py:162
  107.8 4.6 %shard_map.111 = (bf16[256,256]{1,0:T(8,128)(2,1)S(1)}, bf16[256,256]{1,0:T(8,128)(2,1)S(1)}, f32[256,128]{1,0:T(8,128)S(1)}, bf16[3,128,2048]{2,1,0:T(8,128)(2,1)S(1)}, bf16[3,128,2048]{2,1,0:T(8,128)(2,1)S(1)}) custom-call(s32[1]{0:T(128)} %bitcast.11.expert_ref, bf16[512,2176]{1,0:T(8,128)(2,1)S(1)} %bitcast.45, ...), custom_call_target="tpu_custom_call" | custom-call | flops 1610612736 | bytes 8912900 | tf_op jit(solution)/shard_map/pallas_call | solution.py:29
  112.4 1.9 collective-permute-start.4
  114.4 4.6 %shard_map.112 = (f32[256,2176]{1,0:T(8,128)S(1)}, bf16[3,128,2048]{2,1,0:T(8,128)(2,1)S(1)}, bf16[3,128,2048]{2,1,0:T(8,128)(2,1)S(1)}) custom-call(s32[1]{0:T(128)} %bitcast.11.expert_ref, bf16[512,2176]{1,0:T(8,128)(2,1)S(1)} %bitcast.46, bf16[3,128,2048]{2,1,0:T(8,128)(2,1)} %pad_maximum_fusion.a_ref, bf16[3,128,2048]{2,1,0:T(8,128)(2,1)S(1)} %copy-done.5), custom_call_target="tpu_custom_call" | custom-call | flops 2147483648 | bytes 10747908 | tf_op jit(solution)/shard_map/pallas_call | solution.py:29
  118.9 1.1 copy-done.2
  120.1 4.2 %shard_map.113 = bf16[2,256,1152]{2,1,0:T(8,128)(2,1)} custom-call(bf16[256,256]{1,0:T(8,128)(2,1)S(1)} %get-tuple-element.24.gate_ref, bf16[256,256]{1,0:T(8,128)(2,1)S(1)} %get-tuple-element.25.up_ref, f32[256,128]{1,0:T(8,128)S(1)} %get-tuple-element.26.lanes_ref, bf16[3,128,2048]{2,1,0:T(8,128)(2,1)} %collective-permute-done.2.a_ref, ...), custom_call_target="tpu_custom_call" | custom-call | flops 536870912 | bytes 6946816 | tf_op jit(solution)/shard_map/pallas_call | solution.py:29
  124.3 1.8 add_convert_fusion
  126.1 7.6 %all-to-all-start.3 = ((bf16[16,32,1152]{2,1,0:T(8,128)(2,1)}), bf16[16,32,1152]{2,1,0:T(8,128)(2,1)S(1)}, u32[]{:S(2)}, u32[]{:S(2)}) async-start(bf16[16,32,1152]{2,1,0:T(8,128)(2,1)} %bitcast.14), calls=%async_computation.3 | async-start | bytes 2359296 | tf_op jit(solution)/shard_map/all_to_all | solution.py:189
  133.6 2.3 %collective-permute-start.6 = (bf16[3,128,2048]{2,1,0:T(8,128)(2,1)}, bf16[3,128,2048]{2,1,0:T(8,128)(2,1)}, u32[]{:S(2)}, u32[]{:S(2)}) collective-permute-start(bf16[3,128,2048]{2,1,0:T(8,128)(2,1)} %copy-done.6), channel_id=1, source_target_pairs={{0,16},{16,0},{1,17},{17,1},{2,18},{18,2},{3,19},{19,3},{4,20},{20... | collective-permute-start | bytes 4718600 | tf_op jit(solution)/shard_map/ppermute | solution.py:131
  135.9 14.7 %all-to-all-done.3 = bf16[16,32,1152]{2,1,0:T(8,128)(2,1)S(1)} async-done(((bf16[16,32,1152]{2,1,0:T(8,128)(2,1)}), bf16[16,32,1152]{2,1,0:T(8,128)(2,1)S(1)}, u32[]{:S(2)}, u32[]{:S(2)}) %all-to-all-start.3) | async-done | bytes 1179680 | tf_op jit(solution)/shard_map/all_to_all | solution.py:189
  150.6 1.1 shard_map.114
  151.7 9.2 %all-to-all-start.4 = ((bf16[16,8,1152]{2,1,0:T(8,128)(2,1)}), bf16[16,8,1152]{2,1,0:T(8,128)(2,1)}, u32[]{:S(2)}, u32[]{:S(2)}) async-start(bf16[16,8,1152]{2,1,0:T(8,128)(2,1)} %bitcast.16), calls=%async_computation.4 | async-start | bytes 589824 | tf_op jit(solution)/shard_map/all_to_all | solution.py:191
  160.9 2.6 %collective-permute-start.7 = (bf16[3,128,2048]{2,1,0:T(8,128)(2,1)}, bf16[3,128,2048]{2,1,0:T(8,128)(2,1)S(1)}, u32[]{:S(2)}, u32[]{:S(2)}) collective-permute-start(bf16[3,128,2048]{2,1,0:T(8,128)(2,1)} %add_convert_fusion), channel_id=1, source_target_pairs={{0,32},{32,0},{64,96},{96,64},{1,33},{33,1},{65,97},{97,65},{2,34}... | collective-permute-start | bytes 4718600 | tf_op jit(solution)/shard_map/ppermute | solution.py:134
  163.5 4.2 %all-to-all-done.4 = bf16[16,8,1152]{2,1,0:T(8,128)(2,1)} async-done(((bf16[16,8,1152]{2,1,0:T(8,128)(2,1)}), bf16[16,8,1152]{2,1,0:T(8,128)(2,1)}, u32[]{:S(2)}, u32[]{:S(2)}) %all-to-all-start.4) | async-done | bytes 294944 | tf_op jit(solution)/shard_map/all_to_all | solution.py:191
  167.8 0.9 slice_bitcast_fusion
  168.7 3.7 %collective-permute-start.5 = (bf16[4,2,8,1152]{3,2,0,1:T(8,128)(2,1)S(1)}, bf16[4,2,8,1152]{3,2,0,1:T(8,128)(2,1)S(1)}, u32[]{:S(2)}, u32[]{:S(2)}) collective-permute-start(bf16[4,2,8,1152]{3,2,0,1:T(8,128)(2,1)S(1)} %slice_bitcast_fusion), channel_id=1, source_target_pairs={{0,480},{32,64},{64,32},{96,128},{128,96},{160,192},{192,160},{224... | collective-permute-start | bytes 442376 | tf_op jit(solution)/shard_map/ppermute | solution.py:137
  172.4 3.6 %convert_add_fusion = f32[3,128,2048]{2,1,0:T(8,128)} fusion(bf16[3,128,2048]{2,1,0:T(8,128)(2,1)} %collective-permute-done.6, bf16[3,128,2048]{2,1,0:T(8,128)(2,1)S(1)} %copy-done.3), kind=kLoop, calls=%fused_computation | loop fusion | flops 2359296 | bytes 6291456 | tf_op jit(solution)/shard_map/add | solution.py:198
  176.0 0.9 collective-permute-done.5
  176.9 1.0 fusion.6
  177.9 0.7 copy.29
  178.6 5.8 %all-to-all-start.5 = ((bf16[4,2,8,1152]{3,2,1,0:T(8,128)(2,1)}), bf16[4,2,8,1152]{3,2,1,0:T(8,128)(2,1)S(1)}, u32[]{:S(2)}, u32[]{:S(2)}) async-start(bf16[4,2,8,1152]{3,2,1,0:T(8,128)(2,1)} %copy.29), calls=%async_computation.5 | async-start | bytes 294912 | tf_op jit(solution)/shard_map/all_to_all | solution.py:194
  184.4 17.5 %collective-permute-done.7 = bf16[3,128,2048]{2,1,0:T(8,128)(2,1)S(1)} collective-permute-done((bf16[3,128,2048]{2,1,0:T(8,128)(2,1)}, bf16[3,128,2048]{2,1,0:T(8,128)(2,1)S(1)}, u32[]{:S(2)}, u32[]{:S(2)}) %collective-permute-start.7) | collective-permute-done | bytes 1572896 | tf_op jit(solution)/shard_map/ppermute | solution.py:134
  201.9 3.3 %fusion.5 = (bf16[1,1,128,2048]{3,2,1,0:T(8,128)(2,1)}, bf16[1,1,128,2048]{3,2,1,0:T(8,128)(2,1)}, bf16[1,1,128,2048]{3,2,1,0:T(8,128)(2,1)}) fusion(f32[3,128,2048]{2,1,0:T(8,128)} %convert_add_fusion, bf16[3,128,2048]{2,1,0:T(8,128)(2,1)S(1)} %collective-permute-done.7), kind=kLoop, calls=%fused_computation.12 | loop fusion | flops 2359296 | bytes 6291456 | tf_op jit(solution)/shard_map/convert_element_type | solution.py:199
  205.1 0.5 all-to-all-done.5
  205.6 0.6 slice_bitcast_fusion.4
  206.2 0.6 pad_maximum_fusion.3
  (24 shorter events, 0.1 us)
Async XLA Ops:
  0.6 4.8 %copy-start = (bf16[128,8]{0,1:T(8,128)(2,1)S(1)}, bf16[128,8]{0,1:T(8,128)(2,1)}, u32[]{:S(2)}) copy-start(bf16[128,8]{0,1:T(8,128)(2,1)} %param.10) | copy-start | bytes 6148
  0.6 4.6 %copy-start.7 = (s32[128,8]{0,1:T(8,128)S(1)}, s32[128,8]{0,1:T(8,128)}, u32[]{:S(2)}) copy-start(s32[128,8]{0,1:T(8,128)} %param.9) | copy-start | bytes 12292
  3.3 49.7 %collective-permute-start.1 = (bf16[3,128,2048]{2,1,0:T(8,128)(2,1)}, bf16[3,128,2048]{2,1,0:T(8,128)(2,1)S(1)}, u32[]{:S(2)}, u32[]{:S(2)}) collective-permute-start(bf16[3,128,2048]{2,1,0:T(8,128)(2,1)} %pad_maximum_fusion.a_ref), channel_id=1, source_target_pairs={{0,16},{16,0},{1,17},{17,1},{2,18},{18,2},{3,19},{19,3},{4,20},{20... | collective-permute-start | bytes 4718600 | tf_op jit(solution)/shard_map/ppermute | solution.py:131
  42.5 9.7 %collective-permute-start = (bf16[4,2,8,2176]{3,2,0,1:T(8,128)(2,1)S(1)}, bf16[4,2,8,2176]{3,2,0,1:T(8,128)(2,1)S(1)}, u32[]{:S(2)}, u32[]{:S(2)}) collective-permute-start(bf16[4,2,8,2176]{3,2,0,1:T(8,128)(2,1)S(1)} %copy.33), channel_id=1, source_target_pairs={{0,480},{32,64},{64,32},{96,128},{128,96},{160,192},{192,160},{224... | collective-permute-start | bytes 835592 | tf_op jit(solution)/shard_map/ppermute | solution.py:137
  53.0 1.2 copy-start.4
  54.2 38.0 %collective-permute-start.2 = (bf16[3,128,2048]{2,1,0:T(8,128)(2,1)}, bf16[3,128,2048]{2,1,0:T(8,128)(2,1)}, u32[]{:S(2)}, u32[]{:S(2)}) collective-permute-start(bf16[3,128,2048]{2,1,0:T(8,128)(2,1)} %pad_maximum_fusion.a_ref), channel_id=1, source_target_pairs={{0,32},{32,0},{64,96},{96,64},{1,33},{33,1},{65,97},{97,65},{2,34}... | collective-permute-start | bytes 4718600 | tf_op jit(solution)/shard_map/ppermute | solution.py:134
  59.0 15.3 %all-to-all-start.1 = ((bf16[16,8,2176]{2,1,0:T(8,128)(2,1)}), bf16[16,8,2176]{2,1,0:T(8,128)(2,1)S(1)}, u32[]{:S(2)}, u32[]{:S(2)}) async-start(bf16[16,8,2176]{2,1,0:T(8,128)(2,1)} %bitcast.9), calls=%async_computation.1 | async-start | bytes 1114112 | tf_op jit(solution)/shard_map/all_to_all | solution.py:154
  75.5 1.4 copy-start.1
  77.0 30.8 %all-to-all-start.2 = ((bf16[16,32,2176]{2,1,0:T(8,128)(2,1)}), bf16[16,32,2176]{2,1,0:T(8,128)(2,1)S(1)}, u32[]{:S(2)}, u32[]{:S(2)}) async-start(bf16[16,32,2176]{2,1,0:T(8,128)(2,1)} %bitcast.47), calls=%async_computation.2 | async-start | bytes 4456448 | tf_op jit(solution)/shard_map/all_to_all | solution.py:162
  92.2 15.6 %collective-permute-start.3 = (bf16[3,128,2048]{2,1,0:T(8,128)(2,1)}, bf16[3,128,2048]{2,1,0:T(8,128)(2,1)}, u32[]{:S(2)}, u32[]{:S(2)}) collective-permute-start(bf16[3,128,2048]{2,1,0:T(8,128)(2,1)} %collective-permute-done.2.a_ref), channel_id=1, source_target_pairs={{0,16},{16,0},{1,17},{17,1},{2,18},{18,2},{3,19},{19,3},{4,20},{20... | collective-permute-start | bytes 4718600 | tf_op jit(solution)/shard_map/ppermute | solution.py:131
  107.8 6.5 %copy-start.5 = (bf16[3,128,2048]{2,1,0:T(8,128)(2,1)S(1)}, bf16[3,128,2048]{2,1,0:T(8,128)(2,1)}, u32[]{:S(2)}) copy-start(bf16[3,128,2048]{2,1,0:T(8,128)(2,1)} %copy-done.4) | copy-start | bytes 4718596
  112.4 11.8 %collective-permute-start.4 = (bf16[3,128,2048]{2,1,0:T(8,128)(2,1)S(1)}, bf16[3,128,2048]{2,1,0:T(8,128)(2,1)S(1)}, u32[]{:S(2)}, u32[]{:S(2)}) collective-permute-start(bf16[3,128,2048]{2,1,0:T(8,128)(2,1)S(1)} %get-tuple-element.30), channel_id=1, source_target_pairs={{0,16},{16,0},{1,17},{17,1},{2,18},{18,2},{3,19},{19,3},{4,20},{20... | collective-permute-start | bytes 4718600 | tf_op jit(solution)/shard_map/ppermute | solution.py:131
  118.9 1.1 copy-start.2
  120.1 4.2 %copy-start.6 = (bf16[3,128,2048]{2,1,0:T(8,128)(2,1)}, bf16[3,128,2048]{2,1,0:T(8,128)(2,1)S(1)}, u32[]{:S(2)}) copy-start(bf16[3,128,2048]{2,1,0:T(8,128)(2,1)S(1)} %get-tuple-element.33) | copy-start | bytes 4718596
  126.1 24.6 %all-to-all-start.3 = ((bf16[16,32,1152]{2,1,0:T(8,128)(2,1)}), bf16[16,32,1152]{2,1,0:T(8,128)(2,1)S(1)}, u32[]{:S(2)}, u32[]{:S(2)}) async-start(bf16[16,32,1152]{2,1,0:T(8,128)(2,1)} %bitcast.14), calls=%async_computation.3 | async-start | bytes 2359296 | tf_op jit(solution)/shard_map/all_to_all | solution.py:189
  133.6 38.7 %copy-start.3 = (bf16[3,128,2048]{2,1,0:T(8,128)(2,1)S(1)}, bf16[3,128,2048]{2,1,0:T(8,128)(2,1)}, u32[]{:S(2)}) copy-start(bf16[3,128,2048]{2,1,0:T(8,128)(2,1)} %copy-done.2) | copy-start | bytes 4718596
  133.6 38.7 %collective-permute-start.6 = (bf16[3,128,2048]{2,1,0:T(8,128)(2,1)}, bf16[3,128,2048]{2,1,0:T(8,128)(2,1)}, u32[]{:S(2)}, u32[]{:S(2)}) collective-permute-start(bf16[3,128,2048]{2,1,0:T(8,128)(2,1)} %copy-done.6), channel_id=1, source_target_pairs={{0,16},{16,0},{1,17},{17,1},{2,18},{18,2},{3,19},{19,3},{4,20},{20... | collective-permute-start | bytes 4718600 | tf_op jit(solution)/shard_map/ppermute | solution.py:131
  151.7 16.1 %all-to-all-start.4 = ((bf16[16,8,1152]{2,1,0:T(8,128)(2,1)}), bf16[16,8,1152]{2,1,0:T(8,128)(2,1)}, u32[]{:S(2)}, u32[]{:S(2)}) async-start(bf16[16,8,1152]{2,1,0:T(8,128)(2,1)} %bitcast.16), calls=%async_computation.4 | async-start | bytes 589824 | tf_op jit(solution)/shard_map/all_to_all | solution.py:191
  160.9 41.0 %collective-permute-start.7 = (bf16[3,128,2048]{2,1,0:T(8,128)(2,1)}, bf16[3,128,2048]{2,1,0:T(8,128)(2,1)S(1)}, u32[]{:S(2)}, u32[]{:S(2)}) collective-permute-start(bf16[3,128,2048]{2,1,0:T(8,128)(2,1)} %add_convert_fusion), channel_id=1, source_target_pairs={{0,32},{32,0},{64,96},{96,64},{1,33},{33,1},{65,97},{97,65},{2,34}... | collective-permute-start | bytes 4718600 | tf_op jit(solution)/shard_map/ppermute | solution.py:134
  168.7 8.2 %collective-permute-start.5 = (bf16[4,2,8,1152]{3,2,0,1:T(8,128)(2,1)S(1)}, bf16[4,2,8,1152]{3,2,0,1:T(8,128)(2,1)S(1)}, u32[]{:S(2)}, u32[]{:S(2)}) collective-permute-start(bf16[4,2,8,1152]{3,2,0,1:T(8,128)(2,1)S(1)} %slice_bitcast_fusion), channel_id=1, source_target_pairs={{0,480},{32,64},{64,32},{96,128},{128,96},{160,192},{192,160},{224... | collective-permute-start | bytes 442376 | tf_op jit(solution)/shard_map/ppermute | solution.py:137
  178.6 27.0 %all-to-all-start.5 = ((bf16[4,2,8,1152]{3,2,1,0:T(8,128)(2,1)}), bf16[4,2,8,1152]{3,2,1,0:T(8,128)(2,1)S(1)}, u32[]{:S(2)}, u32[]{:S(2)}) async-start(bf16[4,2,8,1152]{3,2,1,0:T(8,128)(2,1)} %copy.29), calls=%async_computation.5 | async-start | bytes 294912 | tf_op jit(solution)/shard_map/all_to_all | solution.py:194

commit v5 on v4

v5 whole, which is shorter than its diff:
```python
import functools

import jax
import jax.numpy as jnp
from jax import lax
from jax.experimental import pallas as pl
from jax.experimental.pallas import tpu as pltpu
from jax.sharding import Mesh, PartitionSpec as P

BF = jnp.bfloat16
F32 = jnp.float32
EL = 4
CAP = 32
LANES = 128
INNER = ((1,), (1,))
PLAIN = ((1,), (0,))
AXES = ("zh", "zq", "core", "expert")
VMEM_BYTES = 28 << 20


def dot(a, b, dims):
    return lax.dot_general(a, b, (dims, ((), ())), preferred_element_type=F32)


def mirror(sizes):
    nh, nq, nc, ne = sizes
    pairs = []
    for u in range(nh):
        for q in range(nq):
            for c in range(nc):
                for e in range(ne):
                    v = (e + 4 * c + q - u) % nh
                    pairs.append((((u * nq + q) * nc + c) * ne + e, ((v * nq + q) * nc + c) * ne + e))
    return pairs


def call(body, args, outs, flops, to_hbm=(), scratch=(), from_hbm=()):
    vmem = pl.BlockSpec(memory_space=pltpu.VMEM)
    smem = pl.BlockSpec(memory_space=pltpu.SMEM)
    hbm = pl.BlockSpec(memory_space=pltpu.HBM)
    moved = sum(a.size * a.dtype.itemsize for a in list(args) + list(outs))
    return pl.pallas_call(
        body,
        out_shape=[pltpu.HBM(o.shape, o.dtype) if i in to_hbm else o for i, o in enumerate(outs)],
        in_specs=[hbm if i in from_hbm else smem if a.ndim == 1 else vmem for i, a in enumerate(args)],
        out_specs=[hbm if i in to_hbm else vmem for i in range(len(outs))],
        scratch_shapes=list(scratch),
        compiler_params=pltpu.CompilerParams(vmem_limit_bytes=VMEM_BYTES),
        cost_estimate=pl.CostEstimate(flops=flops, bytes_accessed=moved, transcendentals=0),
    )(*args)


def pack_body(side_ref, tokens_ref, cotangent_ref, ids_ref, gates_ref, packed_ref, sem):
    rows, width = tokens_ref.shape
    top = ids_ref.shape[0]
    for side, source in enumerate((tokens_ref, cotangent_ref)):

        @pl.when(side_ref[0] == side)
        def _():
            pltpu.make_async_copy(source, packed_ref.at[:, pl.ds(0, width)], sem.at[0]).start()

    meta = [ids_ref[...].astype(F32), gates_ref[...].astype(F32), jnp.zeros((LANES - 2 * top, rows), F32)]
    packed_ref[:, width:] = jnp.concatenate(meta, axis=0).T.astype(BF)
    pltpu.make_async_copy(tokens_ref, packed_ref.at[:, pl.ds(0, width)], sem.at[0]).wait()


def select_body(top, width, block_ref, whole_ref, chosen_ref, pick_ref, held, sem):
    rows, slots = pick_ref.shape
    meta = whole_ref[:, width : width + LANES].astype(F32)
    slot = lax.broadcasted_iota(jnp.int32, (1, slots), 1)
    wanted = (slot // CAP * EL + block_ref[0]).astype(F32)
    named = meta[:, 0:1] == wanted
    for k in range(1, top):
        named = named | (meta[:, k : k + 1] == wanted)
    earlier = lax.broadcasted_iota(jnp.int32, (rows, rows), 0) > lax.broadcasted_iota(jnp.int32, (rows, rows), 1)
    rank = dot(earlier.astype(F32).astype(BF), named.astype(F32).astype(BF), PLAIN)
    pick = jnp.where(named & (rank == (slot % CAP).astype(F32)), 1.0, 0.0)
    pick_ref[...] = pick.astype(BF)
    pick = pick.T.astype(BF)
    copies = []
    for at in range(0, slots, slots // 2):
        rows = pl.ds(at, slots // 2)
        held[rows, :] = dot(pick[at : at + slots // 2], whole_ref[...], PLAIN).astype(BF)
        copies.append(pltpu.make_async_copy(held.at[rows], chosen_ref.at[rows], sem.at[len(copies)]))
        copies[-1].start()
    for copy in copies:
        copy.wait()


def both(a_ref, b_ref, i):
    return jnp.concatenate([a_ref[i], b_ref[i]], axis=0)


def hidden_grads(top, expert_ref, rows_ref, a_ref, b_ref, mine_ref, theirs_ref, mine, theirs, sem):
    _, fq, width = a_ref.shape
    count = rows_ref.shape[0] // 2
    x = rows_ref[:count, :width]
    dy = rows_ref[count:, :width]
    meta = rows_ref[:count, width : width + LANES].astype(F32)
    expert = expert_ref[0].astype(F32)
    g = jnp.sum(jnp.where(meta[:, :top] == expert, meta[:, top : 2 * top], 0.0), axis=1, keepdims=True)
    lane = lax.broadcasted_iota(jnp.int32, (count, LANES), 1)
    mark = jnp.where((meta == expert) & (lane < top), 1.0, 0.0)
    pre_gate = dot(x, both(a_ref, b_ref, 0), INNER)
    pre_up = dot(x, both(a_ref, b_ref, 1), INNER)
    back = dot(dy, both(a_ref, b_ref, 2), INNER)
    sigma = jax.nn.sigmoid(pre_gate)
    active = pre_gate * sigma
    hidden = (active * pre_up).astype(BF).astype(F32)
    lanes = jnp.sum(hidden * back, axis=1, keepdims=True) * mark
    d_hidden = g * back
    d_pre_gate = d_hidden * pre_up * sigma * (1.0 + pre_gate * (1.0 - sigma))
    d_pre_up = d_hidden * active
    scaled = g * hidden
    copies = []
    for i, (left, right) in enumerate(((d_pre_gate, x), (d_pre_up, x), (scaled, dy))):
        grad = dot(left.T.astype(BF), right, PLAIN).astype(BF)
        mine[i] = grad[:fq]
        theirs[i] = grad[fq:]
        copies.append(pltpu.make_async_copy(theirs.at[i], theirs_ref.at[i], sem.at[2 * i]))
        copies.append(pltpu.make_async_copy(mine.at[i], mine_ref.at[i], sem.at[2 * i + 1]))
        copies[-2].start()
        copies[-1].start()
    return d_pre_gate.astype(BF), d_pre_up.astype(BF), lanes, copies


def near_body(top, expert_ref, rows_ref, a_ref, b_ref, sum_ref, *refs):
    width = a_ref.shape[2]
    d_gate, d_up, lanes, copies = hidden_grads(top, expert_ref, rows_ref, a_ref, b_ref, *refs)
    sum_ref[:, :width] = dot(d_gate, both(a_ref, b_ref, 0), PLAIN) + dot(d_up, both(a_ref, b_ref, 1), PLAIN)
    sum_ref[:, width:] = lanes
    for copy in copies:
        copy.wait()


def far_body(top, expert_ref, rows_ref, a_ref, b_ref, sum_ref, reply_ref, *refs):
    width = a_ref.shape[2]
    half = width // 2
    reply, reply_sem = refs[-2:]
    d_gate, d_up, lanes, copies = hidden_grads(top, expert_ref, rows_ref, a_ref, b_ref, *refs[:-2])
    lanes = (lanes + sum_ref[:, width:]).astype(BF)
    for h in range(2):
        at = pl.ds(h * half, half)
        wg = jnp.concatenate([a_ref[0, :, at], b_ref[0, :, at]], axis=0)
        wu = jnp.concatenate([a_ref[1, :, at], b_ref[1, :, at]], axis=0)
        reply[h, :, :half] = (dot(d_gate, wg, PLAIN) + dot(d_up, wu, PLAIN) + sum_ref[:, at]).astype(BF)
        reply[h, :, half:] = lanes
        copies.append(pltpu.make_async_copy(reply.at[h], reply_ref.at[h], reply_sem.at[h]))
        copies[-1].start()
    for copy in copies:
        copy.wait()


def combine_body(pick_ref, home_ref, terms_ref):
    terms_ref[...] = dot(pick_ref[...], home_ref[...], PLAIN).astype(BF)


def finish_body(terms_ref, tokens_ref, gates_ref):
    half = tokens_ref.shape[1] // 2
    for h in range(2):
        total = jnp.sum(terms_ref[:, h].astype(F32), axis=0)
        tokens_ref[:, h * half : (h + 1) * half] = total[:, :half].astype(BF)
        if h == 0:
            gates_ref[...] = total[:, half : half + gates_ref.shape[1]]


def shards(tokens, cotangent, expert_ids, gates, w_gate, w_up, w_down):
    rows, width = tokens.shape
    top = expert_ids.shape[1]
    fq = w_gate.shape[2]
    sizes = tuple(lax.axis_size(a) for a in AXES)
    nh, _, _, cols = sizes
    up, odd, core, col = (lax.axis_index(a) for a in AXES)
    block = up // (nh // EL)
    half = width // 2
    part = rows // cols
    slots = cols * CAP
    wide = width + LANES
    thin = half + LANES
    shape = jax.ShapeDtypeStruct

    def core_swap(v):
        return lax.ppermute(v, "core", [(0, 1), (1, 0)])

    def chip_swap(v):
        return lax.ppermute(v, "zq", [(0, 1), (1, 0)])

    side = (col // (cols // 2)).astype(jnp.int32)[None]
    (packed,) = call(
        pack_body,
        (side, *(pltpu.with_memory_space_constraint(v, pltpu.HBM) for v in (tokens, cotangent)), expert_ids.T, gates.T),
        (shape((rows, wide), BF),),
        0,
        scratch=(pltpu.SemaphoreType.DMA((1,)),),
        from_hbm=(1, 2),
    )
    whole = lax.ppermute(packed, AXES, mirror(sizes))

    own = jnp.stack([w_gate[0, 0], w_up[0, 0], w_down[0, 0]])
    own, whole = lax.optimization_barrier((own, whole))
    far = chip_swap(own)
    far_c = core_swap(far)

    chosen, pick = call(
        functools.partial(select_body, top, width),
        (block.astype(jnp.int32)[None], whole),
        (shape((slots, wide), BF), shape((rows, slots), BF)),
        2 * slots * rows * wide,
        (0,),
        (pltpu.VMEM((slots, wide), BF), pltpu.SemaphoreType.DMA((2,))),
    )
    own_late, chosen = lax.optimization_barrier((own, chosen))
    own_c = core_swap(own_late)
    got = lax.all_to_all(chosen.reshape(cols, CAP, wide), "expert", 0, 0, tiled=True).reshape(slots, wide)

    expert = (col * EL + block).astype(jnp.int32)[None]
    count = slots // 2
    work = 16 * count * width * 2 * fq
    weight_shape = shape((3, fq, width), BF)
    grad_scratch = (*[pltpu.VMEM((3, fq, width), BF)] * 2, pltpu.SemaphoreType.DMA((6,)))
    partial, near_mine, near_theirs = call(
        functools.partial(near_body, top),
        (expert, got, own, own_c),
        (shape((count, wide), F32), weight_shape, weight_shape),
        work,
        (1, 2),
        grad_scratch,
    )
    reply, far_mine, far_theirs = call(
        functools.partial(far_body, top),
        (expert, got, far, far_c, partial),
        (shape((2, count, thin), BF), weight_shape, weight_shape),
        work,
        (0, 1, 2),
        (*grad_scratch, pltpu.VMEM((2, count, thin), BF), pltpu.SemaphoreType.DMA((2,))),
    )
    far_other = core_swap(far_theirs)
    far_in = [chip_swap((far_mine[i].astype(F32) + far_other[i].astype(F32)).astype(BF)) for i in range(3)]

    home = lax.all_to_all(reply.reshape(cols, CAP, thin), "expert", 0, 0, tiled=True)
    home, far_in[2] = lax.optimization_barrier((home, far_in[2]))
    (terms,) = call(combine_body, (pick, home.reshape(slots, thin)), (shape((rows, thin), BF),), 2 * slots * rows * thin)
    spread = lax.all_to_all(terms.reshape(cols, part, thin), "expert", 0, 0, tiled=True)
    spread, far_in[0] = lax.optimization_barrier((spread, far_in[0]))
    spread = spread.reshape(2, nh, part, thin).transpose(1, 0, 2, 3)
    twice = jnp.concatenate([spread, spread])
    ordered = lax.dynamic_slice_in_dim(twice, (up - 4 * core - odd) % nh, nh, axis=0)
    planes = lax.all_to_all(ordered, "zh", 0, 0, tiled=True)
    d_tokens, d_gates = call(finish_body, (planes,), (shape((part, width), BF), shape((part, top), F32)), 0)

    near_sum = near_mine.astype(F32) + core_swap(near_theirs).astype(F32)
    grads = [(near_sum[i] + far_in[i].astype(F32)).astype(BF)[None, None] for i in range(3)]
    return (d_tokens, d_gates, *grads)


def solution(mesh):
    devices = mesh.devices
    inner = Mesh(devices.reshape(devices.shape[0] // 4, 2, 2, devices.shape[1]), AXES)
    dp = AXES[:3]
    tok = P(dp, None)
    wt = P("expert", dp, None, None)
    out = P(AXES, None)
    return jax.shard_map(
        shards,
        mesh=inner,
        in_specs=(tok, tok, tok, tok, wt, wt, wt),
        out_specs=(out, out, wt, wt, wt),
        check_vma=False,
    )
```

time: 208 us -> 184 us (0.88)
  blocking collectives: 35.8 us -> 0 us
  starting transfers between devices: 59.1 us -> 78.4 us
  other arithmetic: 13.9 us -> 8.67 us
  local copies, waits for them, and re-layouts: 7.26 us -> 2.63 us
    all_to_all x1 -> x0, blocking collectives: 35.8 us -> none  [shards(): lax.all_to_all(jnp.broadcast_to(packed, (nb, 2, part, wide)), 'zb', 0, 0,...]
    ppermute x4 -> x5, starting transfers between devices: 15 us -> 32.5 us  [the longest x4 20.7 us: chip_swap(): return lax.ppermute(v, 'zq', [(0, 1), (1, 0)])]
    ppermute x4 -> x5, waiting for transfers between devices: 33.3 us -> 45.6 us  [the longest x1 24.1 us: shards(): whole = lax.ppermute(packed, AXES, mirror(sizes))]
    all_to_all x1, waiting for transfers between devices: 13.7 us -> 2.86 us  [shards(): lax.all_to_all(chosen.reshape(cols, CAP, wide), 'expert', 0, 0, tiled=True)]
    all_to_all x1, waiting for transfers between devices: 14.7 us -> 5.7 us  [shards(): lax.all_to_all(reply.reshape(cols, CAP, thin), 'expert', 0, 0, tiled=True)]
    all_to_all x2 -> x1, waiting for transfers between devices: 8.31 us -> 16.8 us  [shards(): planes = lax.all_to_all(ordered, 'zh', 0, 0, tiled=True)]
    add x1, other arithmetic: 3.65 us -> 0.58 us  [shards(): near_sum = near_mine.astype(F32) + core_swap(near_theirs).astype(F32)]
    convert_element_type x4 -> x1, other arithmetic: 6.07 us -> 3.31 us  [shards(): (far_mine[i].astype(F32) + far_other[i].astype(F32)).astype(BF)]
  transfers between devices with their start and end apart: 13 -> 13, of which waited for: 9 -> 7; matrix products, arithmetic and copies ran while one was open for 6% -> 5% of each run, Pallas kernels for 5% -> 5%
where the time goes in v5:
time: 184 us; the launch traced here: 182 us
  starting transfers between devices  78.4 us (43%)
  waiting for transfers between devices  74.8 us (41%)
  Pallas kernels  17 us (9%)
  other arithmetic  8.67 us (5%)
  local copies, waits for them, and re-layouts  2.63 us (1%)
    ppermute x1, waiting for transfers between devices, shards(): whole = lax.ppermute(packed, AXES, mirror(sizes))  24.1 us
    ppermute x4, waiting for transfers between devices, chip_swap(): return lax.ppermute(v, 'zq', [(0, 1), (1, 0)])  21.5 us
    ppermute x4, starting transfers between devices, chip_swap(): return lax.ppermute(v, 'zq', [(0, 1), (1, 0)])  20.7 us
    pallas_call x6, Pallas kernels, call(): pl.pallas_call(body, out_shape=[pltpu.HBM(o.shape, o.dtype) if i in to_hb...  17 us
    all_to_all x1, waiting for transfers between devices, shards(): planes = lax.all_to_all(ordered, 'zh', 0, 0, tiled=True)  16.8 us
    all_to_all x1, starting transfers between devices, shards(): planes = lax.all_to_all(ordered, 'zh', 0, 0, tiled=True)  14.6 us
    ppermute x1, starting transfers between devices, shards(): whole = lax.ppermute(packed, AXES, mirror(sizes))  11.8 us
    all_to_all x1, starting transfers between devices, shards(): lax.all_to_all(reply.reshape(cols, CAP, thin), 'expert', 0, 0, tiled=True)  8.81 us
  transfers between devices with their start and end apart: 13, of which 7 were waited for; matrix products, arithmetic and copies ran while one was open for 5% of the time, Pallas kernels for 5%

profile of v5, /device:TPU:6, one launch (start us, length us, event | category | flops | bytes accessed | tf_op | source)
XLA Modules:
  0.0 182.3 jit_solution(2929037469706728593)
XLA Ops:
  0.7 0.0 copy-start
  0.7 0.7 copy-done
  1.3 0.0 copy-start.1
  1.3 0.7 copy-done.1
  2.0 1.2 shard_map.110
  3.2 11.8 %collective-permute-start = (bf16[128,2176]{1,0:T(8,128)(2,1)S(1)}, bf16[128,2176]{1,0:T(8,128)(2,1)S(1)}, u32[]{:S(2)}, u32[]{:S(2)}) collective-permute-start(bf16[128,2176]{1,0:T(8,128)(2,1)S(1)} %shard_map.110), channel_id=1, source_target_pairs={{0,0},{1,65},{2,130},{3,195},{4,260},{5,325},{6,390},{7,455},{8,8}... | collective-permute-start | bytes 1671176 | tf_op jit(solution)/shard_map/ppermute | solution.py:197
  15.0 0.0 copy-done.5
  15.0 0.0 copy-done.6
  15.0 0.0 copy-done.7
  15.0 1.3 pad_maximum_fusion.a_ref
  16.4 24.1 %collective-permute-done.whole_ref = bf16[128,2176]{1,0:T(8,128)(2,1)S(1)} collective-permute-done((bf16[128,2176]{1,0:T(8,128)(2,1)S(1)}, bf16[128,2176]{1,0:T(8,128)(2,1)S(1)}, u32[]{:S(2)}, u32[]{:S(2)}) %collective-permute-start) | collective-permute-done | bytes 557088 | tf_op jit(solution)/shard_map/ppermute | solution.py:197
  40.5 12.3 %collective-permute-start.1 = (bf16[3,128,2048]{2,1,0:T(8,128)(2,1)}, bf16[3,128,2048]{2,1,0:T(8,128)(2,1)}, u32[]{:S(2)}, u32[]{:S(2)}) collective-permute-start(bf16[3,128,2048]{2,1,0:T(8,128)(2,1)} %pad_maximum_fusion.a_ref), channel_id=1, source_target_pairs={{0,32},{32,0},{1,33},{33,1},{2,34},{34,2},{3,35},{35,3},{4,36},{36... | collective-permute-start | bytes 4718600 | tf_op jit(solution)/shard_map/ppermute | solution.py:186
  52.8 2.4 %shard_map.111 = (bf16[512,2176]{1,0:T(8,128)(2,1)}, bf16[128,512]{1,0:T(8,128)(2,1)S(1)}) custom-call(s32[1]{0:T(128)} %bitcast.block_ref, bf16[128,2176]{1,0:T(8,128)(2,1)S(1)} %collective-permute-done.whole_ref), custom_call_target="tpu_custom_call" | custom-call | flops 285212672 | bytes 2916356 | tf_op jit(solution)/shard_map/pallas_call | solution.py:42
  55.2 7.2 %all-to-all-start = ((bf16[16,32,2176]{2,1,0:T(8,128)(2,1)}), bf16[16,32,2176]{2,1,0:T(8,128)(2,1)S(1)}, u32[]{:S(2)}, u32[]{:S(2)}) async-start(bf16[16,32,2176]{2,1,0:T(8,128)(2,1)} %bitcast.58), calls=%async_computation | async-start | bytes 4456448 | tf_op jit(solution)/shard_map/all_to_all | solution.py:214
  62.4 1.9 %collective-permute-start.3 = (bf16[3,128,2048]{2,1,0:T(8,128)(2,1)}, bf16[3,128,2048]{2,1,0:T(8,128)(2,1)}, u32[]{:S(2)}, u32[]{:S(2)}) collective-permute-start(bf16[3,128,2048]{2,1,0:T(8,128)(2,1)} %pad_maximum_fusion.a_ref), channel_id=1, source_target_pairs={{0,16},{16,0},{1,17},{17,1},{2,18},{18,2},{3,19},{19,3},{4,20},{20... | collective-permute-start | bytes 4718600 | tf_op jit(solution)/shard_map/ppermute | solution.py:183
  64.3 16.2 %collective-permute-done.1.a_ref = bf16[3,128,2048]{2,1,0:T(8,128)(2,1)} collective-permute-done((bf16[3,128,2048]{2,1,0:T(8,128)(2,1)}, bf16[3,128,2048]{2,1,0:T(8,128)(2,1)}, u32[]{:S(2)}, u32[]{:S(2)}) %collective-permute-start.1) | collective-permute-done | bytes 1572896 | tf_op jit(solution)/shard_map/ppermute | solution.py:186
  80.5 1.9 %collective-permute-start.2 = (bf16[3,128,2048]{2,1,0:T(8,128)(2,1)}, bf16[3,128,2048]{2,1,0:T(8,128)(2,1)}, u32[]{:S(2)}, u32[]{:S(2)}) collective-permute-start(bf16[3,128,2048]{2,1,0:T(8,128)(2,1)} %collective-permute-done.1.a_ref), channel_id=1, source_target_pairs={{0,16},{16,0},{1,17},{17,1},{2,18},{18,2},{3,19},{19,3},{4,20},{20... | collective-permute-start | bytes 4718600 | tf_op jit(solution)/shard_map/ppermute | solution.py:183
  82.4 0.0 collective-permute-done.3.b_ref
  82.4 2.9 %all-to-all-done = bf16[16,32,2176]{2,1,0:T(8,128)(2,1)S(1)} async-done(((bf16[16,32,2176]{2,1,0:T(8,128)(2,1)}), bf16[16,32,2176]{2,1,0:T(8,128)(2,1)S(1)}, u32[]{:S(2)}, u32[]{:S(2)}) %all-to-all-start) | async-done | bytes 2228256 | tf_op jit(solution)/shard_map/all_to_all | solution.py:214
  85.3 5.6 %shard_map.112 = (f32[256,2176]{1,0:T(8,128)S(1)}, bf16[3,128,2048]{2,1,0:T(8,128)(2,1)}, bf16[3,128,2048]{2,1,0:T(8,128)(2,1)}) custom-call(s32[1]{0:T(128)} %bitcast.7.expert_ref, bf16[512,2176]{1,0:T(8,128)(2,1)S(1)} %bitcast.54, bf16[3,128,2048]{2,1,0:T(8,128)(2,1)} %pad_maximum_fusion.a_ref, bf16[3,128,2048]{2,1,0:T(8,128)(2,1)} %collective-permute-done.3.b_ref), custom_call_target="tpu_custom_call" | custom-call | flops 2147483648 | bytes 10747908 | tf_op jit(solution)/shard_map/pallas_call | solution.py:42
  90.9 0.0 collective-permute-done.2.b_ref
  90.9 6.1 %shard_map.113 = (bf16[2,256,1152]{2,1,0:T(8,128)(2,1)}, bf16[3,128,2048]{2,1,0:T(8,128)(2,1)}, bf16[3,128,2048]{2,1,0:T(8,128)(2,1)}) custom-call(s32[1]{0:T(128)} %bitcast.7.expert_ref, bf16[512,2176]{1,0:T(8,128)(2,1)S(1)} %bitcast.55, bf16[3,128,2048]{2,1,0:T(8,128)(2,1)} %collective-permute-done.1.a_ref, ...), custom_call_target="tpu_custom_call" | custom-call | flops 2147483648 | bytes 11927556 | tf_op jit(solution)/shard_map/pallas_call | solution.py:42
  97.0 1.9 %collective-permute-start.4 = (bf16[3,128,2048]{2,1,0:T(8,128)(2,1)}, bf16[3,128,2048]{2,1,0:T(8,128)(2,1)}, u32[]{:S(2)}, u32[]{:S(2)}) collective-permute-start(bf16[3,128,2048]{2,1,0:T(8,128)(2,1)} %get-tuple-element.32), channel_id=1, source_target_pairs={{0,16},{16,0},{1,17},{17,1},{2,18},{18,2},{3,19},{19,3},{4,20},{20... | collective-permute-start | bytes 4718600 | tf_op jit(solution)/shard_map/ppermute | solution.py:183
  98.9 8.8 %all-to-all-start.1 = ((bf16[16,32,1152]{2,1,0:T(8,128)(2,1)}), bf16[16,32,1152]{2,1,0:T(8,128)(2,1)S(1)}, u32[]{:S(2)}, u32[]{:S(2)}) async-start(bf16[16,32,1152]{2,1,0:T(8,128)(2,1)} %bitcast.59), calls=%async_computation.1 | async-start | bytes 2359296 | tf_op jit(solution)/shard_map/all_to_all | solution.py:240
  107.7 2.1 %collective-permute-start.7 = (bf16[3,128,2048]{2,1,0:T(8,128)(2,1)}, bf16[3,128,2048]{2,1,0:T(8,128)(2,1)S(1)}, u32[]{:S(2)}, u32[]{:S(2)}) collective-permute-start(bf16[3,128,2048]{2,1,0:T(8,128)(2,1)} %get-tuple-element.38), channel_id=1, source_target_pairs={{0,16},{16,0},{1,17},{17,1},{2,18},{18,2},{3,19},{19,3},{4,20},{20... | collective-permute-start | bytes 4718600 | tf_op jit(solution)/shard_map/ppermute | solution.py:183
  109.9 0.0 collective-permute-done.4
  109.9 3.3 %fusion.8 = (bf16[128,2048]{1,0:T(8,128)(2,1)}, bf16[128,2048]{1,0:T(8,128)(2,1)}, bf16[128,2048]{1,0:T(8,128)(2,1)}) fusion(bf16[3,128,2048]{2,1,0:T(8,128)(2,1)} %collective-permute-done.4, bf16[3,128,2048]{2,1,0:T(8,128)(2,1)} %get-tuple-element.31), kind=kLoop, calls=%fused_computation.18 | loop fusion | flops 3145728 | bytes 4718592 | tf_op jit(solution)/shard_map/convert_element_type | solution.py:238
  113.2 2.6 %collective-permute-start.5 = (bf16[128,2048]{1,0:T(8,128)(2,1)}, bf16[128,2048]{1,0:T(8,128)(2,1)S(1)}, u32[]{:S(2)}, u32[]{:S(2)}) collective-permute-start(bf16[128,2048]{1,0:T(8,128)(2,1)} %get-tuple-element.46), channel_id=1, source_target_pairs={{0,32},{32,0},{1,33},{33,1},{2,34},{34,2},{3,35},{35,3},{4,36},{36... | collective-permute-start | bytes 1572872 | tf_op jit(solution)/shard_map/ppermute | solution.py:186
  115.8 3.3 %collective-permute-start.6 = (bf16[128,2048]{1,0:T(8,128)(2,1)}, bf16[128,2048]{1,0:T(8,128)(2,1)}, u32[]{:S(2)}, u32[]{:S(2)}) collective-permute-start(bf16[128,2048]{1,0:T(8,128)(2,1)} %get-tuple-element.45), channel_id=1, source_target_pairs={{0,32},{32,0},{1,33},{33,1},{2,34},{34,2},{3,35},{35,3},{4,36},{36... | collective-permute-start | bytes 1572872 | tf_op jit(solution)/shard_map/ppermute | solution.py:186
  119.0 5.7 %all-to-all-done.1 = bf16[16,32,1152]{2,1,0:T(8,128)(2,1)S(1)} async-done(((bf16[16,32,1152]{2,1,0:T(8,128)(2,1)}), bf16[16,32,1152]{2,1,0:T(8,128)(2,1)S(1)}, u32[]{:S(2)}, u32[]{:S(2)}) %all-to-all-start.1) | async-done | bytes 1179680 | tf_op jit(solution)/shard_map/all_to_all | solution.py:240
  124.7 5.3 %collective-permute-done.5 = bf16[128,2048]{1,0:T(8,128)(2,1)S(1)} collective-permute-done((bf16[128,2048]{1,0:T(8,128)(2,1)}, bf16[128,2048]{1,0:T(8,128)(2,1)S(1)}, u32[]{:S(2)}, u32[]{:S(2)}) %collective-permute-start.5) | collective-permute-done | bytes 524320 | tf_op jit(solution)/shard_map/ppermute | solution.py:186
  130.0 0.8 copy-done.3
  130.8 1.1 shard_map.114
  131.9 7.4 %all-to-all-start.2 = ((bf16[16,8,1152]{2,1,0:T(8,128)(2,1)}), bf16[16,8,1152]{2,1,0:T(8,128)(2,1)S(1)}, u32[]{:S(2)}, u32[]{:S(2)}) async-start(bf16[16,8,1152]{2,1,0:T(8,128)(2,1)} %bitcast.13), calls=%async_computation.2 | async-start | bytes 589824 | tf_op jit(solution)/shard_map/all_to_all | solution.py:243
  139.3 2.6 %collective-permute-start.8 = (bf16[128,2048]{1,0:T(8,128)(2,1)}, bf16[128,2048]{1,0:T(8,128)(2,1)}, u32[]{:S(2)}, u32[]{:S(2)}) collective-permute-start(bf16[128,2048]{1,0:T(8,128)(2,1)} %get-tuple-element.44), channel_id=1, source_target_pairs={{0,32},{32,0},{1,33},{33,1},{2,34},{34,2},{3,35},{35,3},{4,36},{36... | collective-permute-start | bytes 1572872 | tf_op jit(solution)/shard_map/ppermute | solution.py:186
  141.9 0.0 collective-permute-done.6
  141.9 3.8 %all-to-all-done.2 = bf16[16,8,1152]{2,1,0:T(8,128)(2,1)S(1)} async-done(((bf16[16,8,1152]{2,1,0:T(8,128)(2,1)}), bf16[16,8,1152]{2,1,0:T(8,128)(2,1)S(1)}, u32[]{:S(2)}, u32[]{:S(2)}) %all-to-all-start.2) | async-done | bytes 294944 | tf_op jit(solution)/shard_map/all_to_all | solution.py:243
  145.7 0.9 fusion.12
  146.6 14.6 %all-to-all-start.3 = ((bf16[8,2,8,1152]{3,2,1,0:T(8,128)(2,1)}), bf16[8,2,8,1152]{3,2,1,0:T(8,128)(2,1)S(1)}, u32[]{:S(2)}, u32[]{:S(2)}) async-start(bf16[8,2,8,1152]{3,2,1,0:T(8,128)(2,1)} %fusion.12), calls=%async_computation.3 | async-start | bytes 589824 | tf_op jit(solution)/shard_map/all_to_all | solution.py:248
  161.2 0.0 collective-permute-done.7
  161.2 0.0 copy-done.2
  161.2 0.0 copy-start.4
  161.2 0.6 convert_add_fusion
  161.8 0.0 collective-permute-done.8
  161.8 0.4 copy-done.4
  162.3 2.6 %fusion.11 = (bf16[1,1,128,2048]{3,2,1,0:T(8,128)(2,1)}, bf16[1,1,128,2048]{3,2,1,0:T(8,128)(2,1)}, bf16[1,1,128,2048]{3,2,1,0:T(8,128)(2,1)}) fusion(bf16[128,2048]{1,0:T(8,128)(2,1)S(1)} %copy-done.4, f32[3,128,2048]{2,1,0:T(8,128)S(1)} %convert_add_fusion, bf16[128,2048]{1,0:T(8,128)(2,1)} %collective-permute-done.8, ...), kind=kLoop, calls=%fused_computation.21 | loop fusion | flops 2359296 | bytes 6291456 | tf_op jit(solution)/shard_map/broadcast_in_dim | solution.py:252
  164.9 16.8 %all-to-all-done.3.terms_ref = bf16[8,2,8,1152]{3,2,1,0:T(8,128)(2,1)S(1)} async-done(((bf16[8,2,8,1152]{3,2,1,0:T(8,128)(2,1)}), bf16[8,2,8,1152]{3,2,1,0:T(8,128)(2,1)S(1)}, u32[]{:S(2)}, u32[]{:S(2)}) %all-to-all-start.3) | async-done | bytes 294944 | tf_op jit(solution)/shard_map/all_to_all | solution.py:248
  181.6 0.7 shard_map.115
  (6 shorter events, 0.0 us)
Async XLA Ops:
  0.7 0.7 copy-start
  1.3 0.7 copy-start.1
  2.0 13.0 %copy-start.5 = (bf16[1,1,128,2048]{3,2,1,0:T(8,128)(2,1)S(1)}, bf16[1,1,128,2048]{3,2,1,0:T(8,128)(2,1)}, u32[]{:S(2)}) copy-start(bf16[1,1,128,2048]{3,2,1,0:T(8,128)(2,1)} %param.13) | copy-start | bytes 1572868
  2.0 13.0 %copy-start.6 = (bf16[1,1,128,2048]{3,2,1,0:T(8,128)(2,1)S(1)}, bf16[1,1,128,2048]{3,2,1,0:T(8,128)(2,1)}, u32[]{:S(2)}) copy-start(bf16[1,1,128,2048]{3,2,1,0:T(8,128)(2,1)} %param.12) | copy-start | bytes 1572868
  2.0 13.0 %copy-start.7 = (bf16[1,1,128,2048]{3,2,1,0:T(8,128)(2,1)S(1)}, bf16[1,1,128,2048]{3,2,1,0:T(8,128)(2,1)}, u32[]{:S(2)}) copy-start(bf16[1,1,128,2048]{3,2,1,0:T(8,128)(2,1)} %param.11) | copy-start | bytes 1572868
  3.2 37.3 %collective-permute-start = (bf16[128,2176]{1,0:T(8,128)(2,1)S(1)}, bf16[128,2176]{1,0:T(8,128)(2,1)S(1)}, u32[]{:S(2)}, u32[]{:S(2)}) collective-permute-start(bf16[128,2176]{1,0:T(8,128)(2,1)S(1)} %shard_map.110), channel_id=1, source_target_pairs={{0,0},{1,65},{2,130},{3,195},{4,260},{5,325},{6,390},{7,455},{8,8}... | collective-permute-start | bytes 1671176 | tf_op jit(solution)/shard_map/ppermute | solution.py:197
  40.5 40.0 %collective-permute-start.1 = (bf16[3,128,2048]{2,1,0:T(8,128)(2,1)}, bf16[3,128,2048]{2,1,0:T(8,128)(2,1)}, u32[]{:S(2)}, u32[]{:S(2)}) collective-permute-start(bf16[3,128,2048]{2,1,0:T(8,128)(2,1)} %pad_maximum_fusion.a_ref), channel_id=1, source_target_pairs={{0,32},{32,0},{1,33},{33,1},{2,34},{34,2},{3,35},{35,3},{4,36},{36... | collective-permute-start | bytes 4718600 | tf_op jit(solution)/shard_map/ppermute | solution.py:186
  55.2 30.1 %all-to-all-start = ((bf16[16,32,2176]{2,1,0:T(8,128)(2,1)}), bf16[16,32,2176]{2,1,0:T(8,128)(2,1)S(1)}, u32[]{:S(2)}, u32[]{:S(2)}) async-start(bf16[16,32,2176]{2,1,0:T(8,128)(2,1)} %bitcast.58), calls=%async_computation | async-start | bytes 4456448 | tf_op jit(solution)/shard_map/all_to_all | solution.py:214
  62.4 20.1 %collective-permute-start.3 = (bf16[3,128,2048]{2,1,0:T(8,128)(2,1)}, bf16[3,128,2048]{2,1,0:T(8,128)(2,1)}, u32[]{:S(2)}, u32[]{:S(2)}) collective-permute-start(bf16[3,128,2048]{2,1,0:T(8,128)(2,1)} %pad_maximum_fusion.a_ref), channel_id=1, source_target_pairs={{0,16},{16,0},{1,17},{17,1},{2,18},{18,2},{3,19},{19,3},{4,20},{20... | collective-permute-start | bytes 4718600 | tf_op jit(solution)/shard_map/ppermute | solution.py:183
  80.5 10.4 %collective-permute-start.2 = (bf16[3,128,2048]{2,1,0:T(8,128)(2,1)}, bf16[3,128,2048]{2,1,0:T(8,128)(2,1)}, u32[]{:S(2)}, u32[]{:S(2)}) collective-permute-start(bf16[3,128,2048]{2,1,0:T(8,128)(2,1)} %collective-permute-done.1.a_ref), channel_id=1, source_target_pairs={{0,16},{16,0},{1,17},{17,1},{2,18},{18,2},{3,19},{19,3},{4,20},{20... | collective-permute-start | bytes 4718600 | tf_op jit(solution)/shard_map/ppermute | solution.py:183
  97.0 12.9 %collective-permute-start.4 = (bf16[3,128,2048]{2,1,0:T(8,128)(2,1)}, bf16[3,128,2048]{2,1,0:T(8,128)(2,1)}, u32[]{:S(2)}, u32[]{:S(2)}) collective-permute-start(bf16[3,128,2048]{2,1,0:T(8,128)(2,1)} %get-tuple-element.32), channel_id=1, source_target_pairs={{0,16},{16,0},{1,17},{17,1},{2,18},{18,2},{3,19},{19,3},{4,20},{20... | collective-permute-start | bytes 4718600 | tf_op jit(solution)/shard_map/ppermute | solution.py:183
  98.9 25.8 %all-to-all-start.1 = ((bf16[16,32,1152]{2,1,0:T(8,128)(2,1)}), bf16[16,32,1152]{2,1,0:T(8,128)(2,1)S(1)}, u32[]{:S(2)}, u32[]{:S(2)}) async-start(bf16[16,32,1152]{2,1,0:T(8,128)(2,1)} %bitcast.59), calls=%async_computation.1 | async-start | bytes 2359296 | tf_op jit(solution)/shard_map/all_to_all | solution.py:240
  107.7 53.5 %collective-permute-start.7 = (bf16[3,128,2048]{2,1,0:T(8,128)(2,1)}, bf16[3,128,2048]{2,1,0:T(8,128)(2,1)S(1)}, u32[]{:S(2)}, u32[]{:S(2)}) collective-permute-start(bf16[3,128,2048]{2,1,0:T(8,128)(2,1)} %get-tuple-element.38), channel_id=1, source_target_pairs={{0,16},{16,0},{1,17},{17,1},{2,18},{18,2},{3,19},{19,3},{4,20},{20... | collective-permute-start | bytes 4718600 | tf_op jit(solution)/shard_map/ppermute | solution.py:183
  113.2 16.8 %collective-permute-start.5 = (bf16[128,2048]{1,0:T(8,128)(2,1)}, bf16[128,2048]{1,0:T(8,128)(2,1)S(1)}, u32[]{:S(2)}, u32[]{:S(2)}) collective-permute-start(bf16[128,2048]{1,0:T(8,128)(2,1)} %get-tuple-element.46), channel_id=1, source_target_pairs={{0,32},{32,0},{1,33},{33,1},{2,34},{34,2},{3,35},{35,3},{4,36},{36... | collective-permute-start | bytes 1572872 | tf_op jit(solution)/shard_map/ppermute | solution.py:186
  115.8 26.1 %collective-permute-start.6 = (bf16[128,2048]{1,0:T(8,128)(2,1)}, bf16[128,2048]{1,0:T(8,128)(2,1)}, u32[]{:S(2)}, u32[]{:S(2)}) collective-permute-start(bf16[128,2048]{1,0:T(8,128)(2,1)} %get-tuple-element.45), channel_id=1, source_target_pairs={{0,32},{32,0},{1,33},{33,1},{2,34},{34,2},{3,35},{35,3},{4,36},{36... | collective-permute-start | bytes 1572872 | tf_op jit(solution)/shard_map/ppermute | solution.py:186
  130.0 0.8 copy-start.3
  131.9 29.3 %copy-start.2 = (bf16[3,128,2048]{2,1,0:T(8,128)(2,1)S(1)}, bf16[3,128,2048]{2,1,0:T(8,128)(2,1)}, u32[]{:S(2)}) copy-start(bf16[3,128,2048]{2,1,0:T(8,128)(2,1)} %get-tuple-element.37) | copy-start | bytes 4718596
  131.9 13.8 %all-to-all-start.2 = ((bf16[16,8,1152]{2,1,0:T(8,128)(2,1)}), bf16[16,8,1152]{2,1,0:T(8,128)(2,1)S(1)}, u32[]{:S(2)}, u32[]{:S(2)}) async-start(bf16[16,8,1152]{2,1,0:T(8,128)(2,1)} %bitcast.13), calls=%async_computation.2 | async-start | bytes 589824 | tf_op jit(solution)/shard_map/all_to_all | solution.py:243
  139.3 22.5 %collective-permute-start.8 = (bf16[128,2048]{1,0:T(8,128)(2,1)}, bf16[128,2048]{1,0:T(8,128)(2,1)}, u32[]{:S(2)}, u32[]{:S(2)}) collective-permute-start(bf16[128,2048]{1,0:T(8,128)(2,1)} %get-tuple-element.44), channel_id=1, source_target_pairs={{0,32},{32,0},{1,33},{33,1},{2,34},{34,2},{3,35},{35,3},{4,36},{36... | collective-permute-start | bytes 1572872 | tf_op jit(solution)/shard_map/ppermute | solution.py:186
  146.6 35.1 %all-to-all-start.3 = ((bf16[8,2,8,1152]{3,2,1,0:T(8,128)(2,1)}), bf16[8,2,8,1152]{3,2,1,0:T(8,128)(2,1)S(1)}, u32[]{:S(2)}, u32[]{:S(2)}) async-start(bf16[8,2,8,1152]{3,2,1,0:T(8,128)(2,1)} %fusion.12), calls=%async_computation.3 | async-start | bytes 589824 | tf_op jit(solution)/shard_map/all_to_all | solution.py:248
  161.2 1.0 copy-start.4

commit v6 on v5

--- a/solution.py
+++ b/solution.py
@@ -238,10 +238,9 @@
     far_in = [chip_swap((far_mine[i].astype(F32) + far_other[i].astype(F32)).astype(BF)) for i in range(3)]
 
     home = lax.all_to_all(reply.reshape(cols, CAP, thin), "expert", 0, 0, tiled=True)
-    home, far_in[2] = lax.optimization_barrier((home, far_in[2]))
     (terms,) = call(combine_body, (pick, home.reshape(slots, thin)), (shape((rows, thin), BF),), 2 * slots * rows * thin)
     spread = lax.all_to_all(terms.reshape(cols, part, thin), "expert", 0, 0, tiled=True)
-    spread, far_in[0] = lax.optimization_barrier((spread, far_in[0]))
+    spread, far_in[0], far_in[2] = lax.optimization_barrier((spread, far_in[0], far_in[2]))
     spread = spread.reshape(2, nh, part, thin).transpose(1, 0, 2, 3)
     twice = jnp.concatenate([spread, spread])
     ordered = lax.dynamic_slice_in_dim(twice, (up - 4 * core - odd) % nh, nh, axis=0)

time: 184 us -> 181 us (0.984)
  waiting for transfers between devices: 74.8 us -> 70.5 us
    ppermute x4, waiting for transfers between devices: 21.5 us -> 16.3 us  [chip_swap(): return lax.ppermute(v, 'zq', [(0, 1), (1, 0)])]
where the time goes in v6:
time: 181 us; the launch traced here: 178 us
  starting transfers between devices  79.5 us (44%)
  waiting for transfers between devices  70.5 us (39%)
  Pallas kernels  16.9 us (9%)
  other arithmetic  8.86 us (5%)
    ppermute x1, waiting for transfers between devices, shards(): whole = lax.ppermute(packed, AXES, mirror(sizes))  24.1 us
    ppermute x4, starting transfers between devices, chip_swap(): return lax.ppermute(v, 'zq', [(0, 1), (1, 0)])  20.6 us
    all_to_all x1, waiting for transfers between devices, shards(): planes = lax.all_to_all(ordered, 'zh', 0, 0, tiled=True)  17.2 us
    pallas_call x6, Pallas kernels, call(): pl.pallas_call(body, out_shape=[pltpu.HBM(o.shape, o.dtype) if i in to_hb...  16.9 us
    ppermute x4, waiting for transfers between devices, chip_swap(): return lax.ppermute(v, 'zq', [(0, 1), (1, 0)])  16.3 us
    all_to_all x1, starting transfers between devices, shards(): planes = lax.all_to_all(ordered, 'zh', 0, 0, tiled=True)  14.6 us
    ppermute x1, starting transfers between devices, shards(): whole = lax.ppermute(packed, AXES, mirror(sizes))  11.8 us
    all_to_all x1, starting transfers between devices, shards(): lax.all_to_all(reply.reshape(cols, CAP, thin), 'expert', 0, 0, tiled=True)  8.82 us
  transfers between devices with their start and end apart: 13, of which 7 were waited for; matrix products, arithmetic and copies ran while one was open for 5% of the time, Pallas kernels for 5%

profile of v6, /device:TPU:6, one launch (start us, length us, event | category | flops | bytes accessed | tf_op | source)
XLA Modules:
  0.0 178.1 jit_solution(4251214462860094445)
XLA Ops:
  0.7 0.0 copy-start
  0.7 0.7 copy-done
  1.3 0.0 copy-start.1
  1.3 0.7 copy-done.1
  2.0 0.0 copy-start.3
  2.0 0.0 copy-start.4
  2.0 1.2 shard_map.110
  3.2 11.8 %collective-permute-start = (bf16[128,2176]{1,0:T(8,128)(2,1)S(1)}, bf16[128,2176]{1,0:T(8,128)(2,1)S(1)}, u32[]{:S(2)}, u32[]{:S(2)}) collective-permute-start(bf16[128,2176]{1,0:T(8,128)(2,1)S(1)} %shard_map.110), channel_id=1, source_target_pairs={{0,0},{1,65},{2,130},{3,195},{4,260},{5,325},{6,390},{7,455},{8,8}... | collective-permute-start | bytes 1671176 | tf_op jit(solution)/shard_map/ppermute | solution.py:197
  15.0 0.0 copy-done.3
  15.0 0.0 copy-done.4
  15.0 0.0 copy-done.5
  15.0 1.3 pad_maximum_fusion.a_ref
  16.4 24.1 %collective-permute-done.whole_ref = bf16[128,2176]{1,0:T(8,128)(2,1)S(1)} collective-permute-done((bf16[128,2176]{1,0:T(8,128)(2,1)S(1)}, bf16[128,2176]{1,0:T(8,128)(2,1)S(1)}, u32[]{:S(2)}, u32[]{:S(2)}) %collective-permute-start) | collective-permute-done | bytes 557088 | tf_op jit(solution)/shard_map/ppermute | solution.py:197
  40.5 12.3 %collective-permute-start.1 = (bf16[3,128,2048]{2,1,0:T(8,128)(2,1)}, bf16[3,128,2048]{2,1,0:T(8,128)(2,1)}, u32[]{:S(2)}, u32[]{:S(2)}) collective-permute-start(bf16[3,128,2048]{2,1,0:T(8,128)(2,1)} %pad_maximum_fusion.a_ref), channel_id=1, source_target_pairs={{0,32},{32,0},{1,33},{33,1},{2,34},{34,2},{3,35},{35,3},{4,36},{36... | collective-permute-start | bytes 4718600 | tf_op jit(solution)/shard_map/ppermute | solution.py:186
  52.8 2.4 %shard_map.111 = (bf16[512,2176]{1,0:T(8,128)(2,1)}, bf16[128,512]{1,0:T(8,128)(2,1)S(1)}) custom-call(s32[1]{0:T(128)} %bitcast.block_ref, bf16[128,2176]{1,0:T(8,128)(2,1)S(1)} %collective-permute-done.whole_ref), custom_call_target="tpu_custom_call" | custom-call | flops 285212672 | bytes 2916356 | tf_op jit(solution)/shard_map/pallas_call | solution.py:42
  55.2 7.2 %all-to-all-start = ((bf16[16,32,2176]{2,1,0:T(8,128)(2,1)}), bf16[16,32,2176]{2,1,0:T(8,128)(2,1)S(1)}, u32[]{:S(2)}, u32[]{:S(2)}) async-start(bf16[16,32,2176]{2,1,0:T(8,128)(2,1)} %bitcast.58), calls=%async_computation | async-start | bytes 4456448 | tf_op jit(solution)/shard_map/all_to_all | solution.py:214
  62.3 1.9 %collective-permute-start.3 = (bf16[3,128,2048]{2,1,0:T(8,128)(2,1)}, bf16[3,128,2048]{2,1,0:T(8,128)(2,1)}, u32[]{:S(2)}, u32[]{:S(2)}) collective-permute-start(bf16[3,128,2048]{2,1,0:T(8,128)(2,1)} %pad_maximum_fusion.a_ref), channel_id=1, source_target_pairs={{0,16},{16,0},{1,17},{17,1},{2,18},{18,2},{3,19},{19,3},{4,20},{20... | collective-permute-start | bytes 4718600 | tf_op jit(solution)/shard_map/ppermute | solution.py:183
  64.3 16.2 %collective-permute-done.1.a_ref = bf16[3,128,2048]{2,1,0:T(8,128)(2,1)} collective-permute-done((bf16[3,128,2048]{2,1,0:T(8,128)(2,1)}, bf16[3,128,2048]{2,1,0:T(8,128)(2,1)}, u32[]{:S(2)}, u32[]{:S(2)}) %collective-permute-start.1) | collective-permute-done | bytes 1572896 | tf_op jit(solution)/shard_map/ppermute | solution.py:186
  80.5 1.9 %collective-permute-start.2 = (bf16[3,128,2048]{2,1,0:T(8,128)(2,1)}, bf16[3,128,2048]{2,1,0:T(8,128)(2,1)}, u32[]{:S(2)}, u32[]{:S(2)}) collective-permute-start(bf16[3,128,2048]{2,1,0:T(8,128)(2,1)} %collective-permute-done.1.a_ref), channel_id=1, source_target_pairs={{0,16},{16,0},{1,17},{17,1},{2,18},{18,2},{3,19},{19,3},{4,20},{20... | collective-permute-start | bytes 4718600 | tf_op jit(solution)/shard_map/ppermute | solution.py:183
  82.4 0.0 collective-permute-done.3.b_ref
  82.4 2.8 %all-to-all-done = bf16[16,32,2176]{2,1,0:T(8,128)(2,1)S(1)} async-done(((bf16[16,32,2176]{2,1,0:T(8,128)(2,1)}), bf16[16,32,2176]{2,1,0:T(8,128)(2,1)S(1)}, u32[]{:S(2)}, u32[]{:S(2)}) %all-to-all-start) | async-done | bytes 2228256 | tf_op jit(solution)/shard_map/all_to_all | solution.py:214
  85.3 5.6 %shard_map.112 = (f32[256,2176]{1,0:T(8,128)S(1)}, bf16[3,128,2048]{2,1,0:T(8,128)(2,1)}, bf16[3,128,2048]{2,1,0:T(8,128)(2,1)}) custom-call(s32[1]{0:T(128)} %bitcast.7.expert_ref, bf16[512,2176]{1,0:T(8,128)(2,1)S(1)} %bitcast.54, bf16[3,128,2048]{2,1,0:T(8,128)(2,1)} %pad_maximum_fusion.a_ref, bf16[3,128,2048]{2,1,0:T(8,128)(2,1)} %collective-permute-done.3.b_ref), custom_call_target="tpu_custom_call" | custom-call | flops 2147483648 | bytes 10747908 | tf_op jit(solution)/shard_map/pallas_call | solution.py:42
  90.9 0.0 collective-permute-done.2.b_ref
  90.9 6.0 %shard_map.113 = (bf16[2,256,1152]{2,1,0:T(8,128)(2,1)}, bf16[3,128,2048]{2,1,0:T(8,128)(2,1)}, bf16[3,128,2048]{2,1,0:T(8,128)(2,1)}) custom-call(s32[1]{0:T(128)} %bitcast.7.expert_ref, bf16[512,2176]{1,0:T(8,128)(2,1)S(1)} %bitcast.55, bf16[3,128,2048]{2,1,0:T(8,128)(2,1)} %collective-permute-done.1.a_ref, ...), custom_call_target="tpu_custom_call" | custom-call | flops 2147483648 | bytes 11927556 | tf_op jit(solution)/shard_map/pallas_call | solution.py:42
  97.0 1.9 %collective-permute-start.4 = (bf16[3,128,2048]{2,1,0:T(8,128)(2,1)}, bf16[3,128,2048]{2,1,0:T(8,128)(2,1)}, u32[]{:S(2)}, u32[]{:S(2)}) collective-permute-start(bf16[3,128,2048]{2,1,0:T(8,128)(2,1)} %get-tuple-element.31), channel_id=1, source_target_pairs={{0,16},{16,0},{1,17},{17,1},{2,18},{18,2},{3,19},{19,3},{4,20},{20... | collective-permute-start | bytes 4718600 | tf_op jit(solution)/shard_map/ppermute | solution.py:183
  98.9 8.8 %all-to-all-start.1 = ((bf16[16,32,1152]{2,1,0:T(8,128)(2,1)}), bf16[16,32,1152]{2,1,0:T(8,128)(2,1)S(1)}, u32[]{:S(2)}, u32[]{:S(2)}) async-start(bf16[16,32,1152]{2,1,0:T(8,128)(2,1)} %bitcast.59), calls=%async_computation.1 | async-start | bytes 2359296 | tf_op jit(solution)/shard_map/all_to_all | solution.py:240
  107.7 2.1 %collective-permute-start.7 = (bf16[3,128,2048]{2,1,0:T(8,128)(2,1)}, bf16[3,128,2048]{2,1,0:T(8,128)(2,1)S(1)}, u32[]{:S(2)}, u32[]{:S(2)}) collective-permute-start(bf16[3,128,2048]{2,1,0:T(8,128)(2,1)} %get-tuple-element.36), channel_id=1, source_target_pairs={{0,16},{16,0},{1,17},{17,1},{2,18},{18,2},{3,19},{19,3},{4,20},{20... | collective-permute-start | bytes 4718600 | tf_op jit(solution)/shard_map/ppermute | solution.py:183
  109.8 0.0 collective-permute-done.4
  109.8 3.3 %fusion.8 = (bf16[128,2048]{1,0:T(8,128)(2,1)}, bf16[128,2048]{1,0:T(8,128)(2,1)}, bf16[128,2048]{1,0:T(8,128)(2,1)}) fusion(bf16[3,128,2048]{2,1,0:T(8,128)(2,1)} %collective-permute-done.4, bf16[3,128,2048]{2,1,0:T(8,128)(2,1)} %get-tuple-element.30), kind=kLoop, calls=%fused_computation.18 | loop fusion | flops 3145728 | bytes 4718592 | tf_op jit(solution)/shard_map/convert_element_type | solution.py:238
  113.2 2.6 %collective-permute-start.6 = (bf16[128,2048]{1,0:T(8,128)(2,1)}, bf16[128,2048]{1,0:T(8,128)(2,1)}, u32[]{:S(2)}, u32[]{:S(2)}) collective-permute-start(bf16[128,2048]{1,0:T(8,128)(2,1)} %get-tuple-element.43), channel_id=1, source_target_pairs={{0,32},{32,0},{1,33},{33,1},{2,34},{34,2},{3,35},{35,3},{4,36},{36... | collective-permute-start | bytes 1572872 | tf_op jit(solution)/shard_map/ppermute | solution.py:186
  115.8 3.2 %collective-permute-start.5 = (bf16[128,2048]{1,0:T(8,128)(2,1)}, bf16[128,2048]{1,0:T(8,128)(2,1)}, u32[]{:S(2)}, u32[]{:S(2)}) collective-permute-start(bf16[128,2048]{1,0:T(8,128)(2,1)} %get-tuple-element.44), channel_id=1, source_target_pairs={{0,32},{32,0},{1,33},{33,1},{2,34},{34,2},{3,35},{35,3},{4,36},{36... | collective-permute-start | bytes 1572872 | tf_op jit(solution)/shard_map/ppermute | solution.py:186
  119.0 5.7 %all-to-all-done.1 = bf16[16,32,1152]{2,1,0:T(8,128)(2,1)S(1)} async-done(((bf16[16,32,1152]{2,1,0:T(8,128)(2,1)}), bf16[16,32,1152]{2,1,0:T(8,128)(2,1)S(1)}, u32[]{:S(2)}, u32[]{:S(2)}) %all-to-all-start.1) | async-done | bytes 1179680 | tf_op jit(solution)/shard_map/all_to_all | solution.py:240
  124.7 1.1 shard_map.114
  125.8 0.0 copy-start.2
  125.8 8.7 %all-to-all-start.2 = ((bf16[16,8,1152]{2,1,0:T(8,128)(2,1)}), bf16[16,8,1152]{2,1,0:T(8,128)(2,1)S(1)}, u32[]{:S(2)}, u32[]{:S(2)}) async-start(bf16[16,8,1152]{2,1,0:T(8,128)(2,1)} %bitcast.12), calls=%async_computation.2 | async-start | bytes 589824 | tf_op jit(solution)/shard_map/all_to_all | solution.py:242
  134.5 2.4 %collective-permute-start.8 = (bf16[128,2048]{1,0:T(8,128)(2,1)}, bf16[128,2048]{1,0:T(8,128)(2,1)}, u32[]{:S(2)}, u32[]{:S(2)}) collective-permute-start(bf16[128,2048]{1,0:T(8,128)(2,1)} %get-tuple-element.42), channel_id=1, source_target_pairs={{0,32},{32,0},{1,33},{33,1},{2,34},{34,2},{3,35},{35,3},{4,36},{36... | collective-permute-start | bytes 1572872 | tf_op jit(solution)/shard_map/ppermute | solution.py:186
  136.9 4.3 %all-to-all-done.2 = bf16[16,8,1152]{2,1,0:T(8,128)(2,1)S(1)} async-done(((bf16[16,8,1152]{2,1,0:T(8,128)(2,1)}), bf16[16,8,1152]{2,1,0:T(8,128)(2,1)S(1)}, u32[]{:S(2)}, u32[]{:S(2)}) %all-to-all-start.2) | async-done | bytes 294944 | tf_op jit(solution)/shard_map/all_to_all | solution.py:242
  141.2 0.0 collective-permute-done.6
  141.2 0.1 collective-permute-done.5
  141.4 0.9 fusion.12
  142.2 14.6 %all-to-all-start.3 = ((bf16[8,2,8,1152]{3,2,1,0:T(8,128)(2,1)}), bf16[8,2,8,1152]{3,2,1,0:T(8,128)(2,1)S(1)}, u32[]{:S(2)}, u32[]{:S(2)}) async-start(bf16[8,2,8,1152]{3,2,1,0:T(8,128)(2,1)} %fusion.12), calls=%async_computation.3 | async-start | bytes 589824 | tf_op jit(solution)/shard_map/all_to_all | solution.py:247
  156.8 0.0 collective-permute-done.7
  156.8 0.0 copy-done.2
  156.9 0.6 convert_add_fusion
  157.4 0.0 collective-permute-done.8
  157.5 2.8 %fusion.11 = (bf16[1,1,128,2048]{3,2,1,0:T(8,128)(2,1)}, bf16[1,1,128,2048]{3,2,1,0:T(8,128)(2,1)}, bf16[1,1,128,2048]{3,2,1,0:T(8,128)(2,1)}) fusion(bf16[128,2048]{1,0:T(8,128)(2,1)} %collective-permute-done.6, f32[3,128,2048]{2,1,0:T(8,128)S(1)} %convert_add_fusion, bf16[128,2048]{1,0:T(8,128)(2,1)} %collective-permute-done.8, ...), kind=kLoop, calls=%fused_computation.21 | loop fusion | flops 2359296 | bytes 6291456 | tf_op jit(solution)/shard_map/broadcast_in_dim | solution.py:251
  160.2 17.2 %all-to-all-done.3.terms_ref = bf16[8,2,8,1152]{3,2,1,0:T(8,128)(2,1)S(1)} async-done(((bf16[8,2,8,1152]{3,2,1,0:T(8,128)(2,1)}), bf16[8,2,8,1152]{3,2,1,0:T(8,128)(2,1)S(1)}, u32[]{:S(2)}, u32[]{:S(2)}) %all-to-all-start.3) | async-done | bytes 294944 | tf_op jit(solution)/shard_map/all_to_all | solution.py:247
  177.5 0.7 shard_map.115
  (2 shorter events, 0.0 us)
Async XLA Ops:
  0.7 0.7 copy-start
  1.3 0.7 copy-start.1
  2.0 13.0 %copy-start.3 = (bf16[1,1,128,2048]{3,2,1,0:T(8,128)(2,1)S(1)}, bf16[1,1,128,2048]{3,2,1,0:T(8,128)(2,1)}, u32[]{:S(2)}) copy-start(bf16[1,1,128,2048]{3,2,1,0:T(8,128)(2,1)} %param.13) | copy-start | bytes 1572868
  2.0 13.0 %copy-start.4 = (bf16[1,1,128,2048]{3,2,1,0:T(8,128)(2,1)S(1)}, bf16[1,1,128,2048]{3,2,1,0:T(8,128)(2,1)}, u32[]{:S(2)}) copy-start(bf16[1,1,128,2048]{3,2,1,0:T(8,128)(2,1)} %param.12) | copy-start | bytes 1572868
  2.0 13.0 %copy-start.5 = (bf16[1,1,128,2048]{3,2,1,0:T(8,128)(2,1)S(1)}, bf16[1,1,128,2048]{3,2,1,0:T(8,128)(2,1)}, u32[]{:S(2)}) copy-start(bf16[1,1,128,2048]{3,2,1,0:T(8,128)(2,1)} %param.11) | copy-start | bytes 1572868
  3.2 37.3 %collective-permute-start = (bf16[128,2176]{1,0:T(8,128)(2,1)S(1)}, bf16[128,2176]{1,0:T(8,128)(2,1)S(1)}, u32[]{:S(2)}, u32[]{:S(2)}) collective-permute-start(bf16[128,2176]{1,0:T(8,128)(2,1)S(1)} %shard_map.110), channel_id=1, source_target_pairs={{0,0},{1,65},{2,130},{3,195},{4,260},{5,325},{6,390},{7,455},{8,8}... | collective-permute-start | bytes 1671176 | tf_op jit(solution)/shard_map/ppermute | solution.py:197
  40.5 40.0 %collective-permute-start.1 = (bf16[3,128,2048]{2,1,0:T(8,128)(2,1)}, bf16[3,128,2048]{2,1,0:T(8,128)(2,1)}, u32[]{:S(2)}, u32[]{:S(2)}) collective-permute-start(bf16[3,128,2048]{2,1,0:T(8,128)(2,1)} %pad_maximum_fusion.a_ref), channel_id=1, source_target_pairs={{0,32},{32,0},{1,33},{33,1},{2,34},{34,2},{3,35},{35,3},{4,36},{36... | collective-permute-start | bytes 4718600 | tf_op jit(solution)/shard_map/ppermute | solution.py:186
  55.2 30.1 %all-to-all-start = ((bf16[16,32,2176]{2,1,0:T(8,128)(2,1)}), bf16[16,32,2176]{2,1,0:T(8,128)(2,1)S(1)}, u32[]{:S(2)}, u32[]{:S(2)}) async-start(bf16[16,32,2176]{2,1,0:T(8,128)(2,1)} %bitcast.58), calls=%async_computation | async-start | bytes 4456448 | tf_op jit(solution)/shard_map/all_to_all | solution.py:214
  62.3 20.1 %collective-permute-start.3 = (bf16[3,128,2048]{2,1,0:T(8,128)(2,1)}, bf16[3,128,2048]{2,1,0:T(8,128)(2,1)}, u32[]{:S(2)}, u32[]{:S(2)}) collective-permute-start(bf16[3,128,2048]{2,1,0:T(8,128)(2,1)} %pad_maximum_fusion.a_ref), channel_id=1, source_target_pairs={{0,16},{16,0},{1,17},{17,1},{2,18},{18,2},{3,19},{19,3},{4,20},{20... | collective-permute-start | bytes 4718600 | tf_op jit(solution)/shard_map/ppermute | solution.py:183
  80.5 10.4 %collective-permute-start.2 = (bf16[3,128,2048]{2,1,0:T(8,128)(2,1)}, bf16[3,128,2048]{2,1,0:T(8,128)(2,1)}, u32[]{:S(2)}, u32[]{:S(2)}) collective-permute-start(bf16[3,128,2048]{2,1,0:T(8,128)(2,1)} %collective-permute-done.1.a_ref), channel_id=1, source_target_pairs={{0,16},{16,0},{1,17},{17,1},{2,18},{18,2},{3,19},{19,3},{4,20},{20... | collective-permute-start | bytes 4718600 | tf_op jit(solution)/shard_map/ppermute | solution.py:183
  97.0 12.9 %collective-permute-start.4 = (bf16[3,128,2048]{2,1,0:T(8,128)(2,1)}, bf16[3,128,2048]{2,1,0:T(8,128)(2,1)}, u32[]{:S(2)}, u32[]{:S(2)}) collective-permute-start(bf16[3,128,2048]{2,1,0:T(8,128)(2,1)} %get-tuple-element.31), channel_id=1, source_target_pairs={{0,16},{16,0},{1,17},{17,1},{2,18},{18,2},{3,19},{19,3},{4,20},{20... | collective-permute-start | bytes 4718600 | tf_op jit(solution)/shard_map/ppermute | solution.py:183
  98.9 25.8 %all-to-all-start.1 = ((bf16[16,32,1152]{2,1,0:T(8,128)(2,1)}), bf16[16,32,1152]{2,1,0:T(8,128)(2,1)S(1)}, u32[]{:S(2)}, u32[]{:S(2)}) async-start(bf16[16,32,1152]{2,1,0:T(8,128)(2,1)} %bitcast.59), calls=%async_computation.1 | async-start | bytes 2359296 | tf_op jit(solution)/shard_map/all_to_all | solution.py:240
  107.7 49.1 %collective-permute-start.7 = (bf16[3,128,2048]{2,1,0:T(8,128)(2,1)}, bf16[3,128,2048]{2,1,0:T(8,128)(2,1)S(1)}, u32[]{:S(2)}, u32[]{:S(2)}) collective-permute-start(bf16[3,128,2048]{2,1,0:T(8,128)(2,1)} %get-tuple-element.36), channel_id=1, source_target_pairs={{0,16},{16,0},{1,17},{17,1},{2,18},{18,2},{3,19},{19,3},{4,20},{20... | collective-permute-start | bytes 4718600 | tf_op jit(solution)/shard_map/ppermute | solution.py:183
  113.2 28.1 %collective-permute-start.6 = (bf16[128,2048]{1,0:T(8,128)(2,1)}, bf16[128,2048]{1,0:T(8,128)(2,1)}, u32[]{:S(2)}, u32[]{:S(2)}) collective-permute-start(bf16[128,2048]{1,0:T(8,128)(2,1)} %get-tuple-element.43), channel_id=1, source_target_pairs={{0,32},{32,0},{1,33},{33,1},{2,34},{34,2},{3,35},{35,3},{4,36},{36... | collective-permute-start | bytes 1572872 | tf_op jit(solution)/shard_map/ppermute | solution.py:186
  115.8 25.6 %collective-permute-start.5 = (bf16[128,2048]{1,0:T(8,128)(2,1)}, bf16[128,2048]{1,0:T(8,128)(2,1)}, u32[]{:S(2)}, u32[]{:S(2)}) collective-permute-start(bf16[128,2048]{1,0:T(8,128)(2,1)} %get-tuple-element.44), channel_id=1, source_target_pairs={{0,32},{32,0},{1,33},{33,1},{2,34},{34,2},{3,35},{35,3},{4,36},{36... | collective-permute-start | bytes 1572872 | tf_op jit(solution)/shard_map/ppermute | solution.py:186
  125.8 31.1 %copy-start.2 = (bf16[3,128,2048]{2,1,0:T(8,128)(2,1)S(1)}, bf16[3,128,2048]{2,1,0:T(8,128)(2,1)}, u32[]{:S(2)}) copy-start(bf16[3,128,2048]{2,1,0:T(8,128)(2,1)} %get-tuple-element.35) | copy-start | bytes 4718596
  125.8 15.5 %all-to-all-start.2 = ((bf16[16,8,1152]{2,1,0:T(8,128)(2,1)}), bf16[16,8,1152]{2,1,0:T(8,128)(2,1)S(1)}, u32[]{:S(2)}, u32[]{:S(2)}) async-start(bf16[16,8,1152]{2,1,0:T(8,128)(2,1)} %bitcast.12), calls=%async_computation.2 | async-start | bytes 589824 | tf_op jit(solution)/shard_map/all_to_all | solution.py:242
  134.5 23.0 %collective-permute-start.8 = (bf16[128,2048]{1,0:T(8,128)(2,1)}, bf16[128,2048]{1,0:T(8,128)(2,1)}, u32[]{:S(2)}, u32[]{:S(2)}) collective-permute-start(bf16[128,2048]{1,0:T(8,128)(2,1)} %get-tuple-element.42), channel_id=1, source_target_pairs={{0,32},{32,0},{1,33},{33,1},{2,34},{34,2},{3,35},{35,3},{4,36},{36... | collective-permute-start | bytes 1572872 | tf_op jit(solution)/shard_map/ppermute | solution.py:186
  142.2 35.2 %all-to-all-start.3 = ((bf16[8,2,8,1152]{3,2,1,0:T(8,128)(2,1)}), bf16[8,2,8,1152]{3,2,1,0:T(8,128)(2,1)S(1)}, u32[]{:S(2)}, u32[]{:S(2)}) async-start(bf16[8,2,8,1152]{3,2,1,0:T(8,128)(2,1)} %fusion.12), calls=%async_computation.3 | async-start | bytes 589824 | tf_op jit(solution)/shard_map/all_to_all | solution.py:247

commit v7 on v6

--- a/solution.py
+++ b/solution.py
@@ -29,7 +29,7 @@
         for q in range(nq):
             for c in range(nc):
                 for e in range(ne):
-                    v = (e + 4 * c + q - u) % nh
+                    v = (e + 4 * c + 7 * q - u) % nh
                     pairs.append((((u * nq + q) * nc + c) * ne + e, ((v * nq + q) * nc + c) * ne + e))
     return pairs
 
@@ -243,7 +243,7 @@
     spread, far_in[0], far_in[2] = lax.optimization_barrier((spread, far_in[0], far_in[2]))
     spread = spread.reshape(2, nh, part, thin).transpose(1, 0, 2, 3)
     twice = jnp.concatenate([spread, spread])
-    ordered = lax.dynamic_slice_in_dim(twice, (up - 4 * core - odd) % nh, nh, axis=0)
+    ordered = lax.dynamic_slice_in_dim(twice, (up - 4 * core - 7 * odd) % nh, nh, axis=0)
     planes = lax.all_to_all(ordered, "zh", 0, 0, tiled=True)
     d_tokens, d_gates = call(finish_body, (planes,), (shape((part, width), BF), shape((part, top), F32)), 0)
 

time: 181 us -> 178 us (0.983)
  waiting for transfers between devices: 70.5 us -> 61.4 us
  starting transfers between devices: 79.5 us -> 85.2 us
    all_to_all x1, starting transfers between devices: 7.16 us -> 17.8 us  [shards(): lax.all_to_all(chosen.reshape(cols, CAP, wide), 'expert', 0, 0, tiled=True)]
    ppermute x1, waiting for transfers between devices: 24.1 us -> 16.8 us  [shards(): whole = lax.ppermute(packed, AXES, mirror(sizes))]
    ppermute x4, starting transfers between devices: 20.6 us -> 15.9 us  [chip_swap(): return lax.ppermute(v, 'zq', [(0, 1), (1, 0)])]
    all_to_all x1, waiting for transfers between devices: 2.83 us -> 0.69 us  [shards(): lax.all_to_all(chosen.reshape(cols, CAP, wide), 'expert', 0, 0, tiled=True)]
where the time goes in v7:
time: 178 us; the launch traced here: 175 us
  starting transfers between devices  85.2 us (48%)
  waiting for transfers between devices  61.4 us (34%)
  Pallas kernels  16.9 us (9%)
  other arithmetic  8.86 us (5%)
    all_to_all x1, starting transfers between devices, shards(): lax.all_to_all(chosen.reshape(cols, CAP, wide), 'expert', 0, 0, tiled=True)  17.8 us
    ppermute x4, waiting for transfers between devices, chip_swap(): return lax.ppermute(v, 'zq', [(0, 1), (1, 0)])  17.1 us
    pallas_call x6, Pallas kernels, call(): pl.pallas_call(body, out_shape=[pltpu.HBM(o.shape, o.dtype) if i in to_hb...  16.9 us
    ppermute x1, waiting for transfers between devices, shards(): whole = lax.ppermute(packed, AXES, mirror(sizes))  16.8 us
    all_to_all x1, waiting for transfers between devices, shards(): planes = lax.all_to_all(ordered, 'zh', 0, 0, tiled=True)  16.3 us
    ppermute x4, starting transfers between devices, chip_swap(): return lax.ppermute(v, 'zq', [(0, 1), (1, 0)])  15.9 us
    all_to_all x1, starting transfers between devices, shards(): planes = lax.all_to_all(ordered, 'zh', 0, 0, tiled=True)  14.5 us
    ppermute x1, starting transfers between devices, shards(): whole = lax.ppermute(packed, AXES, mirror(sizes))  11.8 us
  transfers between devices with their start and end apart: 13, of which 7 were waited for; matrix products, arithmetic and copies ran while one was open for 5% of the time, Pallas kernels for 5%

profile of v7, /device:TPU:6, one launch (start us, length us, event | category | flops | bytes accessed | tf_op | source)
XLA Modules:
  0.0 174.7 jit_solution(12213196477332381539)
XLA Ops:
  0.7 0.0 copy-start
  0.7 0.7 copy-done
  1.3 0.0 copy-start.1
  1.3 0.7 copy-done.1
  2.0 0.0 copy-start.3
  2.0 0.0 copy-start.4
  2.0 1.2 shard_map.110
  3.2 11.8 %collective-permute-start = (bf16[128,2176]{1,0:T(8,128)(2,1)S(1)}, bf16[128,2176]{1,0:T(8,128)(2,1)S(1)}, u32[]{:S(2)}, u32[]{:S(2)}) collective-permute-start(bf16[128,2176]{1,0:T(8,128)(2,1)S(1)} %shard_map.110), channel_id=1, source_target_pairs={{0,0},{1,65},{2,130},{3,195},{4,260},{5,325},{6,390},{7,455},{8,8}... | collective-permute-start | bytes 1671176 | tf_op jit(solution)/shard_map/ppermute | solution.py:197
  15.0 0.0 copy-done.3
  15.0 0.0 copy-done.4
  15.0 0.0 copy-done.5
  15.0 1.3 pad_maximum_fusion.a_ref
  16.4 16.8 %collective-permute-done.whole_ref = bf16[128,2176]{1,0:T(8,128)(2,1)S(1)} collective-permute-done((bf16[128,2176]{1,0:T(8,128)(2,1)S(1)}, bf16[128,2176]{1,0:T(8,128)(2,1)S(1)}, u32[]{:S(2)}, u32[]{:S(2)}) %collective-permute-start) | collective-permute-done | bytes 557088 | tf_op jit(solution)/shard_map/ppermute | solution.py:197
  33.2 8.1 %collective-permute-start.1 = (bf16[3,128,2048]{2,1,0:T(8,128)(2,1)}, bf16[3,128,2048]{2,1,0:T(8,128)(2,1)}, u32[]{:S(2)}, u32[]{:S(2)}) collective-permute-start(bf16[3,128,2048]{2,1,0:T(8,128)(2,1)} %pad_maximum_fusion.a_ref), channel_id=1, source_target_pairs={{0,32},{32,0},{1,33},{33,1},{2,34},{34,2},{3,35},{35,3},{4,36},{36... | collective-permute-start | bytes 4718600 | tf_op jit(solution)/shard_map/ppermute | solution.py:186
  41.3 2.4 %shard_map.111 = (bf16[512,2176]{1,0:T(8,128)(2,1)}, bf16[128,512]{1,0:T(8,128)(2,1)S(1)}) custom-call(s32[1]{0:T(128)} %bitcast.block_ref, bf16[128,2176]{1,0:T(8,128)(2,1)S(1)} %collective-permute-done.whole_ref), custom_call_target="tpu_custom_call" | custom-call | flops 285212672 | bytes 2916356 | tf_op jit(solution)/shard_map/pallas_call | solution.py:42
  43.7 17.8 %all-to-all-start = ((bf16[16,32,2176]{2,1,0:T(8,128)(2,1)}), bf16[16,32,2176]{2,1,0:T(8,128)(2,1)S(1)}, u32[]{:S(2)}, u32[]{:S(2)}) async-start(bf16[16,32,2176]{2,1,0:T(8,128)(2,1)} %bitcast.58), calls=%async_computation | async-start | bytes 4456448 | tf_op jit(solution)/shard_map/all_to_all | solution.py:214
  61.5 1.9 %collective-permute-start.3 = (bf16[3,128,2048]{2,1,0:T(8,128)(2,1)}, bf16[3,128,2048]{2,1,0:T(8,128)(2,1)}, u32[]{:S(2)}, u32[]{:S(2)}) collective-permute-start(bf16[3,128,2048]{2,1,0:T(8,128)(2,1)} %pad_maximum_fusion.a_ref), channel_id=1, source_target_pairs={{0,16},{16,0},{1,17},{17,1},{2,18},{18,2},{3,19},{19,3},{4,20},{20... | collective-permute-start | bytes 4718600 | tf_op jit(solution)/shard_map/ppermute | solution.py:183
  63.4 16.9 %collective-permute-done.1.a_ref = bf16[3,128,2048]{2,1,0:T(8,128)(2,1)} collective-permute-done((bf16[3,128,2048]{2,1,0:T(8,128)(2,1)}, bf16[3,128,2048]{2,1,0:T(8,128)(2,1)}, u32[]{:S(2)}, u32[]{:S(2)}) %collective-permute-start.1) | collective-permute-done | bytes 1572896 | tf_op jit(solution)/shard_map/ppermute | solution.py:186
  80.4 3.3 %collective-permute-start.2 = (bf16[3,128,2048]{2,1,0:T(8,128)(2,1)}, bf16[3,128,2048]{2,1,0:T(8,128)(2,1)}, u32[]{:S(2)}, u32[]{:S(2)}) collective-permute-start(bf16[3,128,2048]{2,1,0:T(8,128)(2,1)} %collective-permute-done.1.a_ref), channel_id=1, source_target_pairs={{0,16},{16,0},{1,17},{17,1},{2,18},{18,2},{3,19},{19,3},{4,20},{20... | collective-permute-start | bytes 4718600 | tf_op jit(solution)/shard_map/ppermute | solution.py:183
  83.7 0.0 collective-permute-done.3.b_ref
  83.7 0.7 all-to-all-done
  84.4 5.6 %shard_map.112 = (f32[256,2176]{1,0:T(8,128)S(1)}, bf16[3,128,2048]{2,1,0:T(8,128)(2,1)}, bf16[3,128,2048]{2,1,0:T(8,128)(2,1)}) custom-call(s32[1]{0:T(128)} %bitcast.7.expert_ref, bf16[512,2176]{1,0:T(8,128)(2,1)S(1)} %bitcast.54, bf16[3,128,2048]{2,1,0:T(8,128)(2,1)} %pad_maximum_fusion.a_ref, bf16[3,128,2048]{2,1,0:T(8,128)(2,1)} %collective-permute-done.3.b_ref), custom_call_target="tpu_custom_call" | custom-call | flops 2147483648 | bytes 10747908 | tf_op jit(solution)/shard_map/pallas_call | solution.py:42
  90.0 0.0 collective-permute-done.2.b_ref
  90.0 6.0 %shard_map.113 = (bf16[2,256,1152]{2,1,0:T(8,128)(2,1)}, bf16[3,128,2048]{2,1,0:T(8,128)(2,1)}, bf16[3,128,2048]{2,1,0:T(8,128)(2,1)}) custom-call(s32[1]{0:T(128)} %bitcast.7.expert_ref, bf16[512,2176]{1,0:T(8,128)(2,1)S(1)} %bitcast.55, bf16[3,128,2048]{2,1,0:T(8,128)(2,1)} %collective-permute-done.1.a_ref, ...), custom_call_target="tpu_custom_call" | custom-call | flops 2147483648 | bytes 11927556 | tf_op jit(solution)/shard_map/pallas_call | solution.py:42
  96.1 1.9 %collective-permute-start.4 = (bf16[3,128,2048]{2,1,0:T(8,128)(2,1)}, bf16[3,128,2048]{2,1,0:T(8,128)(2,1)}, u32[]{:S(2)}, u32[]{:S(2)}) collective-permute-start(bf16[3,128,2048]{2,1,0:T(8,128)(2,1)} %get-tuple-element.31), channel_id=1, source_target_pairs={{0,16},{16,0},{1,17},{17,1},{2,18},{18,2},{3,19},{19,3},{4,20},{20... | collective-permute-start | bytes 4718600 | tf_op jit(solution)/shard_map/ppermute | solution.py:183
  98.0 7.4 %all-to-all-start.1 = ((bf16[16,32,1152]{2,1,0:T(8,128)(2,1)}), bf16[16,32,1152]{2,1,0:T(8,128)(2,1)S(1)}, u32[]{:S(2)}, u32[]{:S(2)}) async-start(bf16[16,32,1152]{2,1,0:T(8,128)(2,1)} %bitcast.59), calls=%async_computation.1 | async-start | bytes 2359296 | tf_op jit(solution)/shard_map/all_to_all | solution.py:240
  105.4 2.1 %collective-permute-start.7 = (bf16[3,128,2048]{2,1,0:T(8,128)(2,1)}, bf16[3,128,2048]{2,1,0:T(8,128)(2,1)S(1)}, u32[]{:S(2)}, u32[]{:S(2)}) collective-permute-start(bf16[3,128,2048]{2,1,0:T(8,128)(2,1)} %get-tuple-element.36), channel_id=1, source_target_pairs={{0,16},{16,0},{1,17},{17,1},{2,18},{18,2},{3,19},{19,3},{4,20},{20... | collective-permute-start | bytes 4718600 | tf_op jit(solution)/shard_map/ppermute | solution.py:183
  107.5 0.0 collective-permute-done.4
  107.5 3.3 %fusion.8 = (bf16[128,2048]{1,0:T(8,128)(2,1)}, bf16[128,2048]{1,0:T(8,128)(2,1)}, bf16[128,2048]{1,0:T(8,128)(2,1)}) fusion(bf16[3,128,2048]{2,1,0:T(8,128)(2,1)} %collective-permute-done.4, bf16[3,128,2048]{2,1,0:T(8,128)(2,1)} %get-tuple-element.30), kind=kLoop, calls=%fused_computation.18 | loop fusion | flops 3145728 | bytes 4718592 | tf_op jit(solution)/shard_map/convert_element_type | solution.py:238
  110.8 2.2 %collective-permute-start.6 = (bf16[128,2048]{1,0:T(8,128)(2,1)}, bf16[128,2048]{1,0:T(8,128)(2,1)}, u32[]{:S(2)}, u32[]{:S(2)}) collective-permute-start(bf16[128,2048]{1,0:T(8,128)(2,1)} %get-tuple-element.43), channel_id=1, source_target_pairs={{0,32},{32,0},{1,33},{33,1},{2,34},{34,2},{3,35},{35,3},{4,36},{36... | collective-permute-start | bytes 1572872 | tf_op jit(solution)/shard_map/ppermute | solution.py:186
  113.0 3.7 %collective-permute-start.5 = (bf16[128,2048]{1,0:T(8,128)(2,1)}, bf16[128,2048]{1,0:T(8,128)(2,1)}, u32[]{:S(2)}, u32[]{:S(2)}) collective-permute-start(bf16[128,2048]{1,0:T(8,128)(2,1)} %get-tuple-element.44), channel_id=1, source_target_pairs={{0,32},{32,0},{1,33},{33,1},{2,34},{34,2},{3,35},{35,3},{4,36},{36... | collective-permute-start | bytes 1572872 | tf_op jit(solution)/shard_map/ppermute | solution.py:186
  116.6 5.7 %all-to-all-done.1 = bf16[16,32,1152]{2,1,0:T(8,128)(2,1)S(1)} async-done(((bf16[16,32,1152]{2,1,0:T(8,128)(2,1)}), bf16[16,32,1152]{2,1,0:T(8,128)(2,1)S(1)}, u32[]{:S(2)}, u32[]{:S(2)}) %all-to-all-start.1) | async-done | bytes 1179680 | tf_op jit(solution)/shard_map/all_to_all | solution.py:240
  122.3 1.1 shard_map.114
  123.4 0.0 copy-start.2
  123.4 8.7 %all-to-all-start.2 = ((bf16[16,8,1152]{2,1,0:T(8,128)(2,1)}), bf16[16,8,1152]{2,1,0:T(8,128)(2,1)S(1)}, u32[]{:S(2)}, u32[]{:S(2)}) async-start(bf16[16,8,1152]{2,1,0:T(8,128)(2,1)} %bitcast.12), calls=%async_computation.2 | async-start | bytes 589824 | tf_op jit(solution)/shard_map/all_to_all | solution.py:242
  132.1 1.9 %collective-permute-start.8 = (bf16[128,2048]{1,0:T(8,128)(2,1)}, bf16[128,2048]{1,0:T(8,128)(2,1)}, u32[]{:S(2)}, u32[]{:S(2)}) collective-permute-start(bf16[128,2048]{1,0:T(8,128)(2,1)} %get-tuple-element.42), channel_id=1, source_target_pairs={{0,32},{32,0},{1,33},{33,1},{2,34},{34,2},{3,35},{35,3},{4,36},{36... | collective-permute-start | bytes 1572872 | tf_op jit(solution)/shard_map/ppermute | solution.py:186
  134.0 4.8 %all-to-all-done.2 = bf16[16,8,1152]{2,1,0:T(8,128)(2,1)S(1)} async-done(((bf16[16,8,1152]{2,1,0:T(8,128)(2,1)}), bf16[16,8,1152]{2,1,0:T(8,128)(2,1)S(1)}, u32[]{:S(2)}, u32[]{:S(2)}) %all-to-all-start.2) | async-done | bytes 294944 | tf_op jit(solution)/shard_map/all_to_all | solution.py:242
  138.8 0.0 collective-permute-done.6
  138.8 0.1 collective-permute-done.5
  139.0 0.9 fusion.12
  139.9 14.5 %all-to-all-start.3 = ((bf16[8,2,8,1152]{3,2,1,0:T(8,128)(2,1)}), bf16[8,2,8,1152]{3,2,1,0:T(8,128)(2,1)S(1)}, u32[]{:S(2)}, u32[]{:S(2)}) async-start(bf16[8,2,8,1152]{3,2,1,0:T(8,128)(2,1)} %fusion.12), calls=%async_computation.3 | async-start | bytes 589824 | tf_op jit(solution)/shard_map/all_to_all | solution.py:247
  154.3 0.0 collective-permute-done.7
  154.3 0.0 copy-done.2
  154.3 0.6 convert_add_fusion
  154.9 0.0 collective-permute-done.8
  154.9 2.8 %fusion.11 = (bf16[1,1,128,2048]{3,2,1,0:T(8,128)(2,1)}, bf16[1,1,128,2048]{3,2,1,0:T(8,128)(2,1)}, bf16[1,1,128,2048]{3,2,1,0:T(8,128)(2,1)}) fusion(bf16[128,2048]{1,0:T(8,128)(2,1)} %collective-permute-done.6, f32[3,128,2048]{2,1,0:T(8,128)S(1)} %convert_add_fusion, bf16[128,2048]{1,0:T(8,128)(2,1)} %collective-permute-done.8, ...), kind=kLoop, calls=%fused_computation.21 | loop fusion | flops 2359296 | bytes 6291456 | tf_op jit(solution)/shard_map/broadcast_in_dim | solution.py:251
  157.7 16.3 %all-to-all-done.3.terms_ref = bf16[8,2,8,1152]{3,2,1,0:T(8,128)(2,1)S(1)} async-done(((bf16[8,2,8,1152]{3,2,1,0:T(8,128)(2,1)}), bf16[8,2,8,1152]{3,2,1,0:T(8,128)(2,1)S(1)}, u32[]{:S(2)}, u32[]{:S(2)}) %all-to-all-start.3) | async-done | bytes 294944 | tf_op jit(solution)/shard_map/all_to_all | solution.py:247
  174.1 0.7 shard_map.115
  (2 shorter events, 0.0 us)
Async XLA Ops:
  0.7 0.7 copy-start
  1.3 0.7 copy-start.1
  2.0 13.0 %copy-start.3 = (bf16[1,1,128,2048]{3,2,1,0:T(8,128)(2,1)S(1)}, bf16[1,1,128,2048]{3,2,1,0:T(8,128)(2,1)}, u32[]{:S(2)}) copy-start(bf16[1,1,128,2048]{3,2,1,0:T(8,128)(2,1)} %param.13) | copy-start | bytes 1572868
  2.0 13.0 %copy-start.4 = (bf16[1,1,128,2048]{3,2,1,0:T(8,128)(2,1)S(1)}, bf16[1,1,128,2048]{3,2,1,0:T(8,128)(2,1)}, u32[]{:S(2)}) copy-start(bf16[1,1,128,2048]{3,2,1,0:T(8,128)(2,1)} %param.12) | copy-start | bytes 1572868
  2.0 13.0 %copy-start.5 = (bf16[1,1,128,2048]{3,2,1,0:T(8,128)(2,1)S(1)}, bf16[1,1,128,2048]{3,2,1,0:T(8,128)(2,1)}, u32[]{:S(2)}) copy-start(bf16[1,1,128,2048]{3,2,1,0:T(8,128)(2,1)} %param.11) | copy-start | bytes 1572868
  3.2 30.0 %collective-permute-start = (bf16[128,2176]{1,0:T(8,128)(2,1)S(1)}, bf16[128,2176]{1,0:T(8,128)(2,1)S(1)}, u32[]{:S(2)}, u32[]{:S(2)}) collective-permute-start(bf16[128,2176]{1,0:T(8,128)(2,1)S(1)} %shard_map.110), channel_id=1, source_target_pairs={{0,0},{1,65},{2,130},{3,195},{4,260},{5,325},{6,390},{7,455},{8,8}... | collective-permute-start | bytes 1671176 | tf_op jit(solution)/shard_map/ppermute | solution.py:197
  33.2 47.2 %collective-permute-start.1 = (bf16[3,128,2048]{2,1,0:T(8,128)(2,1)}, bf16[3,128,2048]{2,1,0:T(8,128)(2,1)}, u32[]{:S(2)}, u32[]{:S(2)}) collective-permute-start(bf16[3,128,2048]{2,1,0:T(8,128)(2,1)} %pad_maximum_fusion.a_ref), channel_id=1, source_target_pairs={{0,32},{32,0},{1,33},{33,1},{2,34},{34,2},{3,35},{35,3},{4,36},{36... | collective-permute-start | bytes 4718600 | tf_op jit(solution)/shard_map/ppermute | solution.py:186
  43.7 40.7 %all-to-all-start = ((bf16[16,32,2176]{2,1,0:T(8,128)(2,1)}), bf16[16,32,2176]{2,1,0:T(8,128)(2,1)S(1)}, u32[]{:S(2)}, u32[]{:S(2)}) async-start(bf16[16,32,2176]{2,1,0:T(8,128)(2,1)} %bitcast.58), calls=%async_computation | async-start | bytes 4456448 | tf_op jit(solution)/shard_map/all_to_all | solution.py:214
  61.5 22.2 %collective-permute-start.3 = (bf16[3,128,2048]{2,1,0:T(8,128)(2,1)}, bf16[3,128,2048]{2,1,0:T(8,128)(2,1)}, u32[]{:S(2)}, u32[]{:S(2)}) collective-permute-start(bf16[3,128,2048]{2,1,0:T(8,128)(2,1)} %pad_maximum_fusion.a_ref), channel_id=1, source_target_pairs={{0,16},{16,0},{1,17},{17,1},{2,18},{18,2},{3,19},{19,3},{4,20},{20... | collective-permute-start | bytes 4718600 | tf_op jit(solution)/shard_map/ppermute | solution.py:183
  80.4 9.6 %collective-permute-start.2 = (bf16[3,128,2048]{2,1,0:T(8,128)(2,1)}, bf16[3,128,2048]{2,1,0:T(8,128)(2,1)}, u32[]{:S(2)}, u32[]{:S(2)}) collective-permute-start(bf16[3,128,2048]{2,1,0:T(8,128)(2,1)} %collective-permute-done.1.a_ref), channel_id=1, source_target_pairs={{0,16},{16,0},{1,17},{17,1},{2,18},{18,2},{3,19},{19,3},{4,20},{20... | collective-permute-start | bytes 4718600 | tf_op jit(solution)/shard_map/ppermute | solution.py:183
  96.1 11.4 %collective-permute-start.4 = (bf16[3,128,2048]{2,1,0:T(8,128)(2,1)}, bf16[3,128,2048]{2,1,0:T(8,128)(2,1)}, u32[]{:S(2)}, u32[]{:S(2)}) collective-permute-start(bf16[3,128,2048]{2,1,0:T(8,128)(2,1)} %get-tuple-element.31), channel_id=1, source_target_pairs={{0,16},{16,0},{1,17},{17,1},{2,18},{18,2},{3,19},{19,3},{4,20},{20... | collective-permute-start | bytes 4718600 | tf_op jit(solution)/shard_map/ppermute | solution.py:183
  98.0 24.3 %all-to-all-start.1 = ((bf16[16,32,1152]{2,1,0:T(8,128)(2,1)}), bf16[16,32,1152]{2,1,0:T(8,128)(2,1)S(1)}, u32[]{:S(2)}, u32[]{:S(2)}) async-start(bf16[16,32,1152]{2,1,0:T(8,128)(2,1)} %bitcast.59), calls=%async_computation.1 | async-start | bytes 2359296 | tf_op jit(solution)/shard_map/all_to_all | solution.py:240
  105.4 48.9 %collective-permute-start.7 = (bf16[3,128,2048]{2,1,0:T(8,128)(2,1)}, bf16[3,128,2048]{2,1,0:T(8,128)(2,1)S(1)}, u32[]{:S(2)}, u32[]{:S(2)}) collective-permute-start(bf16[3,128,2048]{2,1,0:T(8,128)(2,1)} %get-tuple-element.36), channel_id=1, source_target_pairs={{0,16},{16,0},{1,17},{17,1},{2,18},{18,2},{3,19},{19,3},{4,20},{20... | collective-permute-start | bytes 4718600 | tf_op jit(solution)/shard_map/ppermute | solution.py:183
  110.8 28.0 %collective-permute-start.6 = (bf16[128,2048]{1,0:T(8,128)(2,1)}, bf16[128,2048]{1,0:T(8,128)(2,1)}, u32[]{:S(2)}, u32[]{:S(2)}) collective-permute-start(bf16[128,2048]{1,0:T(8,128)(2,1)} %get-tuple-element.43), channel_id=1, source_target_pairs={{0,32},{32,0},{1,33},{33,1},{2,34},{34,2},{3,35},{35,3},{4,36},{36... | collective-permute-start | bytes 1572872 | tf_op jit(solution)/shard_map/ppermute | solution.py:186
  113.0 26.0 %collective-permute-start.5 = (bf16[128,2048]{1,0:T(8,128)(2,1)}, bf16[128,2048]{1,0:T(8,128)(2,1)}, u32[]{:S(2)}, u32[]{:S(2)}) collective-permute-start(bf16[128,2048]{1,0:T(8,128)(2,1)} %get-tuple-element.44), channel_id=1, source_target_pairs={{0,32},{32,0},{1,33},{33,1},{2,34},{34,2},{3,35},{35,3},{4,36},{36... | collective-permute-start | bytes 1572872 | tf_op jit(solution)/shard_map/ppermute | solution.py:186
  123.4 30.9 %copy-start.2 = (bf16[3,128,2048]{2,1,0:T(8,128)(2,1)S(1)}, bf16[3,128,2048]{2,1,0:T(8,128)(2,1)}, u32[]{:S(2)}) copy-start(bf16[3,128,2048]{2,1,0:T(8,128)(2,1)} %get-tuple-element.35) | copy-start | bytes 4718596
  123.4 15.4 %all-to-all-start.2 = ((bf16[16,8,1152]{2,1,0:T(8,128)(2,1)}), bf16[16,8,1152]{2,1,0:T(8,128)(2,1)S(1)}, u32[]{:S(2)}, u32[]{:S(2)}) async-start(bf16[16,8,1152]{2,1,0:T(8,128)(2,1)} %bitcast.12), calls=%async_computation.2 | async-start | bytes 589824 | tf_op jit(solution)/shard_map/all_to_all | solution.py:242
  132.1 22.9 %collective-permute-start.8 = (bf16[128,2048]{1,0:T(8,128)(2,1)}, bf16[128,2048]{1,0:T(8,128)(2,1)}, u32[]{:S(2)}, u32[]{:S(2)}) collective-permute-start(bf16[128,2048]{1,0:T(8,128)(2,1)} %get-tuple-element.42), channel_id=1, source_target_pairs={{0,32},{32,0},{1,33},{33,1},{2,34},{34,2},{3,35},{35,3},{4,36},{36... | collective-permute-start | bytes 1572872 | tf_op jit(solution)/shard_map/ppermute | solution.py:186
  139.9 34.2 %all-to-all-start.3 = ((bf16[8,2,8,1152]{3,2,1,0:T(8,128)(2,1)}), bf16[8,2,8,1152]{3,2,1,0:T(8,128)(2,1)S(1)}, u32[]{:S(2)}, u32[]{:S(2)}) async-start(bf16[8,2,8,1152]{3,2,1,0:T(8,128)(2,1)} %fusion.12), calls=%async_computation.3 | async-start | bytes 589824 | tf_op jit(solution)/shard_map/all_to_all | solution.py:247

commit v8 on v7

--- a/solution.py
+++ b/solution.py
@@ -29,7 +29,7 @@
         for q in range(nq):
             for c in range(nc):
                 for e in range(ne):
-                    v = (e + 4 * c + 7 * q - u) % nh
+                    v = (e + 4 * c + 2 * q - u) % nh
                     pairs.append((((u * nq + q) * nc + c) * ne + e, ((v * nq + q) * nc + c) * ne + e))
     return pairs
 
@@ -243,7 +243,7 @@
     spread, far_in[0], far_in[2] = lax.optimization_barrier((spread, far_in[0], far_in[2]))
     spread = spread.reshape(2, nh, part, thin).transpose(1, 0, 2, 3)
     twice = jnp.concatenate([spread, spread])
-    ordered = lax.dynamic_slice_in_dim(twice, (up - 4 * core - 7 * odd) % nh, nh, axis=0)
+    ordered = lax.dynamic_slice_in_dim(twice, (up - 4 * core - 2 * odd) % nh, nh, axis=0)
     planes = lax.all_to_all(ordered, "zh", 0, 0, tiled=True)
     d_tokens, d_gates = call(finish_body, (planes,), (shape((part, width), BF), shape((part, top), F32)), 0)
 

time: 178 us -> 173 us (0.972)
  starting transfers between devices: 85.2 us -> 68.8 us
  waiting for transfers between devices: 61.4 us -> 73.9 us
    all_to_all x1, starting transfers between devices: 17.8 us -> 8.84 us  [shards(): lax.all_to_all(chosen.reshape(cols, CAP, wide), 'expert', 0, 0, tiled=True)]
    ppermute x4, waiting for transfers between devices: 17.1 us -> 25.5 us  [chip_swap(): return lax.ppermute(v, 'zq', [(0, 1), (1, 0)])]
    ppermute x1, waiting for transfers between devices: 16.8 us -> 24.2 us  [shards(): whole = lax.ppermute(packed, AXES, mirror(sizes))]
    all_to_all x1, waiting for transfers between devices: 4.85 us -> 0.28 us  [shards(): lax.all_to_all(terms.reshape(cols, part, thin), 'expert', 0, 0, tiled=True)]
    all_to_all x1, starting transfers between devices: 14.5 us -> 11.6 us  [shards(): planes = lax.all_to_all(ordered, 'zh', 0, 0, tiled=True)]
    all_to_all x1, waiting for transfers between devices: 16.3 us -> 18.9 us  [shards(): planes = lax.all_to_all(ordered, 'zh', 0, 0, tiled=True)]
    ppermute x4, starting transfers between devices: 15.9 us -> 14 us  [chip_swap(): return lax.ppermute(v, 'zq', [(0, 1), (1, 0)])]
    all_to_all x1, starting transfers between devices: 8.67 us -> 6.86 us  [shards(): lax.all_to_all(terms.reshape(cols, part, thin), 'expert', 0, 0, tiled=True)]
  transfers between devices with their start and end apart: 13 -> 13, of which waited for: 7 -> 6; matrix products, arithmetic and copies ran while one was open for 5% -> 5% of each run, Pallas kernels for 5% -> 5%
where the time goes in v8:
time: 173 us; the launch traced here: 171 us
  waiting for transfers between devices  73.9 us (43%)
  starting transfers between devices  68.8 us (40%)
  Pallas kernels  16.9 us (10%)
  other arithmetic  8.86 us (5%)
    ppermute x4, waiting for transfers between devices, chip_swap(): return lax.ppermute(v, 'zq', [(0, 1), (1, 0)])  25.5 us
    ppermute x1, waiting for transfers between devices, shards(): whole = lax.ppermute(packed, AXES, mirror(sizes))  24.2 us
    all_to_all x1, waiting for transfers between devices, shards(): planes = lax.all_to_all(ordered, 'zh', 0, 0, tiled=True)  18.9 us
    pallas_call x6, Pallas kernels, call(): pl.pallas_call(body, out_shape=[pltpu.HBM(o.shape, o.dtype) if i in to_hb...  16.9 us
    ppermute x4, starting transfers between devices, chip_swap(): return lax.ppermute(v, 'zq', [(0, 1), (1, 0)])  14 us
    ppermute x1, starting transfers between devices, shards(): whole = lax.ppermute(packed, AXES, mirror(sizes))  11.8 us
    all_to_all x1, starting transfers between devices, shards(): planes = lax.all_to_all(ordered, 'zh', 0, 0, tiled=True)  11.6 us
    all_to_all x1, starting transfers between devices, shards(): lax.all_to_all(chosen.reshape(cols, CAP, wide), 'expert', 0, 0, tiled=True)  8.84 us
  transfers between devices with their start and end apart: 13, of which 6 were waited for; matrix products, arithmetic and copies ran while one was open for 5% of the time, Pallas kernels for 5%

profile of v8, /device:TPU:6, one launch (start us, length us, event | category | flops | bytes accessed | tf_op | source)
XLA Modules:
  0.0 170.8 jit_solution(15439368337649316279)
XLA Ops:
  0.7 0.0 copy-start
  0.7 0.7 copy-done
  1.3 0.0 copy-start.1
  1.3 0.7 copy-done.1
  2.0 0.0 copy-start.3
  2.0 0.0 copy-start.4
  2.0 0.0 copy-start.5
  2.0 1.2 shard_map.110
  3.2 11.8 %collective-permute-start = (bf16[128,2176]{1,0:T(8,128)(2,1)S(1)}, bf16[128,2176]{1,0:T(8,128)(2,1)S(1)}, u32[]{:S(2)}, u32[]{:S(2)}) collective-permute-start(bf16[128,2176]{1,0:T(8,128)(2,1)S(1)} %shard_map.110), channel_id=1, source_target_pairs={{0,0},{1,65},{2,130},{3,195},{4,260},{5,325},{6,390},{7,455},{8,8}... | collective-permute-start | bytes 1671176 | tf_op jit(solution)/shard_map/ppermute | solution.py:197
  15.0 0.0 copy-done.3
  15.0 0.0 copy-done.4
  15.0 0.0 copy-done.5
  15.0 1.3 pad_maximum_fusion.a_ref
  16.4 24.2 %collective-permute-done.whole_ref = bf16[128,2176]{1,0:T(8,128)(2,1)S(1)} collective-permute-done((bf16[128,2176]{1,0:T(8,128)(2,1)S(1)}, bf16[128,2176]{1,0:T(8,128)(2,1)S(1)}, u32[]{:S(2)}, u32[]{:S(2)}) %collective-permute-start) | collective-permute-done | bytes 557088 | tf_op jit(solution)/shard_map/ppermute | solution.py:197
  40.6 1.9 %collective-permute-start.1 = (bf16[3,128,2048]{2,1,0:T(8,128)(2,1)}, bf16[3,128,2048]{2,1,0:T(8,128)(2,1)}, u32[]{:S(2)}, u32[]{:S(2)}) collective-permute-start(bf16[3,128,2048]{2,1,0:T(8,128)(2,1)} %pad_maximum_fusion.a_ref), channel_id=1, source_target_pairs={{0,32},{32,0},{1,33},{33,1},{2,34},{34,2},{3,35},{35,3},{4,36},{36... | collective-permute-start | bytes 4718600 | tf_op jit(solution)/shard_map/ppermute | solution.py:186
  42.5 2.4 %shard_map.111 = (bf16[512,2176]{1,0:T(8,128)(2,1)}, bf16[128,512]{1,0:T(8,128)(2,1)S(1)}) custom-call(s32[1]{0:T(128)} %bitcast.block_ref, bf16[128,2176]{1,0:T(8,128)(2,1)S(1)} %collective-permute-done.whole_ref), custom_call_target="tpu_custom_call" | custom-call | flops 285212672 | bytes 2916356 | tf_op jit(solution)/shard_map/pallas_call | solution.py:42
  44.9 8.8 %all-to-all-start = ((bf16[16,32,2176]{2,1,0:T(8,128)(2,1)}), bf16[16,32,2176]{2,1,0:T(8,128)(2,1)S(1)}, u32[]{:S(2)}, u32[]{:S(2)}) async-start(bf16[16,32,2176]{2,1,0:T(8,128)(2,1)} %bitcast.58), calls=%async_computation | async-start | bytes 4456448 | tf_op jit(solution)/shard_map/all_to_all | solution.py:214
  53.7 1.9 %collective-permute-start.3 = (bf16[3,128,2048]{2,1,0:T(8,128)(2,1)}, bf16[3,128,2048]{2,1,0:T(8,128)(2,1)}, u32[]{:S(2)}, u32[]{:S(2)}) collective-permute-start(bf16[3,128,2048]{2,1,0:T(8,128)(2,1)} %pad_maximum_fusion.a_ref), channel_id=1, source_target_pairs={{0,16},{16,0},{1,17},{17,1},{2,18},{18,2},{3,19},{19,3},{4,20},{20... | collective-permute-start | bytes 4718600 | tf_op jit(solution)/shard_map/ppermute | solution.py:183
  55.6 22.7 %collective-permute-done.1.a_ref = bf16[3,128,2048]{2,1,0:T(8,128)(2,1)} collective-permute-done((bf16[3,128,2048]{2,1,0:T(8,128)(2,1)}, bf16[3,128,2048]{2,1,0:T(8,128)(2,1)}, u32[]{:S(2)}, u32[]{:S(2)}) %collective-permute-start.1) | collective-permute-done | bytes 1572896 | tf_op jit(solution)/shard_map/ppermute | solution.py:186
  78.3 1.9 %collective-permute-start.2 = (bf16[3,128,2048]{2,1,0:T(8,128)(2,1)}, bf16[3,128,2048]{2,1,0:T(8,128)(2,1)}, u32[]{:S(2)}, u32[]{:S(2)}) collective-permute-start(bf16[3,128,2048]{2,1,0:T(8,128)(2,1)} %collective-permute-done.1.a_ref), channel_id=1, source_target_pairs={{0,16},{16,0},{1,17},{17,1},{2,18},{18,2},{3,19},{19,3},{4,20},{20... | collective-permute-start | bytes 4718600 | tf_op jit(solution)/shard_map/ppermute | solution.py:183
  80.2 0.0 collective-permute-done.3.b_ref
  80.2 0.0 all-to-all-done
  80.3 5.6 %shard_map.112 = (f32[256,2176]{1,0:T(8,128)S(1)}, bf16[3,128,2048]{2,1,0:T(8,128)(2,1)}, bf16[3,128,2048]{2,1,0:T(8,128)(2,1)}) custom-call(s32[1]{0:T(128)} %bitcast.7.expert_ref, bf16[512,2176]{1,0:T(8,128)(2,1)S(1)} %bitcast.54, bf16[3,128,2048]{2,1,0:T(8,128)(2,1)} %pad_maximum_fusion.a_ref, bf16[3,128,2048]{2,1,0:T(8,128)(2,1)} %collective-permute-done.3.b_ref), custom_call_target="tpu_custom_call" | custom-call | flops 2147483648 | bytes 10747908 | tf_op jit(solution)/shard_map/pallas_call | solution.py:42
  85.9 0.0 collective-permute-done.2.b_ref
  85.9 6.0 %shard_map.113 = (bf16[2,256,1152]{2,1,0:T(8,128)(2,1)}, bf16[3,128,2048]{2,1,0:T(8,128)(2,1)}, bf16[3,128,2048]{2,1,0:T(8,128)(2,1)}) custom-call(s32[1]{0:T(128)} %bitcast.7.expert_ref, bf16[512,2176]{1,0:T(8,128)(2,1)S(1)} %bitcast.55, bf16[3,128,2048]{2,1,0:T(8,128)(2,1)} %collective-permute-done.1.a_ref, ...), custom_call_target="tpu_custom_call" | custom-call | flops 2147483648 | bytes 11927556 | tf_op jit(solution)/shard_map/pallas_call | solution.py:42
  92.0 2.4 %collective-permute-start.4 = (bf16[3,128,2048]{2,1,0:T(8,128)(2,1)}, bf16[3,128,2048]{2,1,0:T(8,128)(2,1)}, u32[]{:S(2)}, u32[]{:S(2)}) collective-permute-start(bf16[3,128,2048]{2,1,0:T(8,128)(2,1)} %get-tuple-element.31), channel_id=1, source_target_pairs={{0,16},{16,0},{1,17},{17,1},{2,18},{18,2},{3,19},{19,3},{4,20},{20... | collective-permute-start | bytes 4718600 | tf_op jit(solution)/shard_map/ppermute | solution.py:183
  94.4 7.6 %all-to-all-start.1 = ((bf16[16,32,1152]{2,1,0:T(8,128)(2,1)}), bf16[16,32,1152]{2,1,0:T(8,128)(2,1)S(1)}, u32[]{:S(2)}, u32[]{:S(2)}) async-start(bf16[16,32,1152]{2,1,0:T(8,128)(2,1)} %bitcast.59), calls=%async_computation.1 | async-start | bytes 2359296 | tf_op jit(solution)/shard_map/all_to_all | solution.py:240
  101.9 1.9 %collective-permute-start.7 = (bf16[3,128,2048]{2,1,0:T(8,128)(2,1)}, bf16[3,128,2048]{2,1,0:T(8,128)(2,1)S(1)}, u32[]{:S(2)}, u32[]{:S(2)}) collective-permute-start(bf16[3,128,2048]{2,1,0:T(8,128)(2,1)} %get-tuple-element.36), channel_id=1, source_target_pairs={{0,16},{16,0},{1,17},{17,1},{2,18},{18,2},{3,19},{19,3},{4,20},{20... | collective-permute-start | bytes 4718600 | tf_op jit(solution)/shard_map/ppermute | solution.py:183
  103.9 0.0 collective-permute-done.4
  103.9 3.3 %fusion.8 = (bf16[128,2048]{1,0:T(8,128)(2,1)}, bf16[128,2048]{1,0:T(8,128)(2,1)}, bf16[128,2048]{1,0:T(8,128)(2,1)}) fusion(bf16[3,128,2048]{2,1,0:T(8,128)(2,1)} %collective-permute-done.4, bf16[3,128,2048]{2,1,0:T(8,128)(2,1)} %get-tuple-element.30), kind=kLoop, calls=%fused_computation.18 | loop fusion | flops 3145728 | bytes 4718592 | tf_op jit(solution)/shard_map/convert_element_type | solution.py:238
  107.2 3.7 %collective-permute-start.6 = (bf16[128,2048]{1,0:T(8,128)(2,1)}, bf16[128,2048]{1,0:T(8,128)(2,1)}, u32[]{:S(2)}, u32[]{:S(2)}) collective-permute-start(bf16[128,2048]{1,0:T(8,128)(2,1)} %get-tuple-element.43), channel_id=1, source_target_pairs={{0,32},{32,0},{1,33},{33,1},{2,34},{34,2},{3,35},{35,3},{4,36},{36... | collective-permute-start | bytes 1572872 | tf_op jit(solution)/shard_map/ppermute | solution.py:186
  110.9 2.1 %collective-permute-start.5 = (bf16[128,2048]{1,0:T(8,128)(2,1)}, bf16[128,2048]{1,0:T(8,128)(2,1)}, u32[]{:S(2)}, u32[]{:S(2)}) collective-permute-start(bf16[128,2048]{1,0:T(8,128)(2,1)} %get-tuple-element.44), channel_id=1, source_target_pairs={{0,32},{32,0},{1,33},{33,1},{2,34},{34,2},{3,35},{35,3},{4,36},{36... | collective-permute-start | bytes 1572872 | tf_op jit(solution)/shard_map/ppermute | solution.py:186
  113.0 5.0 %all-to-all-done.1 = bf16[16,32,1152]{2,1,0:T(8,128)(2,1)S(1)} async-done(((bf16[16,32,1152]{2,1,0:T(8,128)(2,1)}), bf16[16,32,1152]{2,1,0:T(8,128)(2,1)S(1)}, u32[]{:S(2)}, u32[]{:S(2)}) %all-to-all-start.1) | async-done | bytes 1179680 | tf_op jit(solution)/shard_map/all_to_all | solution.py:240
  118.1 1.1 shard_map.114
  119.1 6.9 %all-to-all-start.2 = ((bf16[16,8,1152]{2,1,0:T(8,128)(2,1)}), bf16[16,8,1152]{2,1,0:T(8,128)(2,1)S(1)}, u32[]{:S(2)}, u32[]{:S(2)}) async-start(bf16[16,8,1152]{2,1,0:T(8,128)(2,1)} %bitcast.12), calls=%async_computation.2 | async-start | bytes 589824 | tf_op jit(solution)/shard_map/all_to_all | solution.py:242
  126.0 6.2 %collective-permute-start.8 = (bf16[128,2048]{1,0:T(8,128)(2,1)}, bf16[128,2048]{1,0:T(8,128)(2,1)}, u32[]{:S(2)}, u32[]{:S(2)}) collective-permute-start(bf16[128,2048]{1,0:T(8,128)(2,1)} %get-tuple-element.42), channel_id=1, source_target_pairs={{0,32},{32,0},{1,33},{33,1},{2,34},{34,2},{3,35},{35,3},{4,36},{36... | collective-permute-start | bytes 1572872 | tf_op jit(solution)/shard_map/ppermute | solution.py:186
  132.2 0.3 all-to-all-done.2
  132.5 0.0 collective-permute-done.6
  132.5 2.8 %collective-permute-done.5 = bf16[128,2048]{1,0:T(8,128)(2,1)} collective-permute-done((bf16[128,2048]{1,0:T(8,128)(2,1)}, bf16[128,2048]{1,0:T(8,128)(2,1)}, u32[]{:S(2)}, u32[]{:S(2)}) %collective-permute-start.5) | collective-permute-done | bytes 524320 | tf_op jit(solution)/shard_map/ppermute | solution.py:186
  135.4 0.9 fusion.12
  136.2 11.6 %all-to-all-start.3 = ((bf16[8,2,8,1152]{3,2,1,0:T(8,128)(2,1)}), bf16[8,2,8,1152]{3,2,1,0:T(8,128)(2,1)S(1)}, u32[]{:S(2)}, u32[]{:S(2)}) async-start(bf16[8,2,8,1152]{3,2,1,0:T(8,128)(2,1)} %fusion.12), calls=%async_computation.3 | async-start | bytes 589824 | tf_op jit(solution)/shard_map/all_to_all | solution.py:247
  147.9 0.0 collective-permute-done.7
  147.9 0.0 copy-done.2
  147.9 0.6 convert_add_fusion
  148.5 0.0 collective-permute-done.8
  148.5 2.8 %fusion.11 = (bf16[1,1,128,2048]{3,2,1,0:T(8,128)(2,1)}, bf16[1,1,128,2048]{3,2,1,0:T(8,128)(2,1)}, bf16[1,1,128,2048]{3,2,1,0:T(8,128)(2,1)}) fusion(bf16[128,2048]{1,0:T(8,128)(2,1)} %collective-permute-done.6, f32[3,128,2048]{2,1,0:T(8,128)S(1)} %convert_add_fusion, bf16[128,2048]{1,0:T(8,128)(2,1)} %collective-permute-done.8, ...), kind=kLoop, calls=%fused_computation.21 | loop fusion | flops 2359296 | bytes 6291456 | tf_op jit(solution)/shard_map/broadcast_in_dim | solution.py:251
  151.3 18.9 %all-to-all-done.3.terms_ref = bf16[8,2,8,1152]{3,2,1,0:T(8,128)(2,1)S(1)} async-done(((bf16[8,2,8,1152]{3,2,1,0:T(8,128)(2,1)}), bf16[8,2,8,1152]{3,2,1,0:T(8,128)(2,1)S(1)}, u32[]{:S(2)}, u32[]{:S(2)}) %all-to-all-start.3) | async-done | bytes 294944 | tf_op jit(solution)/shard_map/all_to_all | solution.py:247
  170.2 0.7 shard_map.115
  (2 shorter events, 0.0 us)
Async XLA Ops:
  0.7 0.7 copy-start
  1.3 0.7 copy-start.1
  2.0 13.0 %copy-start.3 = (bf16[1,1,128,2048]{3,2,1,0:T(8,128)(2,1)S(1)}, bf16[1,1,128,2048]{3,2,1,0:T(8,128)(2,1)}, u32[]{:S(2)}) copy-start(bf16[1,1,128,2048]{3,2,1,0:T(8,128)(2,1)} %param.13) | copy-start | bytes 1572868
  2.0 13.0 %copy-start.4 = (bf16[1,1,128,2048]{3,2,1,0:T(8,128)(2,1)S(1)}, bf16[1,1,128,2048]{3,2,1,0:T(8,128)(2,1)}, u32[]{:S(2)}) copy-start(bf16[1,1,128,2048]{3,2,1,0:T(8,128)(2,1)} %param.12) | copy-start | bytes 1572868
  2.0 13.0 %copy-start.5 = (bf16[1,1,128,2048]{3,2,1,0:T(8,128)(2,1)S(1)}, bf16[1,1,128,2048]{3,2,1,0:T(8,128)(2,1)}, u32[]{:S(2)}) copy-start(bf16[1,1,128,2048]{3,2,1,0:T(8,128)(2,1)} %param.11) | copy-start | bytes 1572868
  3.2 37.4 %collective-permute-start = (bf16[128,2176]{1,0:T(8,128)(2,1)S(1)}, bf16[128,2176]{1,0:T(8,128)(2,1)S(1)}, u32[]{:S(2)}, u32[]{:S(2)}) collective-permute-start(bf16[128,2176]{1,0:T(8,128)(2,1)S(1)} %shard_map.110), channel_id=1, source_target_pairs={{0,0},{1,65},{2,130},{3,195},{4,260},{5,325},{6,390},{7,455},{8,8}... | collective-permute-start | bytes 1671176 | tf_op jit(solution)/shard_map/ppermute | solution.py:197
  40.6 37.7 %collective-permute-start.1 = (bf16[3,128,2048]{2,1,0:T(8,128)(2,1)}, bf16[3,128,2048]{2,1,0:T(8,128)(2,1)}, u32[]{:S(2)}, u32[]{:S(2)}) collective-permute-start(bf16[3,128,2048]{2,1,0:T(8,128)(2,1)} %pad_maximum_fusion.a_ref), channel_id=1, source_target_pairs={{0,32},{32,0},{1,33},{33,1},{2,34},{34,2},{3,35},{35,3},{4,36},{36... | collective-permute-start | bytes 4718600 | tf_op jit(solution)/shard_map/ppermute | solution.py:186
  44.9 35.4 %all-to-all-start = ((bf16[16,32,2176]{2,1,0:T(8,128)(2,1)}), bf16[16,32,2176]{2,1,0:T(8,128)(2,1)S(1)}, u32[]{:S(2)}, u32[]{:S(2)}) async-start(bf16[16,32,2176]{2,1,0:T(8,128)(2,1)} %bitcast.58), calls=%async_computation | async-start | bytes 4456448 | tf_op jit(solution)/shard_map/all_to_all | solution.py:214
  53.7 26.5 %collective-permute-start.3 = (bf16[3,128,2048]{2,1,0:T(8,128)(2,1)}, bf16[3,128,2048]{2,1,0:T(8,128)(2,1)}, u32[]{:S(2)}, u32[]{:S(2)}) collective-permute-start(bf16[3,128,2048]{2,1,0:T(8,128)(2,1)} %pad_maximum_fusion.a_ref), channel_id=1, source_target_pairs={{0,16},{16,0},{1,17},{17,1},{2,18},{18,2},{3,19},{19,3},{4,20},{20... | collective-permute-start | bytes 4718600 | tf_op jit(solution)/shard_map/ppermute | solution.py:183
  78.3 7.6 %collective-permute-start.2 = (bf16[3,128,2048]{2,1,0:T(8,128)(2,1)}, bf16[3,128,2048]{2,1,0:T(8,128)(2,1)}, u32[]{:S(2)}, u32[]{:S(2)}) collective-permute-start(bf16[3,128,2048]{2,1,0:T(8,128)(2,1)} %collective-permute-done.1.a_ref), channel_id=1, source_target_pairs={{0,16},{16,0},{1,17},{17,1},{2,18},{18,2},{3,19},{19,3},{4,20},{20... | collective-permute-start | bytes 4718600 | tf_op jit(solution)/shard_map/ppermute | solution.py:183
  92.0 11.9 %collective-permute-start.4 = (bf16[3,128,2048]{2,1,0:T(8,128)(2,1)}, bf16[3,128,2048]{2,1,0:T(8,128)(2,1)}, u32[]{:S(2)}, u32[]{:S(2)}) collective-permute-start(bf16[3,128,2048]{2,1,0:T(8,128)(2,1)} %get-tuple-element.31), channel_id=1, source_target_pairs={{0,16},{16,0},{1,17},{17,1},{2,18},{18,2},{3,19},{19,3},{4,20},{20... | collective-permute-start | bytes 4718600 | tf_op jit(solution)/shard_map/ppermute | solution.py:183
  94.4 23.7 %all-to-all-start.1 = ((bf16[16,32,1152]{2,1,0:T(8,128)(2,1)}), bf16[16,32,1152]{2,1,0:T(8,128)(2,1)S(1)}, u32[]{:S(2)}, u32[]{:S(2)}) async-start(bf16[16,32,1152]{2,1,0:T(8,128)(2,1)} %bitcast.59), calls=%async_computation.1 | async-start | bytes 2359296 | tf_op jit(solution)/shard_map/all_to_all | solution.py:240
  101.9 45.9 %collective-permute-start.7 = (bf16[3,128,2048]{2,1,0:T(8,128)(2,1)}, bf16[3,128,2048]{2,1,0:T(8,128)(2,1)S(1)}, u32[]{:S(2)}, u32[]{:S(2)}) collective-permute-start(bf16[3,128,2048]{2,1,0:T(8,128)(2,1)} %get-tuple-element.36), channel_id=1, source_target_pairs={{0,16},{16,0},{1,17},{17,1},{2,18},{18,2},{3,19},{19,3},{4,20},{20... | collective-permute-start | bytes 4718600 | tf_op jit(solution)/shard_map/ppermute | solution.py:183
  107.2 25.3 %collective-permute-start.6 = (bf16[128,2048]{1,0:T(8,128)(2,1)}, bf16[128,2048]{1,0:T(8,128)(2,1)}, u32[]{:S(2)}, u32[]{:S(2)}) collective-permute-start(bf16[128,2048]{1,0:T(8,128)(2,1)} %get-tuple-element.43), channel_id=1, source_target_pairs={{0,32},{32,0},{1,33},{33,1},{2,34},{34,2},{3,35},{35,3},{4,36},{36... | collective-permute-start | bytes 1572872 | tf_op jit(solution)/shard_map/ppermute | solution.py:186
  110.9 24.4 %collective-permute-start.5 = (bf16[128,2048]{1,0:T(8,128)(2,1)}, bf16[128,2048]{1,0:T(8,128)(2,1)}, u32[]{:S(2)}, u32[]{:S(2)}) collective-permute-start(bf16[128,2048]{1,0:T(8,128)(2,1)} %get-tuple-element.44), channel_id=1, source_target_pairs={{0,32},{32,0},{1,33},{33,1},{2,34},{34,2},{3,35},{35,3},{4,36},{36... | collective-permute-start | bytes 1572872 | tf_op jit(solution)/shard_map/ppermute | solution.py:186
  119.1 28.8 %copy-start.2 = (bf16[3,128,2048]{2,1,0:T(8,128)(2,1)S(1)}, bf16[3,128,2048]{2,1,0:T(8,128)(2,1)}, u32[]{:S(2)}) copy-start(bf16[3,128,2048]{2,1,0:T(8,128)(2,1)} %get-tuple-element.35) | copy-start | bytes 4718596
  119.1 13.4 %all-to-all-start.2 = ((bf16[16,8,1152]{2,1,0:T(8,128)(2,1)}), bf16[16,8,1152]{2,1,0:T(8,128)(2,1)S(1)}, u32[]{:S(2)}, u32[]{:S(2)}) async-start(bf16[16,8,1152]{2,1,0:T(8,128)(2,1)} %bitcast.12), calls=%async_computation.2 | async-start | bytes 589824 | tf_op jit(solution)/shard_map/all_to_all | solution.py:242
  126.0 22.5 %collective-permute-start.8 = (bf16[128,2048]{1,0:T(8,128)(2,1)}, bf16[128,2048]{1,0:T(8,128)(2,1)}, u32[]{:S(2)}, u32[]{:S(2)}) collective-permute-start(bf16[128,2048]{1,0:T(8,128)(2,1)} %get-tuple-element.42), channel_id=1, source_target_pairs={{0,32},{32,0},{1,33},{33,1},{2,34},{34,2},{3,35},{35,3},{4,36},{36... | collective-permute-start | bytes 1572872 | tf_op jit(solution)/shard_map/ppermute | solution.py:186
  136.2 34.0 %all-to-all-start.3 = ((bf16[8,2,8,1152]{3,2,1,0:T(8,128)(2,1)}), bf16[8,2,8,1152]{3,2,1,0:T(8,128)(2,1)S(1)}, u32[]{:S(2)}, u32[]{:S(2)}) async-start(bf16[8,2,8,1152]{3,2,1,0:T(8,128)(2,1)} %fusion.12), calls=%async_computation.3 | async-start | bytes 589824 | tf_op jit(solution)/shard_map/all_to_all | solution.py:247
